TPU v7x, 32 devices: a whole 2x2x4 slice. The times are simulated.
32 devices in a mesh: chan: 8 (over y, x, core), bl: 4 (over z).
Axes of the slice: x: 2, y: 2, z: 4, core: 2. Of those that a mesh axis runs over, the one named last changes fastest.
Arguments:
- visibilities: float32 [2, 2, 192, 8192], P(None, None, 'chan', 'bl'), may hold values from -12 to 12
- coherencies: bfloat16 [2, 4, 2, 192, 8192], P(None, None, None, 'chan', 'bl'), may hold values from -6 to 6
- start_gains: float32 [2, 4, 2, 192, 512], P(None, None, None, 'chan'), may hold values from -4 to 4
- penalty: float32 [4], replicated, may hold values from 100 to 1000
- stations: int32 [2, 8192], P(None, 'bl'), may hold values from 0 to 511, as said below
Outputs:
- gains: float32 [2, 4, 2, 192, 512], P(None, None, None, 'chan')
- consensus: float32 [2, 4, 2, 192, 512], P(None, None, None, 'chan', 'bl')
- dual: float32 [2, 4, 2, 192, 512], P(None, None, None, 'chan', 'bl')
Inputs may be any that keep to these rules, and one draw needn't show every extreme that they name: Each baseline joins two different stations.
All inputs are finite; a program needn't handle non-finite values.
Results may differ from a plain program's by a relative error of at most 0.0003.
Values sent between devices are 32-bit elements; how exact they have to be, the bound alone decides.
No kernel may reach another device: no remote copies, remote signals or barrier semaphores. Data moves between devices by JAX's collectives and lax.ppermute only.
A program may use at most 64 MiB of HBM per device.

v0:
```python
import math

import jax
import jax.numpy as jnp
from jax import lax
from jax.sharding import PartitionSpec as P

POLY = 4
ITERS = 2


def bernstein(rows, total):
    position = (rows.astype(jnp.float32) + 0.5) / total
    columns = [
        math.comb(POLY - 1, degree) * position**degree * (1.0 - position) ** (POLY - 1 - degree)
        for degree in range(POLY)
    ]
    return jnp.stack(columns, axis=1)


def exact_product(values, selector):
    upper = values.astype(jnp.bfloat16)
    rest = values - lax.optimization_barrier(upper).astype(jnp.float32)
    middle = rest.astype(jnp.bfloat16)
    lowest = (rest - lax.optimization_barrier(middle).astype(jnp.float32)).astype(jnp.bfloat16)
    total = jnp.dot(upper, selector, preferred_element_type=jnp.float32)
    total = total + jnp.dot(middle, selector, preferred_element_type=jnp.float32)
    return total + jnp.dot(lowest, selector, preferred_element_type=jnp.float32)


def normals(visibility, coherency, gains, pick_first, pick_second):
    lead = gains.shape[:4]
    stations_all = gains.shape[4]
    links = pick_first.shape[0]
    flat_gains = gains.reshape(-1, stations_all)
    first_gains = exact_product(flat_gains, pick_first.T).reshape(lead + (links,))
    second_gains = exact_product(flat_gains, pick_second.T).reshape(lead + (links,))
    first_real = first_gains[0]
    first_imag = first_gains[1]
    second_real = second_gains[0]
    second_imag = second_gains[1]
    coh_real = coherency[0].astype(jnp.float32)
    coh_imag = coherency[1].astype(jnp.float32)
    pair_real = first_real * second_real + first_imag * second_imag
    pair_imag = first_imag * second_real - first_real * second_imag
    model_real = pair_real * coh_real - pair_imag * coh_imag
    model_imag = pair_real * coh_imag + pair_imag * coh_real
    resid_real = visibility[0] - jnp.sum(model_real, axis=0) + model_real
    resid_imag = visibility[1] - jnp.sum(model_imag, axis=0) + model_imag
    power = coh_real * coh_real + coh_imag * coh_imag
    left_real = second_real * coh_real + second_imag * coh_imag
    left_imag = second_imag * coh_real - second_real * coh_imag
    right_real = first_real * coh_real - first_imag * coh_imag
    right_imag = first_real * coh_imag + first_imag * coh_real
    first_terms = jnp.stack(
        [
            resid_real * left_real - resid_imag * left_imag,
            resid_real * left_imag + resid_imag * left_real,
            (second_real * second_real + second_imag * second_imag) * power,
        ]
    )
    second_terms = jnp.stack(
        [
            resid_real * right_real + resid_imag * right_imag,
            resid_real * right_imag - resid_imag * right_real,
            (first_real * first_real + first_imag * first_imag) * power,
        ]
    )
    out_shape = first_terms.shape[:4] + (stations_all,)
    summed = exact_product(first_terms.reshape(-1, links), pick_first)
    summed = summed + exact_product(second_terms.reshape(-1, links), pick_second)
    return summed.reshape(out_shape)


def update(normal, target, penalty):
    weight = penalty[:, None, None, None]
    divisor = normal[2] + weight
    return jnp.stack(
        [(normal[0] + weight * target[0]) / divisor, (normal[1] + weight * target[1]) / divisor]
    )


def shards(visibilities, coherencies, start_gains, penalty, stations):
    highest = lax.Precision.HIGHEST
    station_ids = jnp.arange(start_gains.shape[4], dtype=jnp.int32)
    pick_first = (stations[0][:, None] == station_ids[None, :]).astype(jnp.bfloat16)
    pick_second = (stations[1][:, None] == station_ids[None, :]).astype(jnp.bfloat16)
    chans = visibilities.shape[2]
    total_chans = chans * lax.axis_size("chan")
    local_rows = lax.axis_index("chan") * chans + jnp.arange(chans, dtype=jnp.int32)
    local_bern = bernstein(local_rows, total_chans)
    full_bern = bernstein(jnp.arange(total_chans, dtype=jnp.int32), total_chans)
    gram_matrix = jnp.dot(full_bern.T, full_bern, precision=highest)
    factor = jnp.linalg.cholesky(gram_matrix)
    share = start_gains.shape[4] // lax.axis_size("bl")
    offset = lax.axis_index("bl") * share
    gains = start_gains
    consensus = start_gains
    dual = jnp.zeros_like(start_gains)
    for iteration in range(ITERS):
        normal = lax.psum(normals(visibilities, coherencies, gains, pick_first, pick_second), "bl")
        gains = update(normal, consensus - dual, penalty)
        partial_value = jnp.einsum("fj,rktfs->jrkts", local_bern, gains + dual, precision=highest)
        partial_value = lax.psum(partial_value, "chan")
        coefficients = jax.scipy.linalg.cho_solve(
            (factor, True), partial_value.reshape(POLY, -1)
        ).reshape(partial_value.shape)
        consensus = jnp.einsum("fj,jrkts->rktfs", local_bern, coefficients, precision=highest)
        dual = dual + gains - consensus
    consensus = lax.dynamic_slice_in_dim(consensus, offset, share, 4)
    dual = lax.dynamic_slice_in_dim(dual, offset, share, 4)
    return (gains, consensus, dual)


def solution(mesh):
    in_specs = (
        P(None, None, "chan", "bl"),
        P(None, None, None, "chan", "bl"),
        P(None, None, None, "chan", None),
        P(),
        P(None, "bl"),
    )
    out_specs = (
        P(None, None, None, "chan", None),
        P(None, None, None, "chan", "bl"),
        P(None, None, None, "chan", "bl"),
    )
    return jax.shard_map(shards, mesh=mesh, in_specs=in_specs, out_specs=out_specs, check_vma=False)
```

profile of v0, /device:TPU:0, one launch (start us, length us, event | category | flops | bytes accessed | tf_op | source)
XLA Modules:
  0.0 314.9 jit_solution(4641253477295303015)
XLA Ops:
  8.0 1.2 bitcast_convert_fusion.5
  9.5 1.6 fusion.11
  11.1 1.6 fusion.9
  12.8 1.6 fusion.21
  14.4 1.6 fusion.23
  16.0 1.6 fusion.28
  17.6 1.7 fusion.29
  19.4 1.6 multiply_add_fusion.7
  22.2 2.7 multiply_subtract_fusion.5
  26.1 0.9 fusion.24
  27.0 1.5 fusion.19
  28.8 0.9 fusion.25
  29.7 1.5 fusion.7
  31.2 1.3 subtract_convert_fusion.3
  32.5 1.5 fusion.18
  34.1 1.3 subtract_convert_fusion.2
  35.4 1.5 fusion.6
  36.9 1.5 fusion.94
  38.4 2.8 fusion.89
  42.6 57.4 %all-reduce.5.cloned.1.call-done = f32[3,4,2,24,512]{4,3,2,1,0:T(8,128)} async-done(((f32[3,4,2,24,512]{4,3,2,1,0:T(8,128)}), f32[3,4,2,24,512]{4,3,2,1,0:T(8,128)}) %all-reduce.5.cloned.1.call-update) | async-done | bytes 1179664 | tf_op jit(solution)/shard_map/psum | solution.py:101
  100.0 1.5 fusion.104
  101.5 1.1 fusion.135
  103.8 52.4 %all-reduce.9.cloned.1.call-done = f32[4,8192]{1,0:T(4,128)} async-done(((f32[4,8192]{1,0:T(4,128)}), f32[4,8192]{1,0:T(4,128)}) %all-reduce.9.cloned.1.call-update) | async-done | bytes 131088 | tf_op jit(solution)/shard_map/psum | solution.py:104
  156.2 1.3 fusion.122
  157.9 2.1 pad_maximum_fusion.4
  160.3 1.6 fusion.3
  161.9 1.6 fusion.15
  163.6 1.6 fusion.4
  165.2 1.6 fusion.16
  166.8 1.7 add_add_fusion
  168.5 1.7 add_add_fusion.1
  170.3 1.6 multiply_add_fusion.3
  173.1 3.1 multiply_subtract_fusion.1
  176.8 0.9 fusion.26
  177.7 1.5 fusion.13
  180.8 1.5 fusion.1
  182.3 1.3 subtract_convert_fusion.1
  183.6 1.5 fusion.12
  185.1 1.3 subtract_convert_fusion
  186.4 1.5 fusion
  188.0 1.5 fusion.96
  189.5 2.8 fusion.92
  192.3 55.4 %all-reduce.7.cloned.1.call-done = f32[3,4,2,24,512]{4,3,2,1,0:T(8,128)} async-done(((f32[3,4,2,24,512]{4,3,2,1,0:T(8,128)}), f32[3,4,2,24,512]{4,3,2,1,0:T(8,128)}) %all-reduce.7.cloned.1.call-update) | async-done | bytes 1179664 | tf_op jit(solution)/shard_map/psum | solution.py:101
  247.7 1.5 fusion.102
  249.2 1.1 fusion.137
  250.4 1.1 fusion.134
  251.5 52.6 %all-reduce.11.cloned.1.call-done = f32[4,8192]{1,0:T(4,128)} async-done(((f32[4,8192]{1,0:T(4,128)}), f32[4,8192]{1,0:T(4,128)}) %all-reduce.11.cloned.1.call-update) | async-done | bytes 131088 | tf_op jit(solution)/shard_map/psum | solution.py:104
  304.2 1.3 fusion.118
  (57 shorter events, 13.0 us)
Async XLA Ops:
  7.2 2.1 copy-start.1
  7.2 92.9 %all-reduce.5.cloned.1.call-start = ((), (), s32[]{:S(2)}) async-start(), calls=%async_computation | async-start | bytes 2359296 | tf_op jit(solution)/shard_map/psum | solution.py:101
  19.4 1.6 copy-start
  21.0 1.1 copy-start.2
  38.4 61.6 %copy-start.6 = (f32[4]{0:T(128)S(1)}, f32[4]{0:T(128)}, u32[]{:S(2)}) copy-start(f32[4]{0:T(128)} %param.10) | copy-start | bytes 52
  41.2 114.9 %all-reduce.9.cloned.1.call-start = ((), (), s32[]{:S(2)}) async-start(), calls=%async_computation.2 | async-start | bytes 262144 | tf_op jit(solution)/shard_map/psum | solution.py:104
  102.7 145.0 %all-reduce.7.cloned.1.call-start = ((), (), s32[]{:S(2)}) async-start(), calls=%async_computation.1 | async-start | bytes 2359296 | tf_op jit(solution)/shard_map/psum | solution.py:101
  171.9 1.1 copy-start.3
  192.3 55.4 %copy-start.4 = (f32[2,4,2,24,512]{4,3,2,1,0:T(8,128)S(1)}, f32[2,4,2,24,512]{4,3,2,1,0:T(8,128)}, u32[]{:S(2)}) copy-start(f32[2,4,2,24,512]{4,3,2,1,0:T(8,128)} %get-tuple-element.41) | copy-start | bytes 2359300
  192.3 56.9 %copy-start.5 = (f32[2,4,2,24,512]{4,3,2,1,0:T(8,128)S(1)}, f32[2,4,2,24,512]{4,3,2,1,0:T(8,128)}, u32[]{:S(2)}) copy-start(f32[2,4,2,24,512]{4,3,2,1,0:T(8,128)} %get-tuple-element.46) | copy-start | bytes 2359300
  192.3 111.9 %all-reduce.11.cloned.1.call-start = ((), (), s32[]{:S(2)}) async-start(), calls=%async_computation.3 | async-start | bytes 262144 | tf_op jit(solution)/shard_map/psum | solution.py:104
Sparse Core Ops, SparseCore 0:
  41.4 58.6 all-reduce.4
  103.6 52.4 all-reduce.8
  192.4 55.2 all-reduce.6
  251.7 52.4 all-reduce.10
where the time goes:
time: 321 us; the launch traced here: 315 us
  waiting for transfers between devices  218 us (68%)
  matrix products  49.2 us (15%)
  other arithmetic  30.5 us (10%)
  between operations  14.5 us (5%)
    psum x2, waiting for transfers between devices, shards(): lax.psum(normals(visibilities, coherencies, gains, pick_first, pick_secon...  113 us
    psum x2, waiting for transfers between devices, shards(): partial_value = lax.psum(partial_value, 'chan')  105 us
    dot_general x8, matrix products, exact_product(): total = jnp.dot(upper, selector, preferred_element_type=jnp.float32)  15.3 us
    dot_general x8, matrix products, exact_product(): jnp.dot(middle, selector, preferred_element_type=jnp.float32)  12.6 us
    dot_general x8, matrix products, exact_product(): return total + jnp.dot(lowest, selector, preferred_element_type=jnp.float32)  12.5 us
  transfers between devices with their start and end apart: 4, of which 4 were waited for; matrix products, arithmetic and copies ran while one was open for 1% of the time, Pallas kernels for 0%

commit v1 on v0

v1 whole, which is shorter than its diff:
```python
import functools
import math

import jax
import jax.numpy as jnp
import numpy as np
from jax import lax
from jax.experimental import pallas as pl
from jax.experimental.pallas import tpu as pltpu
from jax.sharding import PartitionSpec as P

POLY = 4
ITERS = 2
ROWS_BY_COLS = (((1,), (0,)), ((), ()))
ROWS_BY_ROWS = (((1,), (1,)), ((), ()))


def bernstein_tables(total):
    position = (np.arange(total) + 0.5) / total
    basis = np.stack(
        [math.comb(POLY - 1, j) * position**j * (1.0 - position) ** (POLY - 1 - j) for j in range(POLY)], axis=1
    )
    factor = np.linalg.cholesky(basis.T @ basis)
    solved = np.linalg.solve(factor.T, np.linalg.solve(factor, basis.T)).T
    return basis.astype(np.float32), solved.astype(np.float32)


def split(values):
    upper = values.astype(jnp.bfloat16)
    return upper, (values - upper.astype(jnp.float32)).astype(jnp.bfloat16)


def normals_kernel(dirs, chans, *refs):
    gain_refs = refs[:2]
    vis_ref, coh_ref, station_ref = refs[2:5]
    out_refs = refs[5:7]
    parts = refs[7]
    step = pl.program_id(0)
    half = dirs // 2
    count = gain_refs[0].shape[-1]
    rows = 2 * dirs * chans
    width = station_ref.shape[1]

    @pl.when(step == 0)
    def _():
        pieces = [ref[part] for part in range(2) for ref in gain_refs]
        upper, lower = split(jnp.concatenate(pieces, axis=0).reshape(rows, count))
        parts[0] = upper
        parts[1] = lower

    ids = lax.broadcasted_iota(jnp.int32, (count, width), 0)
    picks = [(ids == station_ref[end : end + 1, :]).astype(jnp.float32).astype(jnp.bfloat16) for end in range(2)]
    dot = functools.partial(lax.dot_general, preferred_element_type=jnp.float32)
    first, second = [
        dot(parts[0], pick, ROWS_BY_COLS) + dot(parts[1], pick, ROWS_BY_COLS) for pick in picks
    ]

    def row(values, part, k):
        start = (part * dirs + k) * chans
        return values[start : start + chans]

    rest_real = vis_ref[0, 0]
    rest_imag = vis_ref[1, 0]
    sides = []
    for k in range(dirs):
        coh_real = coh_ref[0, k, 0].astype(jnp.float32)
        coh_imag = coh_ref[1, k, 0].astype(jnp.float32)
        first_real, first_imag = row(first, 0, k), row(first, 1, k)
        second_real, second_imag = row(second, 0, k), row(second, 1, k)
        left_real = second_real * coh_real + second_imag * coh_imag
        left_imag = second_imag * coh_real - second_real * coh_imag
        right_real = first_real * coh_real - first_imag * coh_imag
        right_imag = first_real * coh_imag + first_imag * coh_real
        rest_real = rest_real - (first_real * left_real + first_imag * left_imag)
        rest_imag = rest_imag - (first_imag * left_real - first_real * left_imag)
        sides.append((left_real, left_imag, right_real, right_imag))
    first_terms = []
    second_terms = []
    for group in range(2):
        chosen = sides[group * half : (group + 1) * half]
        first_terms += [rest_real * a - rest_imag * b for a, b, _, _ in chosen]
        first_terms += [rest_real * b + rest_imag * a for a, b, _, _ in chosen]
        first_terms += [a * a + b * b for a, b, _, _ in chosen]
        second_terms += [rest_real * c + rest_imag * d for _, _, c, d in chosen]
        second_terms += [rest_real * d - rest_imag * c for _, _, c, d in chosen]
        second_terms += [c * c + d * d for _, _, c, d in chosen]
    total = None
    for pick, terms in zip(picks, (first_terms, second_terms)):
        for piece in split(jnp.concatenate(terms, axis=0)):
            value = dot(piece, pick, ROWS_BY_ROWS)
            total = value if total is None else total + value
    total = total.reshape(2, 3, half, chans, count)
    for group in range(2):
        ref = out_refs[group]

        @pl.when(step == 0)
        def _():
            ref[...] = total[group]

        @pl.when(step > 0)
        def _():
            ref[...] += total[group]


def normals(gains, visibilities, coherencies, stations, time):
    _, half, chans, count = gains[0].shape
    dirs = 2 * half
    links = visibilities.shape[3]
    width = min(1024, links)
    gain_spec = pl.BlockSpec((2, half, chans, count), lambda i: (0, 0, 0, 0))
    out_spec = pl.BlockSpec((3, half, chans, count), lambda i: (0, 0, 0, 0))
    flops = 2 * 2 * links * count * (2 * 2 * dirs * chans + 2 * 3 * dirs * chans)
    return pl.pallas_call(
        functools.partial(normals_kernel, dirs, chans),
        grid=(links // width,),
        in_specs=[
            gain_spec,
            gain_spec,
            pl.BlockSpec((2, 1, chans, width), lambda i: (0, time, 0, i)),
            pl.BlockSpec((2, dirs, 1, chans, width), lambda i: (0, 0, time, 0, i)),
            pl.BlockSpec((2, width), lambda i: (0, i)),
        ],
        out_specs=[out_spec, out_spec],
        out_shape=[jax.ShapeDtypeStruct((3, half, chans, count), jnp.float32)] * 2,
        scratch_shapes=[pltpu.VMEM((2, 2 * dirs * chans, count), jnp.bfloat16)],
        compiler_params=pltpu.CompilerParams(
            dimension_semantics=("arbitrary",), vmem_limit_bytes=40 * 2**20
        ),
        cost_estimate=pl.CostEstimate(flops=flops, bytes_accessed=4 * 2**20, transcendentals=0),
    )(*gains, visibilities, coherencies, stations)


def shards(visibilities, coherencies, start_gains, penalty, stations):
    _, dirs, times, chans, count = start_gains.shape
    half = dirs // 2
    line = lax.axis_size("bl")
    place = lax.axis_index("bl")
    groups = lax.axis_size("chan")
    share = count // line
    basis_table, solved_table = bernstein_tables(chans * groups)
    first_row = lax.axis_index("chan") * chans
    basis = lax.dynamic_slice_in_dim(jnp.asarray(basis_table), first_row, chans, 0)
    solved = lax.dynamic_slice_in_dim(jnp.asarray(solved_table), first_row, chans, 0)
    inner = line // 2 - 1

    def gather_in(values):
        for hop in range(inner):
            values = values + lax.ppermute(values, "bl", [(hop, hop + 1), (line - 1 - hop, line - 2 - hop)])
        return values + lax.ppermute(values, "bl", [(inner, inner + 1), (inner + 1, inner)])

    def spread_out(values):
        for hop in reversed(range(inner)):
            moved = lax.ppermute(values, "bl", [(hop + 1, hop), (line - 2 - hop, line - 1 - hop)])
            values = jnp.where((place == hop) | (place == line - 1 - hop), moved, values)
        return values

    def project(values):
        return jnp.stack([jnp.sum(basis[:, j, None] * values, axis=2) for j in range(POLY)])

    def chan_sum(values):
        step = 1
        while step < groups:
            values = values + lax.ppermute(values, "chan", [(i, i ^ step) for i in range(groups)])
            step *= 2
        return values

    def smooth(sums):
        return sum(solved[:, j, None] * sums[j][:, :, None, :] for j in range(POLY))

    def own(values):
        return lax.dynamic_slice_in_dim(values, place * share, share, values.ndim - 1)

    def update(total, gains, target, weight):
        divisor = total[2] + weight
        return jnp.stack(
            [(total[part] + gains[part] * total[2] + weight * target[part]) / divisor for part in range(2)]
        )

    weights = [penalty[group * half : (group + 1) * half, None, None] for group in range(2)]
    gains = [
        [start_gains[:, group * half : (group + 1) * half, time] for group in range(2)] for time in range(times)
    ]
    targets = gains
    duals = None
    for iteration in range(ITERS):
        sums = [normals(gains[time], visibilities, coherencies, stations, time) for time in range(times)]
        fresh = []
        for time in range(times):
            row = []
            for group in range(2):
                total = gather_in(sums[time][group])
                row.append(spread_out(update(total, gains[time][group], targets[time][group], weights[group])))
            fresh.append(row)
        if iteration < ITERS - 1:
            targets = []
            own_duals = []
            for time in range(times):
                values = jnp.concatenate(fresh[time], axis=1)
                if duals is not None:
                    values = values + duals[time]
                consensus = smooth(chan_sum(project(values)))
                dual = values - consensus
                aim = consensus - dual
                targets.append([aim[:, :half], aim[:, half:]])
                own_duals.append(dual)
            duals = own_duals
        gains = fresh
    whole = jnp.stack([jnp.concatenate(row, axis=1) for row in gains], axis=2)
    consensus = []
    dual = []
    for time in range(times):
        values = own(jnp.concatenate(gains[time], axis=1)) + own(duals[time])
        flat = smooth(chan_sum(project(values)))
        consensus.append(flat)
        dual.append(values - flat)
    return whole, jnp.stack(consensus, axis=2), jnp.stack(dual, axis=2)


def solution(mesh):
    in_specs = (
        P(None, None, "chan", "bl"),
        P(None, None, None, "chan", "bl"),
        P(None, None, None, "chan", None),
        P(),
        P(None, "bl"),
    )
    out_specs = (
        P(None, None, None, "chan", None),
        P(None, None, None, "chan", "bl"),
        P(None, None, None, "chan", "bl"),
    )
    return jax.shard_map(shards, mesh=mesh, in_specs=in_specs, out_specs=out_specs, check_vma=False)
```

time: 321 us -> 140 us (0.44); the launches traced: 315 us -> 139 us
  waiting for transfers between devices: 218 us -> 56.9 us
  matrix products: 49.2 us -> 0 us
  starting transfers between devices: 0.16 us -> 43.1 us
  Pallas kernels: 0 us -> 23 us
  other arithmetic: 30.5 us -> 9 us
  between operations: 14.5 us -> 1.37 us
    psum x4 -> x0, waiting for transfers between devices: 218 us -> none  [the longest x2 113 us: shards(): lax.psum(normals(visibilities, coherencies, gains, pick_first, pick_secon...]
    ppermute x0 -> x36, waiting for transfers between devices: none -> 56.9 us  [the longest x8 32 us: spread_out(): lax.ppermute(values, 'bl', [(hop + 1, hop), (line - 2 - hop, line - 1 - h...]
    dot_general x29 -> x0, matrix products: 45.8 us -> none  [the longest x8 15.3 us: exact_product(): total = jnp.dot(upper, selector, preferred_element_type=jnp.float32)]
    ppermute x0 -> x36, starting transfers between devices: none -> 43.1 us  [the longest x8 16.5 us: gather_in(): lax.ppermute(values, 'bl', [(hop, hop + 1), (line - 1 - hop, line - 2 - h...]
    pallas_call x0 -> x4, Pallas kernels: none -> 23 us  [normals(): pl.pallas_call(functools.partial(normals_kernel, dirs, chans), grid=(link...]
    convert_element_type x18 -> x0, other arithmetic: 11.8 us -> none  [the longest x6 5.56 us: exact_product(): (rest - lax.optimization_barrier(middle).astype(jnp.float32)).astype(jnp....]
    sub x3 -> x1, other arithmetic: 6.51 us -> 0.34 us  [shards(): aim = consensus - dual]
    another operation x4 -> x0, matrix products: 3.38 us -> none  [shards(): jax.scipy.linalg.cho_solve((factor, True), partial_value.reshape(POLY, -1))]
  transfers between devices with their start and end apart: 4 -> 36, of which waited for: 4 -> 17; matrix products, arithmetic and copies ran while one was open for 1% -> 6% of each run, Pallas kernels for 0% -> 12%
where the time goes in v1:
time: 140 us; the launch traced here: 139 us
  waiting for transfers between devices  56.9 us (41%)
  starting transfers between devices  43.1 us (31%)
  Pallas kernels  23 us (16%)
  other arithmetic  9 us (6%)
  local copies, waits for them, and re-layouts  5.44 us (4%)
    ppermute x8, waiting for transfers between devices, spread_out(): lax.ppermute(values, 'bl', [(hop + 1, hop), (line - 2 - hop, line - 1 - h...  32 us
    pallas_call x4, Pallas kernels, normals(): pl.pallas_call(functools.partial(normals_kernel, dirs, chans), grid=(link...  23 us
    ppermute x8, starting transfers between devices, gather_in(): lax.ppermute(values, 'bl', [(hop, hop + 1), (line - 1 - hop, line - 2 - h...  16.5 us
    ppermute x8, waiting for transfers between devices, gather_in(): lax.ppermute(values, 'bl', [(hop, hop + 1), (line - 1 - hop, line - 2 - h...  15.9 us
    ppermute x8, starting transfers between devices, spread_out(): lax.ppermute(values, 'bl', [(hop + 1, hop), (line - 2 - hop, line - 1 - h...  10.5 us
    ppermute x12, starting transfers between devices, chan_sum(): lax.ppermute(values, 'chan', [(i, i ^ step) for i in range(groups)])  9.35 us
    ppermute x12, waiting for transfers between devices, chan_sum(): lax.ppermute(values, 'chan', [(i, i ^ step) for i in range(groups)])  8.96 us
    ppermute x8, starting transfers between devices, gather_in(): lax.ppermute(values, 'bl', [(inner, inner + 1), (inner + 1, inner)])  6.83 us
  transfers between devices with their start and end apart: 36, of which 17 were waited for; matrix products, arithmetic and copies ran while one was open for 6% of the time, Pallas kernels for 12%

profile of v1, /device:TPU:0, one launch (start us, length us, event | category | flops | bytes accessed | tf_op | source)
XLA Modules:
  0.0 138.9 jit_solution(11361657454150691304)
XLA Ops:
  0.6 1.4 %slice_bitcast_fusion.2 = (f32[2,2,24,512]{3,2,1,0:T(8,128)S(1)}, f32[2,2,24,512]{3,2,1,0:T(8,128)S(1)}, f32[2,2,24,512]{3,2,1,0:T(8,128)S(1)}, f32[2,2,24,512]{3,2,1,0:T(8,128)S(1)}) fusion(f32[2,4,2,24,512]{4,3,2,1,0:T(8,128)} %param.9), kind=kLoop, calls=%fused_computation.37 | loop fusion | bytes 1572864 | tf_op jit(solution)/shard_map/squeeze | solution.py:181
  2.4 1.1 copy-done.1
  4.2 5.7 %shard_map.96 = (f32[3,2,24,512]{3,2,1,0:T(8,128)S(1)}, f32[3,2,24,512]{3,2,1,0:T(8,128)S(1)}) custom-call(f32[2,2,24,512]{3,2,1,0:T(8,128)S(1)} %get-tuple-element.70.refs_0_, f32[2,2,24,512]{3,2,1,0:T(8,128)S(1)} %get-tuple-element.69.refs_1_, f32[2,2,24,2048]{3,2,1,0:T(8,128)S(1)} %copy-done.1, bf16[2,4,2,24,2048]{4,3,2,1,0:T(8,128)(2,1)S(1)} %copy-done, ...), custom_call_target="tpu_custom_call" | custom-call | flops 4026531840 | bytes 4194304 | tf_op jit(solution)/shard_map/pallas_call | solution.py:113
  10.0 5.6 %collective-permute-start.15 = (f32[3,2,24,512]{3,2,1,0:T(8,128)S(1)}, f32[3,2,24,512]{3,2,1,0:T(8,128)}, u32[]{:S(2)}, u32[]{:S(2)}) collective-permute-start(f32[3,2,24,512]{3,2,1,0:T(8,128)S(1)} %get-tuple-element.15), channel_id=1, source_target_pairs={{0,1},{3,2},{4,5},{7,6},{8,9},{11,10},{12,13},{15,14},{16,17},{19,... | collective-permute-start | bytes 884744 | tf_op jit(solution)/shard_map/ppermute | solution.py:148
  15.6 5.7 %shard_map.94 = (f32[3,2,24,512]{3,2,1,0:T(8,128)S(1)}, f32[3,2,24,512]{3,2,1,0:T(8,128)S(1)}) custom-call(f32[2,2,24,512]{3,2,1,0:T(8,128)S(1)} %get-tuple-element.71.refs_0_, f32[2,2,24,512]{3,2,1,0:T(8,128)S(1)} %get-tuple-element.68.refs_1_, f32[2,2,24,2048]{3,2,1,0:T(8,128)S(1)} %copy-done.1, bf16[2,4,2,24,2048]{4,3,2,1,0:T(8,128)(2,1)S(1)} %copy-done, ...), custom_call_target="tpu_custom_call" | custom-call | flops 4026531840 | bytes 4194304 | tf_op jit(solution)/shard_map/pallas_call | solution.py:113
  21.4 2.0 %collective-permute-start = (f32[3,2,24,512]{3,2,1,0:T(8,128)S(1)}, f32[3,2,24,512]{3,2,1,0:T(8,128)}, u32[]{:S(2)}, u32[]{:S(2)}) collective-permute-start(f32[3,2,24,512]{3,2,1,0:T(8,128)S(1)} %get-tuple-element.11), channel_id=1, source_target_pairs={{0,1},{3,2},{4,5},{7,6},{8,9},{11,10},{12,13},{15,14},{16,17},{19,... | collective-permute-start | bytes 884744 | tf_op jit(solution)/shard_map/ppermute | solution.py:148
  23.4 2.0 %collective-permute-start.18 = (f32[3,2,24,512]{3,2,1,0:T(8,128)S(1)}, f32[3,2,24,512]{3,2,1,0:T(8,128)}, u32[]{:S(2)}, u32[]{:S(2)}) collective-permute-start(f32[3,2,24,512]{3,2,1,0:T(8,128)S(1)} %get-tuple-element.16), channel_id=1, source_target_pairs={{0,1},{3,2},{4,5},{7,6},{8,9},{11,10},{12,13},{15,14},{16,17},{19,... | collective-permute-start | bytes 884744 | tf_op jit(solution)/shard_map/ppermute | solution.py:148
  25.4 1.3 collective-permute-start.3
  26.8 1.0 add.417
  27.8 1.4 collective-permute-start.16
  30.1 1.0 add.382
  31.1 1.4 collective-permute-start.1
  32.5 3.9 %collective-permute-done.18 = f32[3,2,24,512]{3,2,1,0:T(8,128)} collective-permute-done((f32[3,2,24,512]{3,2,1,0:T(8,128)S(1)}, f32[3,2,24,512]{3,2,1,0:T(8,128)}, u32[]{:S(2)}, u32[]{:S(2)}) %collective-permute-start.18) | collective-permute-done | bytes 294944 | tf_op jit(solution)/shard_map/ppermute | solution.py:148
  36.4 1.0 add.424
  38.1 3.5 %collective-permute-done.3 = f32[3,2,24,512]{3,2,1,0:T(8,128)S(1)} collective-permute-done((f32[3,2,24,512]{3,2,1,0:T(8,128)S(1)}, f32[3,2,24,512]{3,2,1,0:T(8,128)S(1)}, u32[]{:S(2)}, u32[]{:S(2)}) %collective-permute-start.3) | collective-permute-done | bytes 294944 | tf_op jit(solution)/shard_map/ppermute | solution.py:148
  42.3 1.0 add.418
  43.3 1.0 add.383
  44.6 1.3 collective-permute-start.2
  46.2 1.4 %collective-permute-start.5 = (f32[2,2,24,512]{3,2,1,0:T(8,128)S(1)}, f32[2,2,24,512]{3,2,1,0:T(8,128)S(1)}, u32[]{:S(2)}, u32[]{:S(2)}) collective-permute-start(f32[2,2,24,512]{3,2,1,0:T(8,128)S(1)} %pad_maximum_fusion.6), channel_id=1, source_target_pairs={{1,0},{2,3},{5,4},{6,7},{9,8},{10,11},{13,12},{14,15},{17,16},{18,... | collective-permute-start | bytes 589832 | tf_op jit(solution)/shard_map/ppermute | solution.py:153
  47.6 1.3 collective-permute-start.17
  49.0 1.3 collective-permute-start.20
  50.3 4.6 %collective-permute-done.2 = f32[2,2,24,512]{3,2,1,0:T(8,128)S(1)} collective-permute-done((f32[2,2,24,512]{3,2,1,0:T(8,128)S(1)}, f32[2,2,24,512]{3,2,1,0:T(8,128)S(1)}, u32[]{:S(2)}, u32[]{:S(2)}) %collective-permute-start.2) | collective-permute-done | bytes 196640 | tf_op jit(solution)/shard_map/ppermute | solution.py:153
  54.9 7.5 %collective-permute-done.5 = f32[2,2,24,512]{3,2,1,0:T(8,128)S(1)} collective-permute-done((f32[2,2,24,512]{3,2,1,0:T(8,128)S(1)}, f32[2,2,24,512]{3,2,1,0:T(8,128)S(1)}, u32[]{:S(2)}, u32[]{:S(2)}) %collective-permute-start.5) | collective-permute-done | bytes 196640 | tf_op jit(solution)/shard_map/ppermute | solution.py:153
  62.5 5.8 %shard_map.95 = (f32[3,2,24,512]{3,2,1,0:T(8,128)S(1)}, f32[3,2,24,512]{3,2,1,0:T(8,128)S(1)}) custom-call(f32[2,2,24,512]{3,2,1,0:T(8,128)S(1)} %broadcast_select_fusion.7.refs_0_, f32[2,2,24,512]{3,2,1,0:T(8,128)S(1)} %broadcast_select_fusion.6.refs_1_, f32[2,2,24,2048]{3,2,1,0:T(8,128)S(1)} %copy-done.2, bf16[2,4,2,24,2048]{4,3,2,1,0:T(8,128)(2,1)S(1)} %copy-done, ...), custom_call_target="tpu_custom_call" | custom-call | flops 4026531840 | bytes 4194304 | tf_op jit(solution)/shard_map/pallas_call | solution.py:113
  68.3 1.5 %collective-permute-start.12 = (f32[3,2,24,512]{3,2,1,0:T(8,128)S(1)}, f32[3,2,24,512]{3,2,1,0:T(8,128)S(1)}, u32[]{:S(2)}, u32[]{:S(2)}) collective-permute-start(f32[3,2,24,512]{3,2,1,0:T(8,128)S(1)} %get-tuple-element.14), channel_id=1, source_target_pairs={{0,1},{3,2},{4,5},{7,6},{8,9},{11,10},{12,13},{15,14},{16,17},{19,... | collective-permute-start | bytes 884744 | tf_op jit(solution)/shard_map/ppermute | solution.py:148
  69.7 1.5 %collective-permute-start.6 = (f32[3,2,24,512]{3,2,1,0:T(8,128)S(1)}, f32[3,2,24,512]{3,2,1,0:T(8,128)S(1)}, u32[]{:S(2)}, u32[]{:S(2)}) collective-permute-start(f32[3,2,24,512]{3,2,1,0:T(8,128)S(1)} %get-tuple-element.13), channel_id=1, source_target_pairs={{0,1},{3,2},{4,5},{7,6},{8,9},{11,10},{12,13},{15,14},{16,17},{19,... | collective-permute-start | bytes 884744 | tf_op jit(solution)/shard_map/ppermute | solution.py:148
  73.2 1.6 %collective-permute-start.24 = (f32[4,2,4,512]{3,2,1,0:T(4,128)S(1)}, f32[4,2,4,512]{3,2,1,0:T(4,128)S(1)}, u32[]{:S(2)}, u32[]{:S(2)}) collective-permute-start(f32[4,2,4,512]{3,2,1,0:T(4,128)S(1)} %fusion.52), channel_id=1, source_target_pairs={{0,8},{4,12},{8,0},{12,4},{16,24},{20,28},{24,16},{28,20},{1,9},{5... | collective-permute-start | bytes 196616 | tf_op jit(solution)/shard_map/ppermute | solution.py:163
  75.4 2.4 %collective-permute-done.24 = f32[4,2,4,512]{3,2,1,0:T(4,128)S(1)} collective-permute-done((f32[4,2,4,512]{3,2,1,0:T(4,128)S(1)}, f32[4,2,4,512]{3,2,1,0:T(4,128)S(1)}, u32[]{:S(2)}, u32[]{:S(2)}) %collective-permute-start.24) | collective-permute-done | bytes 65568 | tf_op jit(solution)/shard_map/ppermute | solution.py:163
  77.9 1.6 %collective-permute-start.25 = (f32[4,2,4,512]{3,2,1,0:T(4,128)S(1)}, f32[4,2,4,512]{3,2,1,0:T(4,128)S(1)}, u32[]{:S(2)}, u32[]{:S(2)}) collective-permute-start(f32[4,2,4,512]{3,2,1,0:T(4,128)S(1)} %fusion.61), channel_id=1, source_target_pairs={{0,16},{4,20},{8,24},{12,28},{16,0},{20,4},{24,8},{28,12},{1,17},{... | collective-permute-start | bytes 196616 | tf_op jit(solution)/shard_map/ppermute | solution.py:163
  79.5 1.3 collective-permute-start.10
  80.8 5.7 %shard_map.97 = (f32[3,2,24,512]{3,2,1,0:T(8,128)S(1)}, f32[3,2,24,512]{3,2,1,0:T(8,128)S(1)}) custom-call(f32[2,2,24,512]{3,2,1,0:T(8,128)S(1)} %broadcast_select_fusion.3.refs_0_, f32[2,2,24,512]{3,2,1,0:T(8,128)S(1)} %broadcast_select_fusion.2.refs_1_, f32[2,2,24,2048]{3,2,1,0:T(8,128)S(1)} %copy-done.2, bf16[2,4,2,24,2048]{4,3,2,1,0:T(8,128)(2,1)S(1)} %copy-done, ...), custom_call_target="tpu_custom_call" | custom-call | flops 4026531840 | bytes 4194304 | tf_op jit(solution)/shard_map/pallas_call | solution.py:113
  86.5 1.3 collective-permute-start.27
  87.8 1.3 collective-permute-start.21
  91.1 4.2 %collective-permute-done.27 = f32[3,2,24,512]{3,2,1,0:T(8,128)S(1)} collective-permute-done((f32[3,2,24,512]{3,2,1,0:T(8,128)S(1)}, f32[3,2,24,512]{3,2,1,0:T(8,128)S(1)}, u32[]{:S(2)}, u32[]{:S(2)}) %collective-permute-start.27) | collective-permute-done | bytes 294944 | tf_op jit(solution)/shard_map/ppermute | solution.py:148
  96.0 3.5 %collective-permute-done.21 = f32[3,2,24,512]{3,2,1,0:T(8,128)S(1)} collective-permute-done((f32[3,2,24,512]{3,2,1,0:T(8,128)S(1)}, f32[3,2,24,512]{3,2,1,0:T(8,128)S(1)}, u32[]{:S(2)}, u32[]{:S(2)}) %collective-permute-start.21) | collective-permute-done | bytes 294944 | tf_op jit(solution)/shard_map/ppermute | solution.py:148
  100.6 1.3 collective-permute-start.11
  101.9 1.3 collective-permute-start.14
  103.5 1.3 collective-permute-start.26
  104.9 1.3 collective-permute-start.29
  106.2 5.8 %collective-permute-done.11 = f32[2,2,24,512]{3,2,1,0:T(8,128)S(1)} collective-permute-done((f32[2,2,24,512]{3,2,1,0:T(8,128)S(1)}, f32[2,2,24,512]{3,2,1,0:T(8,128)S(1)}, u32[]{:S(2)}, u32[]{:S(2)}) %collective-permute-start.11) | collective-permute-done | bytes 196640 | tf_op jit(solution)/shard_map/ppermute | solution.py:153
  112.0 2.1 %collective-permute-done.14 = f32[2,2,24,512]{3,2,1,0:T(8,128)S(1)} collective-permute-done((f32[2,2,24,512]{3,2,1,0:T(8,128)S(1)}, f32[2,2,24,512]{3,2,1,0:T(8,128)S(1)}, u32[]{:S(2)}, u32[]{:S(2)}) %collective-permute-start.14) | collective-permute-done | bytes 196640 | tf_op jit(solution)/shard_map/ppermute | solution.py:153
  114.2 9.9 %collective-permute-done.26 = f32[2,2,24,512]{3,2,1,0:T(8,128)S(1)} collective-permute-done((f32[2,2,24,512]{3,2,1,0:T(8,128)S(1)}, f32[2,2,24,512]{3,2,1,0:T(8,128)S(1)}, u32[]{:S(2)}, u32[]{:S(2)}) %collective-permute-start.26) | collective-permute-done | bytes 196640 | tf_op jit(solution)/shard_map/ppermute | solution.py:153
  124.1 2.1 %collective-permute-done.29 = f32[2,2,24,512]{3,2,1,0:T(8,128)S(1)} collective-permute-done((f32[2,2,24,512]{3,2,1,0:T(8,128)S(1)}, f32[2,2,24,512]{3,2,1,0:T(8,128)S(1)}, u32[]{:S(2)}, u32[]{:S(2)}) %collective-permute-start.29) | collective-permute-done | bytes 196640 | tf_op jit(solution)/shard_map/ppermute | solution.py:153
  128.1 1.5 %collective-permute-start.34 = (f32[4,2,4,128]{3,2,1,0:T(4,128)S(1)}, f32[4,2,4,128]{3,2,1,0:T(4,128)S(1)}, u32[]{:S(2)}, u32[]{:S(2)}) collective-permute-start(f32[4,2,4,128]{3,2,1,0:T(4,128)S(1)} %fusion.50), channel_id=1, source_target_pairs={{0,8},{4,12},{8,0},{12,4},{16,24},{20,28},{24,16},{28,20},{1,9},{5... | collective-permute-start | bytes 49160 | tf_op jit(solution)/shard_map/ppermute | solution.py:163
  130.3 1.6 %collective-permute-done.34 = f32[4,2,4,128]{3,2,1,0:T(4,128)S(1)} collective-permute-done((f32[4,2,4,128]{3,2,1,0:T(4,128)S(1)}, f32[4,2,4,128]{3,2,1,0:T(4,128)S(1)}, u32[]{:S(2)}, u32[]{:S(2)}) %collective-permute-start.34) | collective-permute-done | bytes 16416 | tf_op jit(solution)/shard_map/ppermute | solution.py:163
  132.2 1.2 collective-permute-done.31
  134.1 1.6 %collective-permute-done.35 = f32[4,2,4,128]{3,2,1,0:T(4,128)S(1)} collective-permute-done((f32[4,2,4,128]{3,2,1,0:T(4,128)S(1)}, f32[4,2,4,128]{3,2,1,0:T(4,128)S(1)}, u32[]{:S(2)}, u32[]{:S(2)}) %collective-permute-start.35) | collective-permute-done | bytes 16416 | tf_op jit(solution)/shard_map/ppermute | solution.py:163
  135.7 1.5 %collective-permute-done.32 = f32[4,2,4,128]{3,2,1,0:T(4,128)S(1)} collective-permute-done((f32[4,2,4,128]{3,2,1,0:T(4,128)S(1)}, f32[4,2,4,128]{3,2,1,0:T(4,128)S(1)}, u32[]{:S(2)}, u32[]{:S(2)}) %collective-permute-start.32) | collective-permute-done | bytes 16416 | tf_op jit(solution)/shard_map/ppermute | solution.py:163
  (119 shorter events, 16.0 us)
Async XLA Ops:
  0.6 1.8 %copy-start = (bf16[2,4,2,24,2048]{4,3,2,1,0:T(8,128)(2,1)S(1)}, bf16[2,4,2,24,2048]{4,3,2,1,0:T(8,128)(2,1)}, u32[]{:S(2)}) copy-start(bf16[2,4,2,24,2048]{4,3,2,1,0:T(8,128)(2,1)} %refs_3_.7) | copy-start | bytes 4718596
  2.4 1.1 copy-start.1
  3.5 0.7 copy-start.3
  4.2 11.4 %copy-start.4 = (s32[2,2048]{1,0:T(2,128)S(1)}, s32[2,2048]{1,0:T(2,128)}, u32[]{:S(2)}) copy-start(s32[2,2048]{1,0:T(2,128)} %refs_4_.7) | copy-start | bytes 49156
  10.0 16.8 %collective-permute-start.15 = (f32[3,2,24,512]{3,2,1,0:T(8,128)S(1)}, f32[3,2,24,512]{3,2,1,0:T(8,128)}, u32[]{:S(2)}, u32[]{:S(2)}) collective-permute-start(f32[3,2,24,512]{3,2,1,0:T(8,128)S(1)} %get-tuple-element.15), channel_id=1, source_target_pairs={{0,1},{3,2},{4,5},{7,6},{8,9},{11,10},{12,13},{15,14},{16,17},{19,... | collective-permute-start | bytes 884744 | tf_op jit(solution)/shard_map/ppermute | solution.py:148
  15.6 11.1 %copy-start.7 = (f32[192,4]{0,1:T(4,128)S(1)}, f32[192,4]{0,1:T(4,128)}, u32[]{:S(2)}) copy-start(f32[192,4]{0,1:T(4,128)} %constant.27.clone) | copy-start | bytes 9220
  15.6 11.1 %copy-start.8 = (f32[192,4]{0,1:T(4,128)S(1)}, f32[192,4]{0,1:T(4,128)}, u32[]{:S(2)}) copy-start(f32[192,4]{0,1:T(4,128)} %constant.28.clone) | copy-start | bytes 9220
  21.4 11.1 %copy-start.6 = (f32[4]{0:T(128)S(1)}, f32[4]{0:T(128)}, u32[]{:S(2)}) copy-start(f32[4]{0:T(128)} %param.10) | copy-start | bytes 52
  21.4 8.7 %collective-permute-start = (f32[3,2,24,512]{3,2,1,0:T(8,128)S(1)}, f32[3,2,24,512]{3,2,1,0:T(8,128)}, u32[]{:S(2)}, u32[]{:S(2)}) collective-permute-start(f32[3,2,24,512]{3,2,1,0:T(8,128)S(1)} %get-tuple-element.11), channel_id=1, source_target_pairs={{0,1},{3,2},{4,5},{7,6},{8,9},{11,10},{12,13},{15,14},{16,17},{19,... | collective-permute-start | bytes 884744 | tf_op jit(solution)/shard_map/ppermute | solution.py:148
  23.4 13.0 %collective-permute-start.18 = (f32[3,2,24,512]{3,2,1,0:T(8,128)S(1)}, f32[3,2,24,512]{3,2,1,0:T(8,128)}, u32[]{:S(2)}, u32[]{:S(2)}) collective-permute-start(f32[3,2,24,512]{3,2,1,0:T(8,128)S(1)} %get-tuple-element.16), channel_id=1, source_target_pairs={{0,1},{3,2},{4,5},{7,6},{8,9},{11,10},{12,13},{15,14},{16,17},{19,... | collective-permute-start | bytes 884744 | tf_op jit(solution)/shard_map/ppermute | solution.py:148
  25.4 16.2 %collective-permute-start.3 = (f32[3,2,24,512]{3,2,1,0:T(8,128)S(1)}, f32[3,2,24,512]{3,2,1,0:T(8,128)S(1)}, u32[]{:S(2)}, u32[]{:S(2)}) collective-permute-start(f32[3,2,24,512]{3,2,1,0:T(8,128)S(1)} %get-tuple-element.12), channel_id=1, source_target_pairs={{0,1},{3,2},{4,5},{7,6},{8,9},{11,10},{12,13},{15,14},{16,17},{19,... | collective-permute-start | bytes 884744 | tf_op jit(solution)/shard_map/ppermute | solution.py:148
  27.8 14.5 %collective-permute-start.16 = (f32[3,2,24,512]{3,2,1,0:T(8,128)S(1)}, f32[3,2,24,512]{3,2,1,0:T(8,128)}, u32[]{:S(2)}, u32[]{:S(2)}) collective-permute-start(f32[3,2,24,512]{3,2,1,0:T(8,128)S(1)} %add.417), channel_id=1, source_target_pairs={{1,2},{2,1},{5,6},{6,5},{9,10},{10,9},{13,14},{14,13},{17,18},{18,... | collective-permute-start | bytes 884744 | tf_op jit(solution)/shard_map/ppermute | solution.py:149
  31.1 12.2 %collective-permute-start.1 = (f32[3,2,24,512]{3,2,1,0:T(8,128)S(1)}, f32[3,2,24,512]{3,2,1,0:T(8,128)}, u32[]{:S(2)}, u32[]{:S(2)}) collective-permute-start(f32[3,2,24,512]{3,2,1,0:T(8,128)S(1)} %add.382), channel_id=1, source_target_pairs={{1,2},{2,1},{5,6},{6,5},{9,10},{10,9},{13,14},{14,13},{17,18},{18,... | collective-permute-start | bytes 884744 | tf_op jit(solution)/shard_map/ppermute | solution.py:149
  32.5 11.8 %copy-start.5 = (f32[2,4,2,24,512]{4,3,2,1,0:T(8,128)S(1)}, f32[2,4,2,24,512]{4,3,2,1,0:T(8,128)}, u32[]{:S(2)}) copy-start(f32[2,4,2,24,512]{4,3,2,1,0:T(8,128)} %param.9) | copy-start | bytes 2359300
  37.4 8.5 %collective-permute-start.19 = (f32[3,2,24,512]{3,2,1,0:T(8,128)S(1)}, f32[3,2,24,512]{3,2,1,0:T(8,128)S(1)}, u32[]{:S(2)}, u32[]{:S(2)}) collective-permute-start(f32[3,2,24,512]{3,2,1,0:T(8,128)S(1)} %add.424), channel_id=1, source_target_pairs={{1,2},{2,1},{5,6},{6,5},{9,10},{10,9},{13,14},{14,13},{17,18},{18,... | collective-permute-start | bytes 884744 | tf_op jit(solution)/shard_map/ppermute | solution.py:149
  41.6 4.3 %collective-permute-start.4 = (f32[3,2,24,512]{3,2,1,0:T(8,128)S(1)}, f32[3,2,24,512]{3,2,1,0:T(8,128)S(1)}, u32[]{:S(2)}, u32[]{:S(2)}) collective-permute-start(f32[3,2,24,512]{3,2,1,0:T(8,128)S(1)} %add.389), channel_id=1, source_target_pairs={{1,2},{2,1},{5,6},{6,5},{9,10},{10,9},{13,14},{14,13},{17,18},{18,... | collective-permute-start | bytes 884744 | tf_op jit(solution)/shard_map/ppermute | solution.py:149
  44.6 10.3 %collective-permute-start.2 = (f32[2,2,24,512]{3,2,1,0:T(8,128)S(1)}, f32[2,2,24,512]{3,2,1,0:T(8,128)S(1)}, u32[]{:S(2)}, u32[]{:S(2)}) collective-permute-start(f32[2,2,24,512]{3,2,1,0:T(8,128)S(1)} %pad_maximum_fusion.5), channel_id=1, source_target_pairs={{1,0},{2,3},{5,4},{6,7},{9,8},{10,11},{13,12},{14,15},{17,16},{18,... | collective-permute-start | bytes 589832 | tf_op jit(solution)/shard_map/ppermute | solution.py:153
  46.0 16.5 %copy-start.2 = (f32[2,2,24,2048]{3,2,1,0:T(8,128)S(1)}, f32[2,2,24,2048]{3,2,1,0:T(8,128)}, u32[]{:S(2)}) copy-start(f32[2,2,24,2048]{3,2,1,0:T(8,128)} %refs_2_.7) | copy-start | bytes 2359300
  46.2 16.2 %collective-permute-start.5 = (f32[2,2,24,512]{3,2,1,0:T(8,128)S(1)}, f32[2,2,24,512]{3,2,1,0:T(8,128)S(1)}, u32[]{:S(2)}, u32[]{:S(2)}) collective-permute-start(f32[2,2,24,512]{3,2,1,0:T(8,128)S(1)} %pad_maximum_fusion.6), channel_id=1, source_target_pairs={{1,0},{2,3},{5,4},{6,7},{9,8},{10,11},{13,12},{14,15},{17,16},{18,... | collective-permute-start | bytes 589832 | tf_op jit(solution)/shard_map/ppermute | solution.py:153
  47.6 23.6 %collective-permute-start.17 = (f32[2,2,24,512]{3,2,1,0:T(8,128)S(1)}, f32[2,2,24,512]{3,2,1,0:T(8,128)S(1)}, u32[]{:S(2)}, u32[]{:S(2)}) collective-permute-start(f32[2,2,24,512]{3,2,1,0:T(8,128)S(1)} %pad_maximum_fusion.9), channel_id=1, source_target_pairs={{1,0},{2,3},{5,4},{6,7},{9,8},{10,11},{13,12},{14,15},{17,16},{18,... | collective-permute-start | bytes 589832 | tf_op jit(solution)/shard_map/ppermute | solution.py:153
  49.0 22.3 %collective-permute-start.20 = (f32[2,2,24,512]{3,2,1,0:T(8,128)S(1)}, f32[2,2,24,512]{3,2,1,0:T(8,128)S(1)}, u32[]{:S(2)}, u32[]{:S(2)}) collective-permute-start(f32[2,2,24,512]{3,2,1,0:T(8,128)S(1)} %pad_maximum_fusion.10), channel_id=1, source_target_pairs={{1,0},{2,3},{5,4},{6,7},{9,8},{10,11},{13,12},{14,15},{17,16},{18,... | collective-permute-start | bytes 589832 | tf_op jit(solution)/shard_map/ppermute | solution.py:153
  68.3 21.0 %collective-permute-start.12 = (f32[3,2,24,512]{3,2,1,0:T(8,128)S(1)}, f32[3,2,24,512]{3,2,1,0:T(8,128)S(1)}, u32[]{:S(2)}, u32[]{:S(2)}) collective-permute-start(f32[3,2,24,512]{3,2,1,0:T(8,128)S(1)} %get-tuple-element.14), channel_id=1, source_target_pairs={{0,1},{3,2},{4,5},{7,6},{8,9},{11,10},{12,13},{15,14},{16,17},{19,... | collective-permute-start | bytes 884744 | tf_op jit(solution)/shard_map/ppermute | solution.py:148
  69.7 20.3 %collective-permute-start.6 = (f32[3,2,24,512]{3,2,1,0:T(8,128)S(1)}, f32[3,2,24,512]{3,2,1,0:T(8,128)S(1)}, u32[]{:S(2)}, u32[]{:S(2)}) collective-permute-start(f32[3,2,24,512]{3,2,1,0:T(8,128)S(1)} %get-tuple-element.13), channel_id=1, source_target_pairs={{0,1},{3,2},{4,5},{7,6},{8,9},{11,10},{12,13},{15,14},{16,17},{19,... | collective-permute-start | bytes 884744 | tf_op jit(solution)/shard_map/ppermute | solution.py:148
  71.9 1.3 collective-permute-start.23
  72.0 2.8 %collective-permute-start.8 = (f32[4,2,4,512]{3,2,1,0:T(4,128)S(1)}, f32[4,2,4,512]{3,2,1,0:T(4,128)S(1)}, u32[]{:S(2)}, u32[]{:S(2)}) collective-permute-start(f32[4,2,4,512]{3,2,1,0:T(4,128)S(1)} %pad_maximum_fusion.15), channel_id=1, source_target_pairs={{0,4},{4,0},{8,12},{12,8},{16,20},{20,16},{24,28},{28,24},{1,5},{5... | collective-permute-start | bytes 196616 | tf_op jit(solution)/shard_map/ppermute | solution.py:163
  73.2 4.6 %collective-permute-start.24 = (f32[4,2,4,512]{3,2,1,0:T(4,128)S(1)}, f32[4,2,4,512]{3,2,1,0:T(4,128)S(1)}, u32[]{:S(2)}, u32[]{:S(2)}) collective-permute-start(f32[4,2,4,512]{3,2,1,0:T(4,128)S(1)} %fusion.52), channel_id=1, source_target_pairs={{0,8},{4,12},{8,0},{12,4},{16,24},{20,28},{24,16},{28,20},{1,9},{5... | collective-permute-start | bytes 196616 | tf_op jit(solution)/shard_map/ppermute | solution.py:163
  74.8 4.6 %collective-permute-start.9 = (f32[4,2,4,512]{3,2,1,0:T(4,128)S(1)}, f32[4,2,4,512]{3,2,1,0:T(4,128)S(1)}, u32[]{:S(2)}, u32[]{:S(2)}) collective-permute-start(f32[4,2,4,512]{3,2,1,0:T(4,128)S(1)} %fusion.53), channel_id=1, source_target_pairs={{0,8},{4,12},{8,0},{12,4},{16,24},{20,28},{24,16},{28,20},{1,9},{5... | collective-permute-start | bytes 196616 | tf_op jit(solution)/shard_map/ppermute | solution.py:163
  77.9 9.9 %collective-permute-start.25 = (f32[4,2,4,512]{3,2,1,0:T(4,128)S(1)}, f32[4,2,4,512]{3,2,1,0:T(4,128)S(1)}, u32[]{:S(2)}, u32[]{:S(2)}) collective-permute-start(f32[4,2,4,512]{3,2,1,0:T(4,128)S(1)} %fusion.61), channel_id=1, source_target_pairs={{0,16},{4,20},{8,24},{12,28},{16,0},{20,4},{24,8},{28,12},{1,17},{... | collective-permute-start | bytes 196616 | tf_op jit(solution)/shard_map/ppermute | solution.py:163
  79.5 9.7 %collective-permute-start.10 = (f32[4,2,4,512]{3,2,1,0:T(4,128)S(1)}, f32[4,2,4,512]{3,2,1,0:T(4,128)S(1)}, u32[]{:S(2)}, u32[]{:S(2)}) collective-permute-start(f32[4,2,4,512]{3,2,1,0:T(4,128)S(1)} %fusion.62), channel_id=1, source_target_pairs={{0,16},{4,20},{8,24},{12,28},{16,0},{20,4},{24,8},{28,12},{1,17},{... | collective-permute-start | bytes 196616 | tf_op jit(solution)/shard_map/ppermute | solution.py:163
  86.5 8.7 %collective-permute-start.27 = (f32[3,2,24,512]{3,2,1,0:T(8,128)S(1)}, f32[3,2,24,512]{3,2,1,0:T(8,128)S(1)}, u32[]{:S(2)}, u32[]{:S(2)}) collective-permute-start(f32[3,2,24,512]{3,2,1,0:T(8,128)S(1)} %get-tuple-element.18), channel_id=1, source_target_pairs={{0,1},{3,2},{4,5},{7,6},{8,9},{11,10},{12,13},{15,14},{16,17},{19,... | collective-permute-start | bytes 884744 | tf_op jit(solution)/shard_map/ppermute | solution.py:148
  87.8 11.6 %collective-permute-start.21 = (f32[3,2,24,512]{3,2,1,0:T(8,128)S(1)}, f32[3,2,24,512]{3,2,1,0:T(8,128)S(1)}, u32[]{:S(2)}, u32[]{:S(2)}) collective-permute-start(f32[3,2,24,512]{3,2,1,0:T(8,128)S(1)} %get-tuple-element.17), channel_id=1, source_target_pairs={{0,1},{3,2},{4,5},{7,6},{8,9},{11,10},{12,13},{15,14},{16,17},{19,... | collective-permute-start | bytes 884744 | tf_op jit(solution)/shard_map/ppermute | solution.py:148
  89.3 10.9 %collective-permute-start.13 = (f32[3,2,24,512]{3,2,1,0:T(8,128)S(1)}, f32[3,2,24,512]{3,2,1,0:T(8,128)S(1)}, u32[]{:S(2)}, u32[]{:S(2)}) collective-permute-start(f32[3,2,24,512]{3,2,1,0:T(8,128)S(1)} %add.410), channel_id=1, source_target_pairs={{1,2},{2,1},{5,6},{6,5},{9,10},{10,9},{13,14},{14,13},{17,18},{18,... | collective-permute-start | bytes 884744 | tf_op jit(solution)/shard_map/ppermute | solution.py:149
  90.0 10.2 %collective-permute-start.7 = (f32[3,2,24,512]{3,2,1,0:T(8,128)S(1)}, f32[3,2,24,512]{3,2,1,0:T(8,128)S(1)}, u32[]{:S(2)}, u32[]{:S(2)}) collective-permute-start(f32[3,2,24,512]{3,2,1,0:T(8,128)S(1)} %add.396), channel_id=1, source_target_pairs={{1,2},{2,1},{5,6},{6,5},{9,10},{10,9},{13,14},{14,13},{17,18},{18,... | collective-permute-start | bytes 884744 | tf_op jit(solution)/shard_map/ppermute | solution.py:149
  95.3 7.9 %collective-permute-start.28 = (f32[3,2,24,512]{3,2,1,0:T(8,128)S(1)}, f32[3,2,24,512]{3,2,1,0:T(8,128)S(1)}, u32[]{:S(2)}, u32[]{:S(2)}) collective-permute-start(f32[3,2,24,512]{3,2,1,0:T(8,128)S(1)} %add.444), channel_id=1, source_target_pairs={{1,2},{2,1},{5,6},{6,5},{9,10},{10,9},{13,14},{14,13},{17,18},{18,... | collective-permute-start | bytes 884744 | tf_op jit(solution)/shard_map/ppermute | solution.py:149
  99.5 3.7 %collective-permute-start.22 = (f32[3,2,24,512]{3,2,1,0:T(8,128)S(1)}, f32[3,2,24,512]{3,2,1,0:T(8,128)S(1)}, u32[]{:S(2)}, u32[]{:S(2)}) collective-permute-start(f32[3,2,24,512]{3,2,1,0:T(8,128)S(1)} %add.431), channel_id=1, source_target_pairs={{1,2},{2,1},{5,6},{6,5},{9,10},{10,9},{13,14},{14,13},{17,18},{18,... | collective-permute-start | bytes 884744 | tf_op jit(solution)/shard_map/ppermute | solution.py:149
  100.6 11.4 %collective-permute-start.11 = (f32[2,2,24,512]{3,2,1,0:T(8,128)S(1)}, f32[2,2,24,512]{3,2,1,0:T(8,128)S(1)}, u32[]{:S(2)}, u32[]{:S(2)}) collective-permute-start(f32[2,2,24,512]{3,2,1,0:T(8,128)S(1)} %pad_maximum_fusion.7), channel_id=1, source_target_pairs={{1,0},{2,3},{5,4},{6,7},{9,8},{10,11},{13,12},{14,15},{17,16},{18,... | collective-permute-start | bytes 589832 | tf_op jit(solution)/shard_map/ppermute | solution.py:153
  101.9 12.2 %collective-permute-start.14 = (f32[2,2,24,512]{3,2,1,0:T(8,128)S(1)}, f32[2,2,24,512]{3,2,1,0:T(8,128)S(1)}, u32[]{:S(2)}, u32[]{:S(2)}) collective-permute-start(f32[2,2,24,512]{3,2,1,0:T(8,128)S(1)} %pad_maximum_fusion.8), channel_id=1, source_target_pairs={{1,0},{2,3},{5,4},{6,7},{9,8},{10,11},{13,12},{14,15},{17,16},{18,... | collective-permute-start | bytes 589832 | tf_op jit(solution)/shard_map/ppermute | solution.py:153
  103.5 20.5 %collective-permute-start.26 = (f32[2,2,24,512]{3,2,1,0:T(8,128)S(1)}, f32[2,2,24,512]{3,2,1,0:T(8,128)S(1)}, u32[]{:S(2)}, u32[]{:S(2)}) collective-permute-start(f32[2,2,24,512]{3,2,1,0:T(8,128)S(1)} %pad_maximum_fusion.11), channel_id=1, source_target_pairs={{1,0},{2,3},{5,4},{6,7},{9,8},{10,11},{13,12},{14,15},{17,16},{18,... | collective-permute-start | bytes 589832 | tf_op jit(solution)/shard_map/ppermute | solution.py:153
  104.9 21.3 %collective-permute-start.29 = (f32[2,2,24,512]{3,2,1,0:T(8,128)S(1)}, f32[2,2,24,512]{3,2,1,0:T(8,128)S(1)}, u32[]{:S(2)}, u32[]{:S(2)}) collective-permute-start(f32[2,2,24,512]{3,2,1,0:T(8,128)S(1)} %pad_maximum_fusion.12), channel_id=1, source_target_pairs={{1,0},{2,3},{5,4},{6,7},{9,8},{10,11},{13,12},{14,15},{17,16},{18,... | collective-permute-start | bytes 589832 | tf_op jit(solution)/shard_map/ppermute | solution.py:153
  126.5 1.6 %collective-permute-start.33 = (f32[4,2,4,128]{3,2,1,0:T(4,128)S(1)}, f32[4,2,4,128]{3,2,1,0:T(4,128)S(1)}, u32[]{:S(2)}, u32[]{:S(2)}) collective-permute-start(f32[4,2,4,128]{3,2,1,0:T(4,128)S(1)} %pad_maximum_fusion.18), channel_id=1, source_target_pairs={{0,4},{4,0},{8,12},{12,8},{16,20},{20,16},{24,28},{28,24},{1,5},{5... | collective-permute-start | bytes 49160 | tf_op jit(solution)/shard_map/ppermute | solution.py:163
  126.6 3.0 %collective-permute-start.30 = (f32[4,2,4,128]{3,2,1,0:T(4,128)S(1)}, f32[4,2,4,128]{3,2,1,0:T(4,128)S(1)}, u32[]{:S(2)}, u32[]{:S(2)}) collective-permute-start(f32[4,2,4,128]{3,2,1,0:T(4,128)S(1)} %pad_maximum_fusion.17), channel_id=1, source_target_pairs={{0,4},{4,0},{8,12},{12,8},{16,20},{20,16},{24,28},{28,24},{1,5},{5... | collective-permute-start | bytes 49160 | tf_op jit(solution)/shard_map/ppermute | solution.py:163
  128.1 3.8 %collective-permute-start.34 = (f32[4,2,4,128]{3,2,1,0:T(4,128)S(1)}, f32[4,2,4,128]{3,2,1,0:T(4,128)S(1)}, u32[]{:S(2)}, u32[]{:S(2)}) collective-permute-start(f32[4,2,4,128]{3,2,1,0:T(4,128)S(1)} %fusion.50), channel_id=1, source_target_pairs={{0,8},{4,12},{8,0},{12,4},{16,24},{20,28},{24,16},{28,20},{1,9},{5... | collective-permute-start | bytes 49160 | tf_op jit(solution)/shard_map/ppermute | solution.py:163
  129.5 3.8 %collective-permute-start.31 = (f32[4,2,4,128]{3,2,1,0:T(4,128)S(1)}, f32[4,2,4,128]{3,2,1,0:T(4,128)S(1)}, u32[]{:S(2)}, u32[]{:S(2)}) collective-permute-start(f32[4,2,4,128]{3,2,1,0:T(4,128)S(1)} %fusion.51), channel_id=1, source_target_pairs={{0,8},{4,12},{8,0},{12,4},{16,24},{20,28},{24,16},{28,20},{1,9},{5... | collective-permute-start | bytes 49160 | tf_op jit(solution)/shard_map/ppermute | solution.py:163
  131.9 3.8 %collective-permute-start.35 = (f32[4,2,4,128]{3,2,1,0:T(4,128)S(1)}, f32[4,2,4,128]{3,2,1,0:T(4,128)S(1)}, u32[]{:S(2)}, u32[]{:S(2)}) collective-permute-start(f32[4,2,4,128]{3,2,1,0:T(4,128)S(1)} %fusion.59), channel_id=1, source_target_pairs={{0,16},{4,20},{8,24},{12,28},{16,0},{20,4},{24,8},{28,12},{1,17},{... | collective-permute-start | bytes 49160 | tf_op jit(solution)/shard_map/ppermute | solution.py:163
  133.4 3.8 %collective-permute-start.32 = (f32[4,2,4,128]{3,2,1,0:T(4,128)S(1)}, f32[4,2,4,128]{3,2,1,0:T(4,128)S(1)}, u32[]{:S(2)}, u32[]{:S(2)}) collective-permute-start(f32[4,2,4,128]{3,2,1,0:T(4,128)S(1)} %fusion.60), channel_id=1, source_target_pairs={{0,16},{4,20},{8,24},{12,28},{16,0},{20,4},{24,8},{28,12},{1,17},{... | collective-permute-start | bytes 49160 | tf_op jit(solution)/shard_map/ppermute | solution.py:163

commit v2 on v1

v2 whole, which is shorter than its diff:
```python
import functools
import math

import jax
import jax.numpy as jnp
import numpy as np
from jax import lax
from jax.experimental import pallas as pl
from jax.experimental.pallas import tpu as pltpu
from jax.sharding import PartitionSpec as P

POLY = 4
ITERS = 2
GROUPS = 2
LANES = 128
ROWS_BY_COLS = (((1,), (0,)), ((), ()))
ROWS_BY_ROWS = (((1,), (1,)), ((), ()))
VMEM = pltpu.MemorySpace.VMEM
SMEM = pltpu.MemorySpace.SMEM


def bernstein_tables(total):
    position = (np.arange(total) + 0.5) / total
    basis = np.stack(
        [math.comb(POLY - 1, j) * position**j * (1.0 - position) ** (POLY - 1 - j) for j in range(POLY)], axis=1
    )
    factor = np.linalg.cholesky(basis.T @ basis)
    solved = np.linalg.solve(factor.T, np.linalg.solve(factor, basis.T)).T
    return basis.astype(np.float32), solved.astype(np.float32)


def split(values):
    upper = values.astype(jnp.bfloat16)
    return upper, (values - upper.astype(jnp.float32)).astype(jnp.bfloat16)


def normals_kernel(dirs, chans, line, share, time, start, build, *refs):
    refs = list(refs)
    count = line * share
    half = dirs // GROUPS
    if start:
        place_ref, gain_ref = refs.pop(0), refs.pop(0)
        if share % LANES:
            offsets = [r * share for r in range(line)]
        else:
            offsets = [pl.multiple_of((place_ref[0] ^ r) * share, LANES) for r in range(line)]
        blocks = [
            gain_ref[:, :, time, :, pl.ds(offset, share)].reshape(2 * dirs * chans, share) for offset in offsets
        ]
    else:
        pairs = [(refs.pop(0), refs.pop(0)) for _ in range(GROUPS)]
        blocks = [
            jnp.concatenate(
                [pair[r % 2][r // 2, part] for part in range(2) for pair in pairs], axis=0
            ).reshape(2 * dirs * chans, share)
            for r in range(line)
        ]
    vis_ref, coh_ref, ends_ref = refs[:3]
    outs = refs[3:]
    links = vis_ref.shape[3]
    if build:
        ids = lax.broadcasted_iota(jnp.int32, (count, links), 0)
        pick_ref = outs[2 * GROUPS]
        for end in range(2):
            pick_ref[end] = (ids == ends_ref[end : end + 1, :]).astype(jnp.float32).astype(jnp.bfloat16)
    else:
        pick_ref = ends_ref
    dot = functools.partial(lax.dot_general, preferred_element_type=jnp.float32)
    upper, lower = split(jnp.concatenate(blocks, axis=1))
    first, second = [
        dot(upper, pick_ref[end], ROWS_BY_COLS) + dot(lower, pick_ref[end], ROWS_BY_COLS) for end in range(2)
    ]

    def row(values, part, k):
        begin = (part * dirs + k) * chans
        return values[begin : begin + chans]

    rest_real = vis_ref[0, time]
    rest_imag = vis_ref[1, time]
    sides = []
    for k in range(dirs):
        coh_real = coh_ref[0, k, time].astype(jnp.float32)
        coh_imag = coh_ref[1, k, time].astype(jnp.float32)
        first_real, first_imag = row(first, 0, k), row(first, 1, k)
        second_real, second_imag = row(second, 0, k), row(second, 1, k)
        left_real = second_real * coh_real + second_imag * coh_imag
        left_imag = second_imag * coh_real - second_real * coh_imag
        right_real = first_real * coh_real - first_imag * coh_imag
        right_imag = first_real * coh_imag + first_imag * coh_real
        rest_real = rest_real - (first_real * left_real + first_imag * left_imag)
        rest_imag = rest_imag - (first_imag * left_real - first_real * left_imag)
        sides.append((left_real, left_imag, right_real, right_imag))
    terms = [[], []]
    for group in range(GROUPS):
        chosen = sides[group * half : (group + 1) * half]
        terms[0] += [rest_real * a - rest_imag * b for a, b, _, _ in chosen]
        terms[0] += [rest_real * b + rest_imag * a for a, b, _, _ in chosen]
        terms[0] += [a * a + b * b for a, b, _, _ in chosen]
        terms[1] += [rest_real * c + rest_imag * d for _, _, c, d in chosen]
        terms[1] += [rest_real * d - rest_imag * c for _, _, c, d in chosen]
        terms[1] += [c * c + d * d for _, _, c, d in chosen]
    total = None
    for end in range(2):
        for piece in split(jnp.concatenate(terms[end], axis=0)):
            value = dot(piece, pick_ref[end], ROWS_BY_ROWS)
            total = value if total is None else total + value
    rows = 3 * half * chans
    for group in range(GROUPS):
        for r in range(line):
            piece = total[group * rows : (group + 1) * rows, r * share : (r + 1) * share]
            outs[2 * group + r % 2][r // 2] = piece.reshape(3, half, chans, share)


def normals(gains, start, place, visibilities, coherencies, ends, time, line):
    _, dirs, _, chans, links = coherencies.shape
    build = ends.ndim == 2
    count = gains[0].shape[-1] if start else gains[0].shape[-1] * line
    share = count // line
    half = dirs // GROUPS
    whole = pl.BlockSpec(memory_space=VMEM)
    shape = jax.ShapeDtypeStruct((line // 2, 3, half, chans, share), jnp.float32)
    shapes = [shape] * (2 * GROUPS)
    if build:
        shapes.append(jax.ShapeDtypeStruct((2, count, links), jnp.bfloat16))
    operands = list(gains) + [visibilities, coherencies, ends]
    specs = [whole] * len(operands)
    if start:
        operands.insert(0, place)
        specs.insert(0, pl.BlockSpec(memory_space=SMEM))
    flops = 2 * 2 * 2 * links * count * 5 * dirs * chans
    return pl.pallas_call(
        functools.partial(normals_kernel, dirs, chans, line, share, time, start, build),
        in_specs=specs,
        out_specs=[whole] * len(shapes),
        out_shape=shapes,
        compiler_params=pltpu.CompilerParams(vmem_limit_bytes=40 * 2**20),
        cost_estimate=pl.CostEstimate(flops=flops, bytes_accessed=4 * 2**20, transcendentals=0),
    )(*operands)


def assemble_kernel(times, line, share, place_ref, *refs):
    out_ref = refs[-1]
    half = out_ref.shape[1] // GROUPS
    for time in range(times):
        for group in range(GROUPS):
            for r in range(line):
                source = refs[2 * (time * GROUPS + group) + r % 2]
                offset = pl.multiple_of((place_ref[0] ^ r) * share, LANES)
                out_ref[:, group * half : (group + 1) * half, time, :, pl.ds(offset, share)] = source[r // 2]


def assemble(gains, place, shape, line):
    share = shape[-1] // line
    if share % LANES:
        rows = []
        for row in gains:
            groups = []
            for near, far in row:
                blocks = jnp.stack([near, far], axis=1).reshape((line,) + near.shape[1:])
                parts = [lax.dynamic_index_in_dim(blocks, place[0] ^ r, 0, False) for r in range(line)]
                groups.append(jnp.concatenate(parts, axis=-1))
            rows.append(jnp.concatenate(groups, axis=1))
        return jnp.stack(rows, axis=2)
    flat = [block for row in gains for pair in row for block in pair]
    whole = pl.BlockSpec(memory_space=VMEM)
    return pl.pallas_call(
        functools.partial(assemble_kernel, shape[2], line, share),
        in_specs=[pl.BlockSpec(memory_space=SMEM)] + [whole] * len(flat),
        out_specs=whole,
        out_shape=jax.ShapeDtypeStruct(shape, jnp.float32),
        compiler_params=pltpu.CompilerParams(vmem_limit_bytes=16 * 2**20),
    )(place, *flat)


def shards(visibilities, coherencies, start_gains, penalty, stations):
    _, dirs, times, chans, count = start_gains.shape
    half = dirs // GROUPS
    line = lax.axis_size("bl")
    index = lax.axis_index("bl")
    place = index.astype(jnp.int32).reshape(1)
    groups = lax.axis_size("chan")
    share = count // line
    basis_table, solved_table = bernstein_tables(chans * groups)
    first_row = lax.axis_index("chan") * chans
    basis = lax.dynamic_slice_in_dim(jnp.asarray(basis_table), first_row, chans, 0)
    solved = lax.dynamic_slice_in_dim(jnp.asarray(solved_table), first_row, chans, 0)
    relative = ((stations // share) ^ index) * share + stations % share

    def swap(values, axis, size, bit):
        return lax.ppermute(values, axis, [(i, i ^ bit) for i in range(size)])

    def sum_own(keep, send):
        bit = 1
        while True:
            got = swap(send, "bl", line, bit)
            if keep.shape[0] == 1:
                return keep[0] + got[0]
            both = keep + got
            keep, send = both[0::2], both[1::2]
            bit *= 2

    def spread(own):
        blocks = own[None]
        bit = line // 2
        while bit > 1:
            got = swap(blocks, "bl", line, bit)
            blocks = jnp.stack([blocks, got], axis=1).reshape((2 * blocks.shape[0],) + blocks.shape[1:])
            bit //= 2
        return blocks, swap(blocks, "bl", line, 1)

    def project(values):
        return jnp.stack([jnp.sum(basis[:, j, None] * values, axis=2) for j in range(POLY)])

    def chan_sum(values):
        bit = 1
        while bit < groups:
            values = values + swap(values, "chan", groups, bit)
            bit *= 2
        return values

    def smooth(sums):
        return sum(solved[:, j, None] * sums[j][:, :, None, :] for j in range(POLY))

    def update(total, gains, target, weight):
        divisor = total[2] + weight
        return jnp.stack(
            [(total[part] + gains[part] * total[2] + weight * target[part]) / divisor for part in range(2)]
        )

    weights = [penalty[group * half : (group + 1) * half, None, None] for group in range(GROUPS)]
    ordered = start_gains
    if share % LANES:
        parts = [lax.dynamic_slice_in_dim(start_gains, (index ^ r) * share, share, 4) for r in range(line)]
        ordered = jnp.concatenate(parts, axis=4)
    own_start = lax.dynamic_slice_in_dim(start_gains, index * share, share, 4)
    own = [
        [own_start[:, group * half : (group + 1) * half, time] for group in range(GROUPS)] for time in range(times)
    ]
    targets = own
    duals = None
    gains = None
    picks = None
    for iteration in range(ITERS):
        sums = []
        for time in range(times):
            if iteration == 0:
                out = normals(
                    [ordered], True, place, visibilities, coherencies, relative if time == 0 else picks, time, line
                )
                picks = out[2 * GROUPS] if time == 0 else picks
            else:
                flat = [block for pair in gains[time] for block in pair]
                out = normals(flat, False, place, visibilities, coherencies, picks, time, line)
            sums.append(out)
        fresh = []
        gains = []
        for time in range(times):
            fresh.append([])
            gains.append([])
            for group in range(GROUPS):
                total = sum_own(sums[time][2 * group], sums[time][2 * group + 1])
                value = update(total, own[time][group], targets[time][group], weights[group])
                fresh[time].append(value)
                gains[time].append(spread(value))
        own = fresh
        values = [jnp.concatenate(row, axis=1) for row in own]
        if duals is not None:
            values = [value + dual for value, dual in zip(values, duals)]
        sums = chan_sum(jnp.stack([project(value) for value in values]))
        consensus = [smooth(sums[time]) for time in range(times)]
        duals = [value - flat for value, flat in zip(values, consensus)]
        targets = [
            [(flat - dual)[:, group * half : (group + 1) * half] for group in range(GROUPS)]
            for flat, dual in zip(consensus, duals)
        ]
    return (
        assemble(gains, place, start_gains.shape, line),
        jnp.stack(consensus, axis=2),
        jnp.stack(duals, axis=2),
    )


def solution(mesh):
    in_specs = (
        P(None, None, "chan", "bl"),
        P(None, None, None, "chan", "bl"),
        P(None, None, None, "chan", None),
        P(),
        P(None, "bl"),
    )
    out_specs = (
        P(None, None, None, "chan", None),
        P(None, None, None, "chan", "bl"),
        P(None, None, None, "chan", "bl"),
    )
    return jax.shard_map(shards, mesh=mesh, in_specs=in_specs, out_specs=out_specs, check_vma=False)
```

time: 140 us -> 119 us (0.85)
  waiting for transfers between devices: 56.9 us -> 33.8 us
  starting transfers between devices: 43.1 us -> 45.7 us
  Pallas kernels: 23 us -> 20.9 us
  local copies, waits for them, and re-layouts: 5.44 us -> 7.24 us
    ppermute x36 -> x38, waiting for transfers between devices: 56.9 us -> 33.8 us  [swap(): return lax.ppermute(values, axis, [(i, i ^ bit) for i in range(size)])]
    ppermute x36 -> x38, starting transfers between devices: 43.1 us -> 45.7 us  [swap(): return lax.ppermute(values, axis, [(i, i ^ bit) for i in range(size)])]
    pallas_call x4 -> x5, Pallas kernels: 23 us -> 20.9 us  [the longest x4 19.9 us: normals(): pl.pallas_call(functools.partial(normals_kernel, dirs, chans, line, share...]
    squeeze x1 -> x0, local copies, waits for them, and re-layouts: 1.41 us -> none  [shards(): start_gains[:, group * half:(group + 1) * half, time]]
    unnamed x20 -> x28, local copies, waits for them, and re-layouts: 3.84 us -> 5.1 us
    add x29 -> x23, other arithmetic: 5.8 us -> 5.77 us  [the longest x8 3.93 us: sum_own(): both = keep + got]
  transfers between devices with their start and end apart: 36 -> 38, of which waited for: 17 -> 21; matrix products, arithmetic and copies ran while one was open for 6% -> 9% of each run, Pallas kernels for 12% -> 8%
where the time goes in v2:
time: 119 us
  starting transfers between devices  45.7 us (38%)
  waiting for transfers between devices  33.8 us (28%)
  Pallas kernels  20.9 us (18%)
  other arithmetic  9.69 us (8%)
  local copies, waits for them, and re-layouts  7.24 us (6%)
  between operations  1.23 us (1%)
    ppermute x38, starting transfers between devices, swap(): return lax.ppermute(values, axis, [(i, i ^ bit) for i in range(size)])  45.7 us
    ppermute x38, waiting for transfers between devices, swap(): return lax.ppermute(values, axis, [(i, i ^ bit) for i in range(size)])  33.8 us
    pallas_call x4, Pallas kernels, normals(): pl.pallas_call(functools.partial(normals_kernel, dirs, chans, line, share...  19.9 us
    unnamed x28, local copies, waits for them, and re-layouts  5.1 us
    add x8, other arithmetic, sum_own(): both = keep + got  3.93 us
  transfers between devices with their start and end apart: 38, of which 21 were waited for; matrix products, arithmetic and copies ran while one was open for 9% of the time, Pallas kernels for 8%

profile of v2, /device:TPU:0, one launch (start us, length us, event | category | flops | bytes accessed | tf_op | source)
XLA Modules:
  0.0 118.5 jit_solution(2224669970715809394)
XLA Ops:
  1.4 1.1 copy-done
  2.6 1.4 %copy-done.1 = bf16[2,4,2,24,2048]{4,3,2,1,0:T(8,128)(2,1)S(1)} copy-done((bf16[2,4,2,24,2048]{4,3,2,1,0:T(8,128)(2,1)S(1)}, bf16[2,4,2,24,2048]{4,3,2,1,0:T(8,128)(2,1)}, u32[]{:S(2)}) %copy-start.1) | copy-done | bytes 1572888
  4.0 1.1 copy-done.3
  5.1 5.6 %shard_map.94 = (f32[2,3,2,24,128]{4,3,2,1,0:T(8,128)S(1)}, f32[2,3,2,24,128]{4,3,2,1,0:T(8,128)S(1)}, f32[2,3,2,24,128]{4,3,2,1,0:T(8,128)S(1)}, f32[2,3,2,24,1...) custom-call(s32[1]{0:T(128)} %bitcast.refs_0_.place_ref, f32[2,4,2,24,512]{4,3,2,1,0:T(8,128)S(1)} %copy-done, ...), custom_call_target="tpu_custom_call" | custom-call | flops 4026531840 | bytes 4194304 | tf_op jit(solution)/shard_map/pallas_call | solution.py:131
  10.8 4.7 %shard_map.96 = (f32[2,3,2,24,128]{4,3,2,1,0:T(8,128)S(1)}, f32[2,3,2,24,128]{4,3,2,1,0:T(8,128)S(1)}, f32[2,3,2,24,128]{4,3,2,1,0:T(8,128)S(1)}, f32[2,3,2,24,128]{4,3,2,1,0:T(8,128)S(1)}) custom-call(s32[1]{0:T(128)} %bitcast.refs_0_.place_ref, f32[2,4,2,24,512]{4,3,2,1,0:T(8,128)S(1)} %copy-done, f32[2,2,24,2048]{3,2,1,0:T(8,128)S(1)} %copy-done.3, ...), custom_call_target="tpu_custom_call" | custom-call | flops 4026531840 | bytes 4194304 | tf_op jit(solution)/shard_map/pallas_call | solution.py:131
  15.5 3.1 %collective-permute-start.12 = (f32[2,3,2,24,128]{4,3,2,1,0:T(8,128)S(1)}, f32[2,3,2,24,128]{4,3,2,1,0:T(8,128)}, u32[]{:S(2)}, u32[]{:S(2)}) collective-permute-start(f32[2,3,2,24,128]{4,3,2,1,0:T(8,128)S(1)} %get-tuple-element.30), channel_id=1, source_target_pairs={{0,1},{1,0},{2,3},{3,2},{4,5},{5,4},{6,7},{7,6},{8,9},{9,8},{10,11... | collective-permute-start | bytes 442376 | tf_op jit(solution)/shard_map/ppermute | solution.py:190
  18.7 1.9 %collective-permute-start.10 = (f32[2,3,2,24,128]{4,3,2,1,0:T(8,128)S(1)}, f32[2,3,2,24,128]{4,3,2,1,0:T(8,128)}, u32[]{:S(2)}, u32[]{:S(2)}) collective-permute-start(f32[2,3,2,24,128]{4,3,2,1,0:T(8,128)S(1)} %get-tuple-element.28), channel_id=1, source_target_pairs={{0,1},{1,0},{2,3},{3,2},{4,5},{5,4},{6,7},{7,6},{8,9},{9,8},{10,11... | collective-permute-start | bytes 442376 | tf_op jit(solution)/shard_map/ppermute | solution.py:190
  21.4 2.0 %collective-permute-done.12 = f32[2,3,2,24,128]{4,3,2,1,0:T(8,128)} collective-permute-done((f32[2,3,2,24,128]{4,3,2,1,0:T(8,128)S(1)}, f32[2,3,2,24,128]{4,3,2,1,0:T(8,128)}, u32[]{:S(2)}, u32[]{:S(2)}) %collective-permute-start.12) | collective-permute-done | bytes 147488 | tf_op jit(solution)/shard_map/ppermute | solution.py:190
  23.4 0.9 add.515
  25.0 3.1 %collective-permute-start.13 = (f32[1,3,2,24,128]{4,3,2,1,0:T(8,128)}, f32[1,3,2,24,128]{4,3,2,1,0:T(8,128)}, u32[]{:S(2)}, u32[]{:S(2)}) collective-permute-start(f32[1,3,2,24,128]{4,3,2,1,0:T(8,128)} %slice.576), channel_id=1, source_target_pairs={{0,2},{1,3},{2,0},{3,1},{4,6},{5,7},{6,4},{7,5},{8,10},{9,11},{10,... | collective-permute-start | bytes 221192 | tf_op jit(solution)/shard_map/ppermute | solution.py:190
  28.9 1.1 add.497
  30.0 1.0 collective-permute-start.5
  31.0 1.1 collective-permute-done.10
  33.0 2.0 %collective-permute-start.11 = (f32[1,3,2,24,128]{4,3,2,1,0:T(8,128)S(1)}, f32[1,3,2,24,128]{4,3,2,1,0:T(8,128)S(1)}, u32[]{:S(2)}, u32[]{:S(2)}) collective-permute-start(f32[1,3,2,24,128]{4,3,2,1,0:T(8,128)S(1)} %slice.571), channel_id=1, source_target_pairs={{0,2},{1,3},{2,0},{3,1},{4,6},{5,7},{6,4},{7,5},{8,10},{9,11},{10,... | collective-permute-start | bytes 221192 | tf_op jit(solution)/shard_map/ppermute | solution.py:190
  36.2 1.2 %collective-permute-start.1 = (f32[1,3,2,24,128]{4,3,2,1,0:T(8,128)S(1)}, f32[1,3,2,24,128]{4,3,2,1,0:T(8,128)S(1)}, u32[]{:S(2)}, u32[]{:S(2)}) collective-permute-start(f32[1,3,2,24,128]{4,3,2,1,0:T(8,128)S(1)} %slice.557), channel_id=1, source_target_pairs={{0,2},{1,3},{2,0},{3,1},{4,6},{5,7},{6,4},{7,5},{8,10},{9,11},{10,... | collective-permute-start | bytes 221192 | tf_op jit(solution)/shard_map/ppermute | solution.py:190
  38.3 2.5 %collective-permute-done.5 = f32[1,3,2,24,128]{4,3,2,1,0:T(8,128)S(1)} collective-permute-done((f32[1,3,2,24,128]{4,3,2,1,0:T(8,128)S(1)}, f32[1,3,2,24,128]{4,3,2,1,0:T(8,128)S(1)}, u32[]{:S(2)}, u32[]{:S(2)}) %collective-permute-start.5) | collective-permute-done | bytes 73760 | tf_op jit(solution)/shard_map/ppermute | solution.py:190
  44.9 2.8 %collective-permute-start.23 = (f32[1,2,2,24,128]{4,3,2,1,0:T(8,128)S(1)}, f32[1,2,2,24,128]{4,3,2,1,0:T(8,128)S(1)}, u32[]{:S(2)}, u32[]{:S(2)}) collective-permute-start(f32[1,2,2,24,128]{4,3,2,1,0:T(8,128)S(1)} %get-tuple-element.100), channel_id=1, source_target_pairs={{0,2},{1,3},{2,0},{3,1},{4,6},{5,7},{6,4},{7,5},{8,10},{9,11},{10,... | collective-permute-start | bytes 147464 | tf_op jit(solution)/shard_map/ppermute | solution.py:190
  47.9 2.8 %collective-permute-start.2 = (f32[1,2,2,24,128]{4,3,2,1,0:T(8,128)S(1)}, f32[1,2,2,24,128]{4,3,2,1,0:T(8,128)S(1)}, u32[]{:S(2)}, u32[]{:S(2)}) collective-permute-start(f32[1,2,2,24,128]{4,3,2,1,0:T(8,128)S(1)} %get-tuple-element.87), channel_id=1, source_target_pairs={{0,2},{1,3},{2,0},{3,1},{4,6},{5,7},{6,4},{7,5},{8,10},{9,11},{10,... | collective-permute-start | bytes 147464 | tf_op jit(solution)/shard_map/ppermute | solution.py:190
  50.7 1.5 %collective-permute-start.15 = (f32[2,4,2,4,128]{4,3,2,1,0:T(4,128)S(1)}, f32[2,4,2,4,128]{4,3,2,1,0:T(4,128)S(1)}, u32[]{:S(2)}, u32[]{:S(2)}) collective-permute-start(f32[2,4,2,4,128]{4,3,2,1,0:T(4,128)S(1)} %fusion.80), channel_id=1, source_target_pairs={{0,8},{4,12},{8,0},{12,4},{16,24},{20,28},{24,16},{28,20},{1,9},{5... | collective-permute-start | bytes 98312 | tf_op jit(solution)/shard_map/ppermute | solution.py:190
  52.2 1.4 %collective-permute-start.26 = (f32[2,2,2,24,128]{4,3,2,1,0:T(8,128)S(1)}, f32[2,2,2,24,128]{4,3,2,1,0:T(8,128)S(1)}, u32[]{:S(2)}, u32[]{:S(2)}) collective-permute-start(f32[2,2,2,24,128]{4,3,2,1,0:T(8,128)S(1)} %maximum_bitcast_fusion.5.refs_2_), channel_id=1, source_target_pairs={{0,1},{1,0},{2,3},{3,2},{4,5},{5,4},{6,7},{7,6},{8,9},{9,8},{10,11... | collective-permute-start | bytes 294920 | tf_op jit(solution)/shard_map/ppermute | solution.py:190
  53.6 1.5 %collective-permute-done.23 = f32[1,2,2,24,128]{4,3,2,1,0:T(8,128)S(1)} collective-permute-done((f32[1,2,2,24,128]{4,3,2,1,0:T(8,128)S(1)}, f32[1,2,2,24,128]{4,3,2,1,0:T(8,128)S(1)}, u32[]{:S(2)}, u32[]{:S(2)}) %collective-permute-start.23) | collective-permute-done | bytes 49184 | tf_op jit(solution)/shard_map/ppermute | solution.py:190
  55.2 1.4 %collective-permute-done.6 = f32[1,2,2,24,128]{4,3,2,1,0:T(8,128)S(1)} collective-permute-done((f32[1,2,2,24,128]{4,3,2,1,0:T(8,128)S(1)}, f32[1,2,2,24,128]{4,3,2,1,0:T(8,128)S(1)}, u32[]{:S(2)}, u32[]{:S(2)}) %collective-permute-start.6) | collective-permute-done | bytes 49184 | tf_op jit(solution)/shard_map/ppermute | solution.py:190
  57.3 1.5 %collective-permute-start.16 = (f32[2,4,2,4,128]{4,3,2,1,0:T(4,128)S(1)}, f32[2,4,2,4,128]{4,3,2,1,0:T(4,128)S(1)}, u32[]{:S(2)}, u32[]{:S(2)}) collective-permute-start(f32[2,4,2,4,128]{4,3,2,1,0:T(4,128)S(1)} %fusion.83), channel_id=1, source_target_pairs={{0,16},{4,20},{8,24},{12,28},{16,0},{20,4},{24,8},{28,12},{1,17},{... | collective-permute-start | bytes 98312 | tf_op jit(solution)/shard_map/ppermute | solution.py:190
  58.9 1.5 %collective-permute-start.3 = (f32[2,2,2,24,128]{4,3,2,1,0:T(8,128)S(1)}, f32[2,2,2,24,128]{4,3,2,1,0:T(8,128)S(1)}, u32[]{:S(2)}, u32[]{:S(2)}) collective-permute-start(f32[2,2,2,24,128]{4,3,2,1,0:T(8,128)S(1)} %maximum_bitcast_fusion.refs_0_), channel_id=1, source_target_pairs={{0,1},{1,0},{2,3},{3,2},{4,5},{5,4},{6,7},{7,6},{8,9},{9,8},{10,11... | collective-permute-start | bytes 294920 | tf_op jit(solution)/shard_map/ppermute | solution.py:190
  60.4 0.9 collective-permute-done.16
  61.5 2.1 %collective-permute-done.7.refs_3_ = f32[2,2,2,24,128]{4,3,2,1,0:T(8,128)S(1)} collective-permute-done((f32[2,2,2,24,128]{4,3,2,1,0:T(8,128)S(1)}, f32[2,2,2,24,128]{4,3,2,1,0:T(8,128)S(1)}, u32[]{:S(2)}, u32[]{:S(2)}) %collective-permute-start.7) | collective-permute-done | bytes 98336 | tf_op jit(solution)/shard_map/ppermute | solution.py:190
  63.5 1.3 %collective-permute-done.3.refs_1_ = f32[2,2,2,24,128]{4,3,2,1,0:T(8,128)S(1)} collective-permute-done((f32[2,2,2,24,128]{4,3,2,1,0:T(8,128)S(1)}, f32[2,2,2,24,128]{4,3,2,1,0:T(8,128)S(1)}, u32[]{:S(2)}, u32[]{:S(2)}) %collective-permute-start.3) | collective-permute-done | bytes 98336 | tf_op jit(solution)/shard_map/ppermute | solution.py:190
  64.8 4.9 %shard_map.95 = (f32[2,3,2,24,128]{4,3,2,1,0:T(8,128)S(1)}, f32[2,3,2,24,128]{4,3,2,1,0:T(8,128)S(1)}, f32[2,3,2,24,128]{4,3,2,1,0:T(8,128)S(1)}, f32[2,3,2,24,128]{4,3,2,1,0:T(8,128)S(1)}) custom-call(f32[2,2,2,24,128]{4,3,2,1,0:T(8,128)S(1)} %maximum_bitcast_fusion.refs_0_, f32[2,2,2,24,128]{4,3,2,1,0:T(8,128)S(1)} %collective-permute-done.3.refs_1_, ...), custom_call_target="tpu_custom_call" | custom-call | flops 4026531840 | bytes 4194304 | tf_op jit(solution)/shard_map/pallas_call | solution.py:131
  70.0 4.7 %shard_map.97 = (f32[2,3,2,24,128]{4,3,2,1,0:T(8,128)S(1)}, f32[2,3,2,24,128]{4,3,2,1,0:T(8,128)S(1)}, f32[2,3,2,24,128]{4,3,2,1,0:T(8,128)S(1)}, f32[2,3,2,24,128]{4,3,2,1,0:T(8,128)S(1)}) custom-call(f32[2,2,2,24,128]{4,3,2,1,0:T(8,128)S(1)} %maximum_bitcast_fusion.4.refs_0_, f32[2,2,2,24,128]{4,3,2,1,0:T(8,128)S(1)} %collective-permute-done.24.refs_1_, ...), custom_call_target="tpu_custom_call" | custom-call | flops 4026531840 | bytes 4194304 | tf_op jit(solution)/shard_map/pallas_call | solution.py:131
  74.7 1.8 %collective-permute-start.27 = (f32[2,3,2,24,128]{4,3,2,1,0:T(8,128)S(1)}, f32[2,3,2,24,128]{4,3,2,1,0:T(8,128)S(1)}, u32[]{:S(2)}, u32[]{:S(2)}) collective-permute-start(f32[2,3,2,24,128]{4,3,2,1,0:T(8,128)S(1)} %get-tuple-element.34), channel_id=1, source_target_pairs={{0,1},{1,0},{2,3},{3,2},{4,5},{5,4},{6,7},{7,6},{8,9},{9,8},{10,11... | collective-permute-start | bytes 442376 | tf_op jit(solution)/shard_map/ppermute | solution.py:190
  76.8 1.8 %collective-permute-start.19 = (f32[2,3,2,24,128]{4,3,2,1,0:T(8,128)S(1)}, f32[2,3,2,24,128]{4,3,2,1,0:T(8,128)S(1)}, u32[]{:S(2)}, u32[]{:S(2)}) collective-permute-start(f32[2,3,2,24,128]{4,3,2,1,0:T(8,128)S(1)} %get-tuple-element.32), channel_id=1, source_target_pairs={{0,1},{1,0},{2,3},{3,2},{4,5},{5,4},{6,7},{7,6},{8,9},{9,8},{10,11... | collective-permute-start | bytes 442376 | tf_op jit(solution)/shard_map/ppermute | solution.py:190
  78.6 1.5 %collective-permute-start.9 = (f32[1,3,2,24,128]{4,3,2,1,0:T(8,128)S(1)}, f32[1,3,2,24,128]{4,3,2,1,0:T(8,128)S(1)}, u32[]{:S(2)}, u32[]{:S(2)}) collective-permute-start(f32[1,3,2,24,128]{4,3,2,1,0:T(8,128)S(1)} %slice.567), channel_id=1, source_target_pairs={{0,2},{1,3},{2,0},{3,1},{4,6},{5,7},{6,4},{7,5},{8,10},{9,11},{10,... | collective-permute-start | bytes 221192 | tf_op jit(solution)/shard_map/ppermute | solution.py:190
  80.2 2.2 %collective-permute-done.27 = f32[2,3,2,24,128]{4,3,2,1,0:T(8,128)S(1)} collective-permute-done((f32[2,3,2,24,128]{4,3,2,1,0:T(8,128)S(1)}, f32[2,3,2,24,128]{4,3,2,1,0:T(8,128)S(1)}, u32[]{:S(2)}, u32[]{:S(2)}) %collective-permute-start.27) | collective-permute-done | bytes 147488 | tf_op jit(solution)/shard_map/ppermute | solution.py:190
  82.4 2.4 %collective-permute-start.28 = (f32[1,3,2,24,128]{4,3,2,1,0:T(8,128)S(1)}, f32[1,3,2,24,128]{4,3,2,1,0:T(8,128)S(1)}, u32[]{:S(2)}, u32[]{:S(2)}) collective-permute-start(f32[1,3,2,24,128]{4,3,2,1,0:T(8,128)S(1)} %slice.595), channel_id=1, source_target_pairs={{0,2},{1,3},{2,0},{3,1},{4,6},{5,7},{6,4},{7,5},{8,10},{9,11},{10,... | collective-permute-start | bytes 221192 | tf_op jit(solution)/shard_map/ppermute | solution.py:190
  84.7 3.6 %collective-permute-done.31 = f32[2,3,2,24,128]{4,3,2,1,0:T(8,128)S(1)} collective-permute-done((f32[2,3,2,24,128]{4,3,2,1,0:T(8,128)S(1)}, f32[2,3,2,24,128]{4,3,2,1,0:T(8,128)S(1)}, u32[]{:S(2)}, u32[]{:S(2)}) %collective-permute-start.31) | collective-permute-done | bytes 147488 | tf_op jit(solution)/shard_map/ppermute | solution.py:190
  88.4 1.5 %collective-permute-done.19 = f32[2,3,2,24,128]{4,3,2,1,0:T(8,128)S(1)} collective-permute-done((f32[2,3,2,24,128]{4,3,2,1,0:T(8,128)S(1)}, f32[2,3,2,24,128]{4,3,2,1,0:T(8,128)S(1)}, u32[]{:S(2)}, u32[]{:S(2)}) %collective-permute-start.19) | collective-permute-done | bytes 147488 | tf_op jit(solution)/shard_map/ppermute | solution.py:190
  89.9 1.5 %collective-permute-start.20 = (f32[1,3,2,24,128]{4,3,2,1,0:T(8,128)S(1)}, f32[1,3,2,24,128]{4,3,2,1,0:T(8,128)S(1)}, u32[]{:S(2)}, u32[]{:S(2)}) collective-permute-start(f32[1,3,2,24,128]{4,3,2,1,0:T(8,128)S(1)} %slice.588), channel_id=1, source_target_pairs={{0,2},{1,3},{2,0},{3,1},{4,6},{5,7},{6,4},{7,5},{8,10},{9,11},{10,... | collective-permute-start | bytes 221192 | tf_op jit(solution)/shard_map/ppermute | solution.py:190
  91.5 6.0 %collective-permute-done.20 = f32[1,3,2,24,128]{4,3,2,1,0:T(8,128)S(1)} collective-permute-done((f32[1,3,2,24,128]{4,3,2,1,0:T(8,128)S(1)}, f32[1,3,2,24,128]{4,3,2,1,0:T(8,128)S(1)}, u32[]{:S(2)}, u32[]{:S(2)}) %collective-permute-start.20) | collective-permute-done | bytes 73760 | tf_op jit(solution)/shard_map/ppermute | solution.py:190
  98.3 2.9 %collective-permute-start.29 = (f32[1,2,2,24,128]{4,3,2,1,0:T(8,128)S(1)}, f32[1,2,2,24,128]{4,3,2,1,0:T(8,128)S(1)}, u32[]{:S(2)}, u32[]{:S(2)}) collective-permute-start(f32[1,2,2,24,128]{4,3,2,1,0:T(8,128)S(1)} %get-tuple-element.105), channel_id=1, source_target_pairs={{0,2},{1,3},{2,0},{3,1},{4,6},{5,7},{6,4},{7,5},{8,10},{9,11},{10,... | collective-permute-start | bytes 147464 | tf_op jit(solution)/shard_map/ppermute | solution.py:190
  101.3 2.8 %collective-permute-start.17 = (f32[1,2,2,24,128]{4,3,2,1,0:T(8,128)S(1)}, f32[1,2,2,24,128]{4,3,2,1,0:T(8,128)S(1)}, u32[]{:S(2)}, u32[]{:S(2)}) collective-permute-start(f32[1,2,2,24,128]{4,3,2,1,0:T(8,128)S(1)} %get-tuple-element.93), channel_id=1, source_target_pairs={{0,2},{1,3},{2,0},{3,1},{4,6},{5,7},{6,4},{7,5},{8,10},{9,11},{10,... | collective-permute-start | bytes 147464 | tf_op jit(solution)/shard_map/ppermute | solution.py:190
  104.7 1.6 %collective-permute-done.33 = f32[1,2,2,24,128]{4,3,2,1,0:T(8,128)S(1)} collective-permute-done((f32[1,2,2,24,128]{4,3,2,1,0:T(8,128)S(1)}, f32[1,2,2,24,128]{4,3,2,1,0:T(8,128)S(1)}, u32[]{:S(2)}, u32[]{:S(2)}) %collective-permute-start.33) | collective-permute-done | bytes 49184 | tf_op jit(solution)/shard_map/ppermute | solution.py:190
  106.4 1.5 %collective-permute-done.29 = f32[1,2,2,24,128]{4,3,2,1,0:T(8,128)S(1)} collective-permute-done((f32[1,2,2,24,128]{4,3,2,1,0:T(8,128)S(1)}, f32[1,2,2,24,128]{4,3,2,1,0:T(8,128)S(1)}, u32[]{:S(2)}, u32[]{:S(2)}) %collective-permute-start.29) | collective-permute-done | bytes 49184 | tf_op jit(solution)/shard_map/ppermute | solution.py:190
  109.0 1.0 collective-permute-start.22
  110.1 1.6 %collective-permute-start.37 = (f32[2,4,2,4,128]{4,3,2,1,0:T(4,128)S(1)}, f32[2,4,2,4,128]{4,3,2,1,0:T(4,128)S(1)}, u32[]{:S(2)}, u32[]{:S(2)}) collective-permute-start(f32[2,4,2,4,128]{4,3,2,1,0:T(4,128)S(1)} %fusion.82), channel_id=1, source_target_pairs={{0,16},{4,20},{8,24},{12,28},{16,0},{20,4},{24,8},{28,12},{1,17},{... | collective-permute-start | bytes 98312 | tf_op jit(solution)/shard_map/ppermute | solution.py:190
  111.8 1.1 collective-permute-start.18
  112.8 1.3 %collective-permute-done.37 = f32[2,4,2,4,128]{4,3,2,1,0:T(4,128)S(1)} collective-permute-done((f32[2,4,2,4,128]{4,3,2,1,0:T(4,128)S(1)}, f32[2,4,2,4,128]{4,3,2,1,0:T(4,128)S(1)}, u32[]{:S(2)}, u32[]{:S(2)}) %collective-permute-start.37) | collective-permute-done | bytes 32800 | tf_op jit(solution)/shard_map/ppermute | solution.py:190
  116.4 1.1 collective-permute-done.18.refs_1_
  117.6 1.0 shard_map.98
  (133 shorter events, 16.8 us)
Async XLA Ops:
  10.7 4.8 %copy-start.5 = (bf16[2,512,2048]{2,1,0:T(8,128)(2,1)}, bf16[2,512,2048]{2,1,0:T(8,128)(2,1)S(1)}, u32[]{:S(2)}) copy-start(bf16[2,512,2048]{2,1,0:T(8,128)(2,1)S(1)} %get-tuple-element.24.refs_6_.refs_4_) | copy-start | bytes 12582916
  10.8 10.0 %copy-start.11 = (f32[192,4]{0,1:T(4,128)S(1)}, f32[192,4]{0,1:T(4,128)}, u32[]{:S(2)}) copy-start(f32[192,4]{0,1:T(4,128)} %constant.51.clone) | copy-start | bytes 9220
  10.8 10.0 %copy-start.12 = (f32[192,4]{0,1:T(4,128)S(1)}, f32[192,4]{0,1:T(4,128)}, u32[]{:S(2)}) copy-start(f32[192,4]{0,1:T(4,128)} %constant.52.clone) | copy-start | bytes 9220
  15.5 49.3 %copy-start.2 = (bf16[2,4,2,24,2048]{4,3,2,1,0:T(8,128)(2,1)S(1)}, bf16[2,4,2,24,2048]{4,3,2,1,0:T(8,128)(2,1)}, u32[]{:S(2)}) copy-start(bf16[2,4,2,24,2048]{4,3,2,1,0:T(8,128)(2,1)} %refs_5_.3) | copy-start | bytes 4718596
  15.5 49.3 %copy-start.4 = (f32[2,2,24,2048]{3,2,1,0:T(8,128)S(1)}, f32[2,2,24,2048]{3,2,1,0:T(8,128)}, u32[]{:S(2)}) copy-start(f32[2,2,24,2048]{3,2,1,0:T(8,128)} %refs_4_.3) | copy-start | bytes 2359300
  15.5 7.8 %collective-permute-start.12 = (f32[2,3,2,24,128]{4,3,2,1,0:T(8,128)S(1)}, f32[2,3,2,24,128]{4,3,2,1,0:T(8,128)}, u32[]{:S(2)}, u32[]{:S(2)}) collective-permute-start(f32[2,3,2,24,128]{4,3,2,1,0:T(8,128)S(1)} %get-tuple-element.30), channel_id=1, source_target_pairs={{0,1},{1,0},{2,3},{3,2},{4,5},{5,4},{6,7},{7,6},{8,9},{9,8},{10,11... | collective-permute-start | bytes 442376 | tf_op jit(solution)/shard_map/ppermute | solution.py:190
  18.6 10.3 %collective-permute-start.4 = (f32[2,3,2,24,128]{4,3,2,1,0:T(8,128)S(1)}, f32[2,3,2,24,128]{4,3,2,1,0:T(8,128)}, u32[]{:S(2)}, u32[]{:S(2)}) collective-permute-start(f32[2,3,2,24,128]{4,3,2,1,0:T(8,128)S(1)} %get-tuple-element.23), channel_id=1, source_target_pairs={{0,1},{1,0},{2,3},{3,2},{4,5},{5,4},{6,7},{7,6},{8,9},{9,8},{10,11... | collective-permute-start | bytes 442376 | tf_op jit(solution)/shard_map/ppermute | solution.py:190
  18.7 13.4 %collective-permute-start.10 = (f32[2,3,2,24,128]{4,3,2,1,0:T(8,128)S(1)}, f32[2,3,2,24,128]{4,3,2,1,0:T(8,128)}, u32[]{:S(2)}, u32[]{:S(2)}) collective-permute-start(f32[2,3,2,24,128]{4,3,2,1,0:T(8,128)S(1)} %get-tuple-element.28), channel_id=1, source_target_pairs={{0,1},{1,0},{2,3},{3,2},{4,5},{5,4},{6,7},{7,6},{8,9},{9,8},{10,11... | collective-permute-start | bytes 442376 | tf_op jit(solution)/shard_map/ppermute | solution.py:190
  20.6 14.6 %collective-permute-start = (f32[2,3,2,24,128]{4,3,2,1,0:T(8,128)S(1)}, f32[2,3,2,24,128]{4,3,2,1,0:T(8,128)}, u32[]{:S(2)}, u32[]{:S(2)}) collective-permute-start(f32[2,3,2,24,128]{4,3,2,1,0:T(8,128)S(1)} %get-tuple-element.21), channel_id=1, source_target_pairs={{0,1},{1,0},{2,3},{3,2},{4,5},{5,4},{6,7},{7,6},{8,9},{9,8},{10,11... | collective-permute-start | bytes 442376 | tf_op jit(solution)/shard_map/ppermute | solution.py:190
  24.3 20.1 %copy-start.7 = (f32[24]{0:T(128)S(1)}, f32[24]{0:T(128)}, u32[]{:S(2)}) copy-start(f32[24]{0:T(128)} %get-tuple-element.134) | copy-start | bytes 292
  24.3 20.1 %copy-start.8 = (f32[24]{0:T(128)S(1)}, f32[24]{0:T(128)}, u32[]{:S(2)}) copy-start(f32[24]{0:T(128)} %get-tuple-element.136) | copy-start | bytes 292
  24.3 20.1 %copy-start.9 = (f32[24]{0:T(128)S(1)}, f32[24]{0:T(128)}, u32[]{:S(2)}) copy-start(f32[24]{0:T(128)} %get-tuple-element.137) | copy-start | bytes 292
  24.4 20.1 %copy-start.10 = (f32[24]{0:T(128)S(1)}, f32[24]{0:T(128)}, u32[]{:S(2)}) copy-start(f32[24]{0:T(128)} %get-tuple-element.135) | copy-start | bytes 292
  25.0 12.4 %collective-permute-start.13 = (f32[1,3,2,24,128]{4,3,2,1,0:T(8,128)}, f32[1,3,2,24,128]{4,3,2,1,0:T(8,128)}, u32[]{:S(2)}, u32[]{:S(2)}) collective-permute-start(f32[1,3,2,24,128]{4,3,2,1,0:T(8,128)} %slice.576), channel_id=1, source_target_pairs={{0,2},{1,3},{2,0},{3,1},{4,6},{5,7},{6,4},{7,5},{8,10},{9,11},{10,... | collective-permute-start | bytes 221192 | tf_op jit(solution)/shard_map/ppermute | solution.py:190
  28.9 35.9 %copy-start.6 = (bf16[2,512,2048]{2,1,0:T(8,128)(2,1)S(1)}, bf16[2,512,2048]{2,1,0:T(8,128)(2,1)}, u32[]{:S(2)}) copy-start(bf16[2,512,2048]{2,1,0:T(8,128)(2,1)} %copy-done.5) | copy-start | bytes 12582916
  30.0 10.9 %collective-permute-start.5 = (f32[1,3,2,24,128]{4,3,2,1,0:T(8,128)S(1)}, f32[1,3,2,24,128]{4,3,2,1,0:T(8,128)S(1)}, u32[]{:S(2)}, u32[]{:S(2)}) collective-permute-start(f32[1,3,2,24,128]{4,3,2,1,0:T(8,128)S(1)} %slice.562), channel_id=1, source_target_pairs={{0,2},{1,3},{2,0},{3,1},{4,6},{5,7},{6,4},{7,5},{8,10},{9,11},{10,... | collective-permute-start | bytes 221192 | tf_op jit(solution)/shard_map/ppermute | solution.py:190
  33.0 8.9 %collective-permute-start.11 = (f32[1,3,2,24,128]{4,3,2,1,0:T(8,128)S(1)}, f32[1,3,2,24,128]{4,3,2,1,0:T(8,128)S(1)}, u32[]{:S(2)}, u32[]{:S(2)}) collective-permute-start(f32[1,3,2,24,128]{4,3,2,1,0:T(8,128)S(1)} %slice.571), channel_id=1, source_target_pairs={{0,2},{1,3},{2,0},{3,1},{4,6},{5,7},{6,4},{7,5},{8,10},{9,11},{10,... | collective-permute-start | bytes 221192 | tf_op jit(solution)/shard_map/ppermute | solution.py:190
  36.2 6.5 %collective-permute-start.1 = (f32[1,3,2,24,128]{4,3,2,1,0:T(8,128)S(1)}, f32[1,3,2,24,128]{4,3,2,1,0:T(8,128)S(1)}, u32[]{:S(2)}, u32[]{:S(2)}) collective-permute-start(f32[1,3,2,24,128]{4,3,2,1,0:T(8,128)S(1)} %slice.557), channel_id=1, source_target_pairs={{0,2},{1,3},{2,0},{3,1},{4,6},{5,7},{6,4},{7,5},{8,10},{9,11},{10,... | collective-permute-start | bytes 221192 | tf_op jit(solution)/shard_map/ppermute | solution.py:190
  44.7 6.0 %collective-permute-start.14 = (f32[2,4,2,4,128]{4,3,2,1,0:T(4,128)S(1)}, f32[2,4,2,4,128]{4,3,2,1,0:T(4,128)S(1)}, u32[]{:S(2)}, u32[]{:S(2)}) collective-permute-start(f32[2,4,2,4,128]{4,3,2,1,0:T(4,128)S(1)} %pad_maximum_fusion.10), channel_id=1, source_target_pairs={{0,4},{4,0},{8,12},{12,8},{16,20},{20,16},{24,28},{28,24},{1,5},{5... | collective-permute-start | bytes 98312 | tf_op jit(solution)/shard_map/ppermute | solution.py:190
  44.8 7.4 %collective-permute-start.25 = (f32[1,2,2,24,128]{4,3,2,1,0:T(8,128)S(1)}, f32[1,2,2,24,128]{4,3,2,1,0:T(8,128)S(1)}, u32[]{:S(2)}, u32[]{:S(2)}) collective-permute-start(f32[1,2,2,24,128]{4,3,2,1,0:T(8,128)S(1)} %get-tuple-element.103), channel_id=1, source_target_pairs={{0,2},{1,3},{2,0},{3,1},{4,6},{5,7},{6,4},{7,5},{8,10},{9,11},{10,... | collective-permute-start | bytes 147464 | tf_op jit(solution)/shard_map/ppermute | solution.py:190
  44.9 10.2 %collective-permute-start.23 = (f32[1,2,2,24,128]{4,3,2,1,0:T(8,128)S(1)}, f32[1,2,2,24,128]{4,3,2,1,0:T(8,128)S(1)}, u32[]{:S(2)}, u32[]{:S(2)}) collective-permute-start(f32[1,2,2,24,128]{4,3,2,1,0:T(8,128)S(1)} %get-tuple-element.100), channel_id=1, source_target_pairs={{0,2},{1,3},{2,0},{3,1},{4,6},{5,7},{6,4},{7,5},{8,10},{9,11},{10,... | collective-permute-start | bytes 147464 | tf_op jit(solution)/shard_map/ppermute | solution.py:190
  47.8 8.9 %collective-permute-start.6 = (f32[1,2,2,24,128]{4,3,2,1,0:T(8,128)S(1)}, f32[1,2,2,24,128]{4,3,2,1,0:T(8,128)S(1)}, u32[]{:S(2)}, u32[]{:S(2)}) collective-permute-start(f32[1,2,2,24,128]{4,3,2,1,0:T(8,128)S(1)} %get-tuple-element.90), channel_id=1, source_target_pairs={{0,2},{1,3},{2,0},{3,1},{4,6},{5,7},{6,4},{7,5},{8,10},{9,11},{10,... | collective-permute-start | bytes 147464 | tf_op jit(solution)/shard_map/ppermute | solution.py:190
  47.9 11.0 %collective-permute-start.2 = (f32[1,2,2,24,128]{4,3,2,1,0:T(8,128)S(1)}, f32[1,2,2,24,128]{4,3,2,1,0:T(8,128)S(1)}, u32[]{:S(2)}, u32[]{:S(2)}) collective-permute-start(f32[1,2,2,24,128]{4,3,2,1,0:T(8,128)S(1)} %get-tuple-element.87), channel_id=1, source_target_pairs={{0,2},{1,3},{2,0},{3,1},{4,6},{5,7},{6,4},{7,5},{8,10},{9,11},{10,... | collective-permute-start | bytes 147464 | tf_op jit(solution)/shard_map/ppermute | solution.py:190
  50.7 6.6 %collective-permute-start.15 = (f32[2,4,2,4,128]{4,3,2,1,0:T(4,128)S(1)}, f32[2,4,2,4,128]{4,3,2,1,0:T(4,128)S(1)}, u32[]{:S(2)}, u32[]{:S(2)}) collective-permute-start(f32[2,4,2,4,128]{4,3,2,1,0:T(4,128)S(1)} %fusion.80), channel_id=1, source_target_pairs={{0,8},{4,12},{8,0},{12,4},{16,24},{20,28},{24,16},{28,20},{1,9},{5... | collective-permute-start | bytes 98312 | tf_op jit(solution)/shard_map/ppermute | solution.py:190
  52.2 17.8 %collective-permute-start.26 = (f32[2,2,2,24,128]{4,3,2,1,0:T(8,128)S(1)}, f32[2,2,2,24,128]{4,3,2,1,0:T(8,128)S(1)}, u32[]{:S(2)}, u32[]{:S(2)}) collective-permute-start(f32[2,2,2,24,128]{4,3,2,1,0:T(8,128)S(1)} %maximum_bitcast_fusion.5.refs_2_), channel_id=1, source_target_pairs={{0,1},{1,0},{2,3},{3,2},{4,5},{5,4},{6,7},{7,6},{8,9},{9,8},{10,11... | collective-permute-start | bytes 294920 | tf_op jit(solution)/shard_map/ppermute | solution.py:190
  55.1 14.8 %collective-permute-start.24 = (f32[2,2,2,24,128]{4,3,2,1,0:T(8,128)S(1)}, f32[2,2,2,24,128]{4,3,2,1,0:T(8,128)S(1)}, u32[]{:S(2)}, u32[]{:S(2)}) collective-permute-start(f32[2,2,2,24,128]{4,3,2,1,0:T(8,128)S(1)} %maximum_bitcast_fusion.4.refs_0_), channel_id=1, source_target_pairs={{0,1},{1,0},{2,3},{3,2},{4,5},{5,4},{6,7},{7,6},{8,9},{9,8},{10,11... | collective-permute-start | bytes 294920 | tf_op jit(solution)/shard_map/ppermute | solution.py:190
  56.7 6.8 %collective-permute-start.7 = (f32[2,2,2,24,128]{4,3,2,1,0:T(8,128)S(1)}, f32[2,2,2,24,128]{4,3,2,1,0:T(8,128)S(1)}, u32[]{:S(2)}, u32[]{:S(2)}) collective-permute-start(f32[2,2,2,24,128]{4,3,2,1,0:T(8,128)S(1)} %maximum_bitcast_fusion.1.refs_2_), channel_id=1, source_target_pairs={{0,1},{1,0},{2,3},{3,2},{4,5},{5,4},{6,7},{7,6},{8,9},{9,8},{10,11... | collective-permute-start | bytes 294920 | tf_op jit(solution)/shard_map/ppermute | solution.py:190
  57.3 4.0 %collective-permute-start.16 = (f32[2,4,2,4,128]{4,3,2,1,0:T(4,128)S(1)}, f32[2,4,2,4,128]{4,3,2,1,0:T(4,128)S(1)}, u32[]{:S(2)}, u32[]{:S(2)}) collective-permute-start(f32[2,4,2,4,128]{4,3,2,1,0:T(4,128)S(1)} %fusion.83), channel_id=1, source_target_pairs={{0,16},{4,20},{8,24},{12,28},{16,0},{20,4},{24,8},{28,12},{1,17},{... | collective-permute-start | bytes 98312 | tf_op jit(solution)/shard_map/ppermute | solution.py:190
  58.9 5.9 %collective-permute-start.3 = (f32[2,2,2,24,128]{4,3,2,1,0:T(8,128)S(1)}, f32[2,2,2,24,128]{4,3,2,1,0:T(8,128)S(1)}, u32[]{:S(2)}, u32[]{:S(2)}) collective-permute-start(f32[2,2,2,24,128]{4,3,2,1,0:T(8,128)S(1)} %maximum_bitcast_fusion.refs_0_), channel_id=1, source_target_pairs={{0,1},{1,0},{2,3},{3,2},{4,5},{5,4},{6,7},{7,6},{8,9},{9,8},{10,11... | collective-permute-start | bytes 294920 | tf_op jit(solution)/shard_map/ppermute | solution.py:190
  69.7 8.9 %collective-permute-start.8 = (f32[2,3,2,24,128]{4,3,2,1,0:T(8,128)S(1)}, f32[2,3,2,24,128]{4,3,2,1,0:T(8,128)S(1)}, u32[]{:S(2)}, u32[]{:S(2)}) collective-permute-start(f32[2,3,2,24,128]{4,3,2,1,0:T(8,128)S(1)} %get-tuple-element.26), channel_id=1, source_target_pairs={{0,1},{1,0},{2,3},{3,2},{4,5},{5,4},{6,7},{7,6},{8,9},{9,8},{10,11... | collective-permute-start | bytes 442376 | tf_op jit(solution)/shard_map/ppermute | solution.py:190
  74.7 7.7 %collective-permute-start.27 = (f32[2,3,2,24,128]{4,3,2,1,0:T(8,128)S(1)}, f32[2,3,2,24,128]{4,3,2,1,0:T(8,128)S(1)}, u32[]{:S(2)}, u32[]{:S(2)}) collective-permute-start(f32[2,3,2,24,128]{4,3,2,1,0:T(8,128)S(1)} %get-tuple-element.34), channel_id=1, source_target_pairs={{0,1},{1,0},{2,3},{3,2},{4,5},{5,4},{6,7},{7,6},{8,9},{9,8},{10,11... | collective-permute-start | bytes 442376 | tf_op jit(solution)/shard_map/ppermute | solution.py:190
  76.5 11.8 %collective-permute-start.31 = (f32[2,3,2,24,128]{4,3,2,1,0:T(8,128)S(1)}, f32[2,3,2,24,128]{4,3,2,1,0:T(8,128)S(1)}, u32[]{:S(2)}, u32[]{:S(2)}) collective-permute-start(f32[2,3,2,24,128]{4,3,2,1,0:T(8,128)S(1)} %get-tuple-element.36), channel_id=1, source_target_pairs={{0,1},{1,0},{2,3},{3,2},{4,5},{5,4},{6,7},{7,6},{8,9},{9,8},{10,11... | collective-permute-start | bytes 442376 | tf_op jit(solution)/shard_map/ppermute | solution.py:190
  76.8 13.1 %collective-permute-start.19 = (f32[2,3,2,24,128]{4,3,2,1,0:T(8,128)S(1)}, f32[2,3,2,24,128]{4,3,2,1,0:T(8,128)S(1)}, u32[]{:S(2)}, u32[]{:S(2)}) collective-permute-start(f32[2,3,2,24,128]{4,3,2,1,0:T(8,128)S(1)} %get-tuple-element.32), channel_id=1, source_target_pairs={{0,1},{1,0},{2,3},{3,2},{4,5},{5,4},{6,7},{7,6},{8,9},{9,8},{10,11... | collective-permute-start | bytes 442376 | tf_op jit(solution)/shard_map/ppermute | solution.py:190
  78.6 12.8 %collective-permute-start.9 = (f32[1,3,2,24,128]{4,3,2,1,0:T(8,128)S(1)}, f32[1,3,2,24,128]{4,3,2,1,0:T(8,128)S(1)}, u32[]{:S(2)}, u32[]{:S(2)}) collective-permute-start(f32[1,3,2,24,128]{4,3,2,1,0:T(8,128)S(1)} %slice.567), channel_id=1, source_target_pairs={{0,2},{1,3},{2,0},{3,1},{4,6},{5,7},{6,4},{7,5},{8,10},{9,11},{10,... | collective-permute-start | bytes 221192 | tf_op jit(solution)/shard_map/ppermute | solution.py:190
  82.4 15.2 %collective-permute-start.28 = (f32[1,3,2,24,128]{4,3,2,1,0:T(8,128)S(1)}, f32[1,3,2,24,128]{4,3,2,1,0:T(8,128)S(1)}, u32[]{:S(2)}, u32[]{:S(2)}) collective-permute-start(f32[1,3,2,24,128]{4,3,2,1,0:T(8,128)S(1)} %slice.595), channel_id=1, source_target_pairs={{0,2},{1,3},{2,0},{3,1},{4,6},{5,7},{6,4},{7,5},{8,10},{9,11},{10,... | collective-permute-start | bytes 221192 | tf_op jit(solution)/shard_map/ppermute | solution.py:190
  88.4 9.3 %collective-permute-start.32 = (f32[1,3,2,24,128]{4,3,2,1,0:T(8,128)S(1)}, f32[1,3,2,24,128]{4,3,2,1,0:T(8,128)S(1)}, u32[]{:S(2)}, u32[]{:S(2)}) collective-permute-start(f32[1,3,2,24,128]{4,3,2,1,0:T(8,128)S(1)} %slice.606), channel_id=1, source_target_pairs={{0,2},{1,3},{2,0},{3,1},{4,6},{5,7},{6,4},{7,5},{8,10},{9,11},{10,... | collective-permute-start | bytes 221192 | tf_op jit(solution)/shard_map/ppermute | solution.py:190
  89.9 7.5 %collective-permute-start.20 = (f32[1,3,2,24,128]{4,3,2,1,0:T(8,128)S(1)}, f32[1,3,2,24,128]{4,3,2,1,0:T(8,128)S(1)}, u32[]{:S(2)}, u32[]{:S(2)}) collective-permute-start(f32[1,3,2,24,128]{4,3,2,1,0:T(8,128)S(1)} %slice.588), channel_id=1, source_target_pairs={{0,2},{1,3},{2,0},{3,1},{4,6},{5,7},{6,4},{7,5},{8,10},{9,11},{10,... | collective-permute-start | bytes 221192 | tf_op jit(solution)/shard_map/ppermute | solution.py:190
  98.1 6.0 %collective-permute-start.35 = (f32[2,4,2,4,128]{4,3,2,1,0:T(4,128)S(1)}, f32[2,4,2,4,128]{4,3,2,1,0:T(4,128)S(1)}, u32[]{:S(2)}, u32[]{:S(2)}) collective-permute-start(f32[2,4,2,4,128]{4,3,2,1,0:T(4,128)S(1)} %pad_maximum_fusion.11), channel_id=1, source_target_pairs={{0,4},{4,0},{8,12},{12,8},{16,20},{20,16},{24,28},{28,24},{1,5},{5... | collective-permute-start | bytes 98312 | tf_op jit(solution)/shard_map/ppermute | solution.py:190
  98.2 8.1 %collective-permute-start.33 = (f32[1,2,2,24,128]{4,3,2,1,0:T(8,128)S(1)}, f32[1,2,2,24,128]{4,3,2,1,0:T(8,128)S(1)}, u32[]{:S(2)}, u32[]{:S(2)}) collective-permute-start(f32[1,2,2,24,128]{4,3,2,1,0:T(8,128)S(1)} %get-tuple-element.108), channel_id=1, source_target_pairs={{0,2},{1,3},{2,0},{3,1},{4,6},{5,7},{6,4},{7,5},{8,10},{9,11},{10,... | collective-permute-start | bytes 147464 | tf_op jit(solution)/shard_map/ppermute | solution.py:190
  98.3 9.6 %collective-permute-start.29 = (f32[1,2,2,24,128]{4,3,2,1,0:T(8,128)S(1)}, f32[1,2,2,24,128]{4,3,2,1,0:T(8,128)S(1)}, u32[]{:S(2)}, u32[]{:S(2)}) collective-permute-start(f32[1,2,2,24,128]{4,3,2,1,0:T(8,128)S(1)} %get-tuple-element.105), channel_id=1, source_target_pairs={{0,2},{1,3},{2,0},{3,1},{4,6},{5,7},{6,4},{7,5},{8,10},{9,11},{10,... | collective-permute-start | bytes 147464 | tf_op jit(solution)/shard_map/ppermute | solution.py:190
  101.2 7.8 %collective-permute-start.21 = (f32[1,2,2,24,128]{4,3,2,1,0:T(8,128)S(1)}, f32[1,2,2,24,128]{4,3,2,1,0:T(8,128)S(1)}, u32[]{:S(2)}, u32[]{:S(2)}) collective-permute-start(f32[1,2,2,24,128]{4,3,2,1,0:T(8,128)S(1)} %get-tuple-element.96), channel_id=1, source_target_pairs={{0,2},{1,3},{2,0},{3,1},{4,6},{5,7},{6,4},{7,5},{8,10},{9,11},{10,... | collective-permute-start | bytes 147464 | tf_op jit(solution)/shard_map/ppermute | solution.py:190
  101.3 10.5 %collective-permute-start.17 = (f32[1,2,2,24,128]{4,3,2,1,0:T(8,128)S(1)}, f32[1,2,2,24,128]{4,3,2,1,0:T(8,128)S(1)}, u32[]{:S(2)}, u32[]{:S(2)}) collective-permute-start(f32[1,2,2,24,128]{4,3,2,1,0:T(8,128)S(1)} %get-tuple-element.93), channel_id=1, source_target_pairs={{0,2},{1,3},{2,0},{3,1},{4,6},{5,7},{6,4},{7,5},{8,10},{9,11},{10,... | collective-permute-start | bytes 147464 | tf_op jit(solution)/shard_map/ppermute | solution.py:190
  104.2 5.9 %collective-permute-start.36 = (f32[2,4,2,4,128]{4,3,2,1,0:T(4,128)S(1)}, f32[2,4,2,4,128]{4,3,2,1,0:T(4,128)S(1)}, u32[]{:S(2)}, u32[]{:S(2)}) collective-permute-start(f32[2,4,2,4,128]{4,3,2,1,0:T(4,128)S(1)} %fusion.79), channel_id=1, source_target_pairs={{0,8},{4,12},{8,0},{12,4},{16,24},{20,28},{24,16},{28,20},{1,9},{5... | collective-permute-start | bytes 98312 | tf_op jit(solution)/shard_map/ppermute | solution.py:190
  106.4 9.5 %collective-permute-start.34 = (f32[2,2,2,24,128]{4,3,2,1,0:T(8,128)S(1)}, f32[2,2,2,24,128]{4,3,2,1,0:T(8,128)S(1)}, u32[]{:S(2)}, u32[]{:S(2)}) collective-permute-start(f32[2,2,2,24,128]{4,3,2,1,0:T(8,128)S(1)} %maximum_bitcast_fusion.7.refs_6_), channel_id=1, source_target_pairs={{0,1},{1,0},{2,3},{3,2},{4,5},{5,4},{6,7},{7,6},{8,9},{9,8},{10,11... | collective-permute-start | bytes 294920 | tf_op jit(solution)/shard_map/ppermute | solution.py:190
  107.9 7.9 %collective-permute-start.30 = (f32[2,2,2,24,128]{4,3,2,1,0:T(8,128)S(1)}, f32[2,2,2,24,128]{4,3,2,1,0:T(8,128)S(1)}, u32[]{:S(2)}, u32[]{:S(2)}) collective-permute-start(f32[2,2,2,24,128]{4,3,2,1,0:T(8,128)S(1)} %maximum_bitcast_fusion.6.refs_4_), channel_id=1, source_target_pairs={{0,1},{1,0},{2,3},{3,2},{4,5},{5,4},{6,7},{7,6},{8,9},{9,8},{10,11... | collective-permute-start | bytes 294920 | tf_op jit(solution)/shard_map/ppermute | solution.py:190
  109.0 7.4 %collective-permute-start.22 = (f32[2,2,2,24,128]{4,3,2,1,0:T(8,128)S(1)}, f32[2,2,2,24,128]{4,3,2,1,0:T(8,128)S(1)}, u32[]{:S(2)}, u32[]{:S(2)}) collective-permute-start(f32[2,2,2,24,128]{4,3,2,1,0:T(8,128)S(1)} %maximum_bitcast_fusion.3.refs_2_), channel_id=1, source_target_pairs={{0,1},{1,0},{2,3},{3,2},{4,5},{5,4},{6,7},{7,6},{8,9},{9,8},{10,11... | collective-permute-start | bytes 294920 | tf_op jit(solution)/shard_map/ppermute | solution.py:190
  110.1 4.0 %collective-permute-start.37 = (f32[2,4,2,4,128]{4,3,2,1,0:T(4,128)S(1)}, f32[2,4,2,4,128]{4,3,2,1,0:T(4,128)S(1)}, u32[]{:S(2)}, u32[]{:S(2)}) collective-permute-start(f32[2,4,2,4,128]{4,3,2,1,0:T(4,128)S(1)} %fusion.82), channel_id=1, source_target_pairs={{0,16},{4,20},{8,24},{12,28},{16,0},{20,4},{24,8},{28,12},{1,17},{... | collective-permute-start | bytes 98312 | tf_op jit(solution)/shard_map/ppermute | solution.py:190
  111.8 5.8 %collective-permute-start.18 = (f32[2,2,2,24,128]{4,3,2,1,0:T(8,128)S(1)}, f32[2,2,2,24,128]{4,3,2,1,0:T(8,128)S(1)}, u32[]{:S(2)}, u32[]{:S(2)}) collective-permute-start(f32[2,2,2,24,128]{4,3,2,1,0:T(8,128)S(1)} %maximum_bitcast_fusion.2.refs_0_), channel_id=1, source_target_pairs={{0,1},{1,0},{2,3},{3,2},{4,5},{5,4},{6,7},{7,6},{8,9},{9,8},{10,11... | collective-permute-start | bytes 294920 | tf_op jit(solution)/shard_map/ppermute | solution.py:190
  (3 other events, 3.7 us)

commit v3 on v0

v3 whole, which is shorter than its diff:
```python
import functools
import math

import jax
import jax.numpy as jnp
import numpy as np
from jax import lax
from jax.experimental import pallas as pl
from jax.experimental.pallas import tpu as pltpu
from jax.sharding import PartitionSpec as P

POLY = 4
ITERS = 2
LANES = 128
SUBLANES = 8
DIRECT_SUM = False
EARLY = False
STEP_BEFORE = 99
DIRECT_SPREAD = (False, False)
CHUNKING = "times"
ROWS_BY_COLS = (((1,), (0,)), ((), ()))
ROWS_BY_ROWS = (((1,), (1,)), ((), ()))
VMEM = pltpu.MemorySpace.VMEM
HBM = pltpu.MemorySpace.HBM
WHOLE = pl.BlockSpec(memory_space=VMEM)
OUTSIDE = pl.BlockSpec(memory_space=pl.ANY)
SCALARS = pl.BlockSpec(memory_space=pltpu.MemorySpace.SMEM)
CHEAP = pl.CostEstimate(flops=2**20, bytes_accessed=2**10, transcendentals=0)


def run(kernel, token, in_specs, out_shape, operands, scratch=(), limit=4):
    count = len(token)
    return pl.pallas_call(
        lambda *refs: kernel(*refs[count:]),
        in_specs=[OUTSIDE] * count + list(in_specs),
        out_specs=[WHOLE] * len(out_shape),
        out_shape=list(out_shape),
        scratch_shapes=list(scratch),
        compiler_params=pltpu.CompilerParams(vmem_limit_bytes=limit * 2**20),
        cost_estimate=CHEAP,
    )(*token, *operands)


def bernstein_tables(total):
    position = (np.arange(total) + 0.5) / total
    basis = np.stack(
        [math.comb(POLY - 1, j) * position**j * (1.0 - position) ** (POLY - 1 - j) for j in range(POLY)], axis=1
    )
    factor = np.linalg.cholesky(basis.T @ basis)
    solved = np.linalg.solve(factor.T, np.linalg.solve(factor, basis.T)).T
    return basis.astype(np.float32), solved.astype(np.float32)


def split(values):
    upper = values.astype(jnp.bfloat16)
    return upper, (values - upper.astype(jnp.float32)).astype(jnp.bfloat16)


def chunks_of(times, chans):
    if CHUNKING == "channels" and chans % SUBLANES == 0:
        return [(0, times, f, f + SUBLANES) for f in range(0, chans, SUBLANES)]
    return [(t, t + 1, 0, chans) for t in range(times)]


def block_of(refs, r):
    return refs[r % 2][r // 2] if len(refs) == 2 else refs[r][0]


def normals_kernel(chunk, line, share, start, fill, sources, *refs):
    t0, t1, f0, f1 = chunk
    refs = list(refs)
    place_ref = refs.pop(0)
    gain_refs = [refs.pop(0) for _ in range(sources)]
    vis_ref, coh_ref, pick_ref = [refs.pop(0) for _ in range(3)]
    outs = [refs.pop(0) for _ in range(line if DIRECT_SUM else 2)]
    own_ref = refs.pop(0) if start else None
    dirs, links = coh_ref.shape[1], coh_ref.shape[4]
    rows = (t1 - t0) * (f1 - f0)
    offsets = [(place_ref[0] ^ r) * share for r in range(line)]
    copies = []
    if fill:
        station_hbm, pick_ref = pick_ref, refs.pop(0)
        station_ref, sems = refs[-2:]
        pairs = [(station_hbm, station_ref)]
        for t in range(vis_ref.shape[1]):
            pairs += [
                (gain_refs[0].at[:, :, t], refs[0].at[:, :, t]),
                (vis_ref.at[:, t], refs[1].at[:, t]),
                (coh_ref.at[:, :, t], refs[2].at[:, :, t]),
            ]
        gain_refs, vis_ref, coh_ref = [refs[0]], refs[1], refs[2]
        copies = [pltpu.make_async_copy(src, dst, sems.at[i]) for i, (src, dst) in enumerate(pairs)]
        for copy in copies:
            copy.start()
        copies[0].wait()
        build_picks(line, share, offsets, station_ref, pick_ref)
        for t in range(t0, t1):
            copies[1 + 3 * t].wait()
    if start:
        if share % LANES:
            offsets = [r * share for r in range(line)]
        else:
            offsets = [pl.multiple_of(offset, LANES) for offset in offsets]
        blocks = [gain_refs[0][:, :, t0:t1, f0:f1, pl.ds(offset, share)] for offset in offsets]
        own_ref[...] = blocks[0]
    else:
        blocks = [block_of(gain_refs, r) for r in range(line)]
    blocks = [block.reshape(2 * dirs * rows, share) for block in blocks]
    dot = functools.partial(lax.dot_general, preferred_element_type=jnp.float32)
    upper, lower = split(jnp.concatenate(blocks, axis=1))
    first, second = [
        dot(upper, pick_ref[end], ROWS_BY_COLS) + dot(lower, pick_ref[end], ROWS_BY_COLS) for end in range(2)
    ]

    def row(values, part, k):
        begin = (part * dirs + k) * rows
        return values[begin : begin + rows]

    def coherency(part, k):
        low = f0 // 16 * 16
        high = min(-(-f1 // 16) * 16, coh_ref.shape[3])
        values = coh_ref[part, k, t0:t1, low:high].astype(jnp.float32)
        return values[:, f0 - low : f1 - low].reshape(rows, links)

    for t in range(t0, t1 if fill else t0):
        copies[2 + 3 * t].wait()
        copies[3 + 3 * t].wait()
    rest_real = vis_ref[0, t0:t1, f0:f1].reshape(rows, links)
    rest_imag = vis_ref[1, t0:t1, f0:f1].reshape(rows, links)
    sides = []
    for k in range(dirs):
        coh_real, coh_imag = coherency(0, k), coherency(1, k)
        first_real, first_imag = row(first, 0, k), row(first, 1, k)
        second_real, second_imag = row(second, 0, k), row(second, 1, k)
        left_real = second_real * coh_real + second_imag * coh_imag
        left_imag = second_imag * coh_real - second_real * coh_imag
        right_real = first_real * coh_real - first_imag * coh_imag
        right_imag = first_real * coh_imag + first_imag * coh_real
        rest_real = rest_real - (first_real * left_real + first_imag * left_imag)
        rest_imag = rest_imag - (first_imag * left_real - first_real * left_imag)
        sides.append((left_real, left_imag, right_real, right_imag))
    terms = [[], []]
    terms[0] += [rest_real * a - rest_imag * b for a, b, _, _ in sides]
    terms[0] += [rest_real * b + rest_imag * a for a, b, _, _ in sides]
    terms[0] += [a * a + b * b for a, b, _, _ in sides]
    terms[1] += [rest_real * c + rest_imag * d for _, _, c, d in sides]
    terms[1] += [rest_real * d - rest_imag * c for _, _, c, d in sides]
    terms[1] += [c * c + d * d for _, _, c, d in sides]
    total = None
    for end in range(2):
        for piece in split(jnp.concatenate(terms[end], axis=0)):
            value = dot(piece, pick_ref[end], ROWS_BY_ROWS)
            total = value if total is None else total + value
    for r in range(line):
        piece = total[:, r * share : (r + 1) * share].reshape(3, dirs, t1 - t0, f1 - f0, share)
        if DIRECT_SUM:
            outs[r][0] = piece
        else:
            outs[r % 2][r // 2] = piece
    for t in range(vis_ref.shape[1] if fill else 0):
        if not t0 <= t < t1:
            for copy in copies[1 + 3 * t : 4 + 3 * t]:
                copy.wait()


def build_picks(line, share, offsets, station_ref, pick_ref):
    links = station_ref.shape[1]
    one, zero = jnp.ones((), jnp.bfloat16), jnp.zeros((), jnp.bfloat16)
    ids = lax.broadcasted_iota(jnp.int32, (share, links), 0).astype(jnp.float32).astype(jnp.bfloat16)
    for end in range(2):
        for r in range(line):
            number = station_ref[end : end + 1, :] - offsets[r]
            number = jnp.where((number >= 0) & (number < share), number, -1)
            number = number.astype(jnp.float32).astype(jnp.bfloat16)
            pick_ref[end, r * share : (r + 1) * share] = jnp.where(ids == number, one, zero)


def picks_kernel(line, share, place_ref, station_ref, pick_ref):
    offsets = [(place_ref[0] ^ r) * share for r in range(line)]
    build_picks(line, share, offsets, station_ref, pick_ref)


def make_picks(line, count, place, stations, token):
    shapes = [VMEM((2, count, stations.shape[1]), jnp.bfloat16)]
    kernel = functools.partial(picks_kernel, line, count // line)
    return run(kernel, token, [SCALARS, WHOLE], shapes, [place, stations], (), 8)[0]


def normals(chunk, line, start, fill, place, gains, visibilities, coherencies, picks, token):
    t0, t1, f0, f1 = chunk
    dirs, links = coherencies.shape[1], coherencies.shape[4]
    count = gains[0].shape[-1] if start else gains[0].shape[-1] * line
    share = count // line
    piece = (dirs, t1 - t0, f1 - f0, share)
    lead = [1] * line if DIRECT_SUM else [line // 2] * 2
    shapes = [jax.ShapeDtypeStruct((n, 3) + piece, jnp.float32) for n in lead]
    scratch = []
    if start:
        shapes.append(jax.ShapeDtypeStruct((2,) + piece, jnp.float32))
    if fill:
        shapes.append(VMEM((2, count, links), jnp.bfloat16))
        times = visibilities.shape[1]
        scratch = [pltpu.VMEM((2, links), jnp.int32), pltpu.SemaphoreType.DMA((1 + 3 * times,))]
        shapes += [VMEM(x.shape, x.dtype) for x in (gains[0], visibilities, coherencies)]
    spaces = [HBM if fill else VMEM] * (len(gains) + 3)
    sources = [*gains, visibilities, coherencies, picks]
    sources = [pltpu.with_memory_space_constraint(x, space) for x, space in zip(sources, spaces)]
    specs = [OUTSIDE if space is HBM else WHOLE for space in spaces]
    kernel = functools.partial(normals_kernel, chunk, line, share, start, fill, len(gains))
    return run(kernel, token, [SCALARS] + specs, shapes, [place, *sources], scratch, 32)


def add_kernel(keep_ref, got_ref, own_ref, send_ref):
    for i in range(own_ref.shape[0]):
        own_ref[i] = keep_ref[2 * i] + got_ref[2 * i]
        send_ref[i] = keep_ref[2 * i + 1] + got_ref[2 * i + 1]


def add_parts(keep, got, token):
    shape = jax.ShapeDtypeStruct((keep.shape[0] // 2,) + keep.shape[1:], keep.dtype)
    return run(add_kernel, token, [WHOLE] * 2, [shape] * 2, [keep, got])


def update_kernel(chunk, parts, first, chans, penalty_ref, place_ref, basis_ref, before_ref, *refs):
    t0, t1, f0, f1 = chunk
    part_refs = refs[:parts]
    extra = refs[parts:-2]
    new_ref, sum_ref = refs[-2:]
    sum_ref[...] = before_ref[...]
    basis = basis_ref[pl.ds(place_ref[1] * chans + f0, f1 - f0)]
    for k in range(new_ref.shape[1]):
        load = penalty_ref[k]
        for t in range(t0, t1):
            weight = sum(ref[0, 2, k, t - t0] for ref in part_refs)
            divisor = weight + load
            for part in range(2):
                gain = extra[0][part, k, t - t0]
                target = gain if first else extra[1][part, k, t, f0:f1]
                total = sum(ref[0, part, k, t - t0] for ref in part_refs)
                new = (total + gain * weight + load * target) / divisor
                new_ref[part, k, t - t0] = new
                value = new if first else new + extra[2][part, k, t, f0:f1]
                for j in range(POLY):
                    row = jnp.sum(basis[:, j : j + 1] * value, axis=0, keepdims=True)
                    sum_ref[t, j, part, k : k + 1] += row


def update(chunk, first, chans, penalty, place, basis, before, parts, extra, token):
    shapes = [
        jax.ShapeDtypeStruct((2,) + parts[0].shape[2:], jnp.float32),
        jax.ShapeDtypeStruct(before.shape, jnp.float32),
    ]
    operands = [basis, before, *parts, *extra]
    kernel = functools.partial(update_kernel, chunk, len(parts), first, chans)
    return run(kernel, token, [SCALARS] * 2 + [WHOLE] * len(operands), shapes, [penalty, place, *operands])


def smooth_kernel(chunks, first, chans, place_ref, solved_ref, sum_ref, *refs):
    one_ref, two_ref = refs[-2:]
    solved = solved_ref[pl.ds(place_ref[1] * chans, chans)]
    for (t0, t1, f0, f1), gain_ref in zip(chunks, refs):
        for part in range(2):
            for k in range(one_ref.shape[1]):
                for t in range(t0, t1):
                    flat = sum(
                        solved[f0:f1, j : j + 1] * sum_ref[t, j, part, k : k + 1] for j in range(POLY)
                    )
                    value = gain_ref[part, k, t - t0]
                    at = (part, k, t, slice(f0, f1))
                    if first:
                        dual = value - flat
                        one_ref[at] = flat - dual
                    else:
                        dual = refs[len(chunks)][at] + value - flat
                        one_ref[at] = flat
                    two_ref[at] = dual


def smooth(chunks, first, place, solved, sums, gains, extra, dims, token):
    operands = [solved, sums, *gains, *extra]
    shapes = [jax.ShapeDtypeStruct(dims, jnp.float32)] * 2
    kernel = functools.partial(smooth_kernel, chunks, first, dims[3])
    return run(kernel, token, [SCALARS] + [WHOLE] * len(operands), shapes, [place, *operands])


def assemble_kernel(chunks, line, share, place_ref, *refs):
    out_ref = refs[-1]
    each = (len(refs) - 1) // len(chunks)
    for i, (t0, t1, f0, f1) in enumerate(chunks):
        for r in range(line):
            offset = pl.multiple_of((place_ref[0] ^ r) * share, LANES)
            out_ref[:, :, t0:t1, f0:f1, pl.ds(offset, share)] = block_of(refs[i * each : (i + 1) * each], r)


def assemble(chunks, line, place, gains, dims):
    share = dims[-1] // line
    if share % LANES:
        whole = jnp.zeros(dims, jnp.float32)
        for (t0, t1, f0, f1), blocks in zip(chunks, gains):
            stacked = jnp.stack([block_of(blocks, r) for r in range(line)])
            parts = [lax.dynamic_index_in_dim(stacked, place[0] ^ r, 0, False) for r in range(line)]
            whole = whole.at[:, :, t0:t1, f0:f1].set(jnp.concatenate(parts, axis=-1))
        return whole
    flat = [block for blocks in gains for block in blocks]
    kernel = functools.partial(assemble_kernel, chunks, line, share)
    shapes = [jax.ShapeDtypeStruct(dims, jnp.float32)]
    return run(kernel, [], [SCALARS] + [WHOLE] * len(flat), shapes, [place, *flat])[0]


def shards(visibilities, coherencies, start_gains, penalty, stations):
    dims = start_gains.shape
    _, dirs, times, chans, count = dims
    line = lax.axis_size("bl")
    index = lax.axis_index("bl")
    place = jnp.stack([index, lax.axis_index("chan")]).astype(jnp.int32)
    groups = lax.axis_size("chan")
    share = count // line
    basis, solved = [jnp.asarray(table) for table in bernstein_tables(chans * groups)]

    def swap(values, axis, size, bit):
        return lax.ppermute(values, axis, [(i, i ^ bit) for i in range(size)])

    def chan_steps(values):
        steps = [values]
        bit = 1
        while bit < groups:
            steps.append(steps[-1] + swap(steps[-1], "chan", groups, bit))
            bit *= 2
        return steps

    ordered = start_gains
    if share % LANES:
        parts = [lax.dynamic_slice_in_dim(start_gains, (index ^ r) * share, share, 4) for r in range(line)]
        ordered = jnp.concatenate(parts, axis=4)
    own_dims = dims[:4] + (share,)
    chunks = chunks_of(times, chans)
    token = []
    gains = own = targets = duals = projected = None

    def spread(values, direct):
        blocks, bit, arrived = values[None], line // 2, None
        if direct:
            blocks = [blocks] + [swap(blocks, "bl", line, r) for r in range(1, line)]
            return blocks, blocks[1]
        while bit > 1:
            got = swap(blocks, "bl", line, bit)
            arrived = got if arrived is None else arrived
            blocks = jnp.stack([blocks, got], axis=1).reshape((2 * blocks.shape[0],) + blocks.shape[1:])
            bit //= 2
        return [blocks, swap(blocks, "bl", line, 1)], arrived

    for iteration in range(ITERS):
        first = iteration == 0
        parts, fresh = [], []
        if not first:
            picks = make_picks(line, count, place, stations, token)
            token = [picks]
            steps = chan_steps(projected)
        for c, chunk in enumerate(chunks):
            fill = first and c == 0
            if not first and c + STEP_BEFORE < len(steps):
                token = token + [steps[c + STEP_BEFORE]]
            out = normals(
                chunk,
                line,
                first,
                fill,
                place,
                [ordered] if first else gains[c],
                visibilities,
                coherencies,
                stations if fill else picks,
                token,
            )
            token = [out[0]]
            count_sent = line if DIRECT_SUM else 2
            if DIRECT_SUM:
                parts.append([out[0]] + [swap(out[r], "bl", line, r) for r in range(1, line)])
            else:
                parts.append([out[0], swap(out[1], "bl", line, 1)])
            rest = list(out[count_sent:])
            if first:
                fresh.append(rest.pop(0))
            if fill:
                picks, ordered, visibilities, coherencies = rest
        if first:
            own = fresh
        else:
            targets, duals = smooth(chunks, True, place, solved, steps[-1], own, [], own_dims, [])
        bit = 2
        while bit < line and not DIRECT_SUM:
            for c in range(len(chunks)):
                keep, send = add_parts(*parts[c], token)
                parts[c] = [keep, swap(send, "bl", line, bit)]
                token = [keep]
            bit *= 2
        gains, fresh = [], []
        projected = jnp.zeros((times, POLY, 2, dirs, share), jnp.float32)
        for c, chunk in enumerate(chunks):
            extra = [own[c]] if first else [own[c], targets, duals]
            new, projected = update(chunk, first, chans, penalty, place, basis, projected, parts[c], extra, token)
            pair, arrived = spread(new, DIRECT_SPREAD[iteration])
            token = [new] if first or not EARLY else [new, arrived]
            gains.append(pair)
            fresh.append(new)
        own = fresh
    steps = chan_steps(projected)
    consensus, dual = smooth(chunks, False, place, solved, steps[-1], own, [duals], own_dims, [])
    return assemble(chunks, line, place, gains, dims), consensus, dual


def solution(mesh):
    in_specs = (
        P(None, None, "chan", "bl"),
        P(None, None, None, "chan", "bl"),
        P(None, None, None, "chan", None),
        P(),
        P(None, "bl"),
    )
    out_specs = (
        P(None, None, None, "chan", None),
        P(None, None, None, "chan", "bl"),
        P(None, None, None, "chan", "bl"),
    )
    return jax.shard_map(shards, mesh=mesh, in_specs=in_specs, out_specs=out_specs, check_vma=False)
```

time: 321 us -> 102 us (0.32); the launches traced: 315 us -> 101 us
  waiting for transfers between devices: 218 us -> 44.7 us
  matrix products: 49.2 us -> 0 us
  other arithmetic: 30.5 us -> 0.19 us
  Pallas kernels: 0 us -> 30.2 us
  starting transfers between devices: 0.16 us -> 25.3 us
  between operations: 14.5 us -> 0.85 us
    psum x4 -> x0, waiting for transfers between devices: 218 us -> none  [the longest x2 113 us: shards(): lax.psum(normals(visibilities, coherencies, gains, pick_first, pick_secon...]
    dot_general x29 -> x0, matrix products: 45.8 us -> none  [the longest x8 15.3 us: exact_product(): total = jnp.dot(upper, selector, preferred_element_type=jnp.float32)]
    ppermute x0 -> x22, waiting for transfers between devices: none -> 44.7 us  [swap(): return lax.ppermute(values, axis, [(i, i ^ bit) for i in range(size)])]
    pallas_call x0 -> x16, Pallas kernels: none -> 30.2 us  [run(): pl.pallas_call(lambda *refs: kernel(*refs[count:]), in_specs=[OUTSIDE] *...]
    ppermute x0 -> x22, starting transfers between devices: none -> 25.3 us  [swap(): return lax.ppermute(values, axis, [(i, i ^ bit) for i in range(size)])]
    convert_element_type x18 -> x0, other arithmetic: 11.8 us -> none  [the longest x6 5.56 us: exact_product(): (rest - lax.optimization_barrier(middle).astype(jnp.float32)).astype(jnp....]
    sub x3 -> x0, other arithmetic: 6.51 us -> none  [the longest x2 5.78 us: normals(): resid_real * left_real - resid_imag * left_imag]
    add x5 -> x6, other arithmetic: 4.49 us -> 0.06 us  [chan_steps(): steps.append(steps[-1] + swap(steps[-1], 'chan', groups, bit))]
  transfers between devices with their start and end apart: 4 -> 22, of which waited for: 4 -> 16; matrix products, arithmetic and copies ran while one was open for 1% -> 0% of each run, Pallas kernels for 0% -> 22%
where the time goes in v3:
time: 102 us; the launch traced here: 101 us
  waiting for transfers between devices  44.7 us (44%)
  Pallas kernels  30.2 us (30%)
  starting transfers between devices  25.3 us (25%)
    ppermute x22, waiting for transfers between devices, swap(): return lax.ppermute(values, axis, [(i, i ^ bit) for i in range(size)])  44.7 us
    pallas_call x16, Pallas kernels, run(): pl.pallas_call(lambda *refs: kernel(*refs[count:]), in_specs=[OUTSIDE] *...  30.2 us
    ppermute x22, starting transfers between devices, swap(): return lax.ppermute(values, axis, [(i, i ^ bit) for i in range(size)])  25.3 us
  transfers between devices with their start and end apart: 22, of which 16 were waited for; matrix products, arithmetic and copies ran while one was open for 0% of the time, Pallas kernels for 22%

profile of v3, /device:TPU:0, one launch (start us, length us, event | category | flops | bytes accessed | tf_op | source)
XLA Modules:
  0.0 101.3 jit_solution(11766081925966489337)
XLA Ops:
  0.6 0.1 pad_add_fusion.refs_0_.refs_1_.refs_2_
  0.7 6.9 %shard_map.94 = (f32[2,3,4,1,24,128]{5,4,3,2,1,0:T(8,128)S(1)}, f32[2,3,4,1,24,128]{5,4,3,2,1,0:T(8,128)S(1)}, f32[2,4,1,24,128]{4,3,2,1,0:T(8,128)S(1)}, bf16[2...) custom-call(s32[2]{0:T(128)S(1)} %pad_add_fusion.refs_0_.refs_1_.ref, ...), custom_call_target="tpu_custom_call" | custom-call | flops 1048576 | bytes 1024 | tf_op jit(solution)/shard_map/pallas_call | solution.py:33
  7.6 3.1 %collective-permute-start = (f32[2,3,4,1,24,128]{5,4,3,2,1,0:T(8,128)S(1)}, f32[2,3,4,1,24,128]{5,4,3,2,1,0:T(8,128)S(1)}, u32[]{:S(2)}, u32[]{:S(2)}) collective-permute-start(f32[2,3,4,1,24,128]{5,4,3,2,1,0:T(8,128)S(1)} %get-tuple-element.43), channel_id=1, source_target_pairs={{0,1},{1,0},{2,3},{3,2},{4,5},{5,4},{6,7},{7,6},{8,9},{9,8},{10,11... | collective-permute-start | bytes 884744 | tf_op jit(solution)/shard_map/ppermute | solution.py:321
  10.7 5.2 %shard_map.95 = (f32[2,3,4,1,24,128]{5,4,3,2,1,0:T(8,128)S(1)}, f32[2,3,4,1,24,128]{5,4,3,2,1,0:T(8,128)S(1)}, f32[2,4,1,24,128]{4,3,2,1,0:T(8,128)S(1)}) custom-call(f32[2,3,4,1,24,128]{5,4,3,2,1,0:T(8,128)S(1)} %get-tuple-element.37.refs_0_.refs_1_, s32[2]{0:T(128)S(1)} %pad_add_fusion.refs_0_.refs_1_.refs_2_, ...), custom_call_target="tpu_custom_call" | custom-call | flops 1048576 | bytes 1024 | tf_op jit(solution)/shard_map/pallas_call | solution.py:33
  15.9 0.1 collective-permute-start.1
  16.1 1.9 %collective-permute-done.refs_2_ = f32[2,3,4,1,24,128]{5,4,3,2,1,0:T(8,128)S(1)} collective-permute-done((f32[2,3,4,1,24,128]{5,4,3,2,1,0:T(8,128)S(1)}, f32[2,3,4,1,24,128]{5,4,3,2,1,0:T(8,128)S(1)}, u32[]{:S(2)}, u32[]{:S(2)}) %collective-permute-start) | collective-permute-done | bytes 294944 | tf_op jit(solution)/shard_map/ppermute | solution.py:321
  18.0 2.6 %collective-permute-start.2 = (f32[1,3,4,1,24,128]{5,4,3,2,1,0:T(8,128)S(1)}, f32[1,3,4,1,24,128]{5,4,3,2,1,0:T(8,128)S(1)}, u32[]{:S(2)}, u32[]{:S(2)}) collective-permute-start(f32[1,3,4,1,24,128]{5,4,3,2,1,0:T(8,128)S(1)} %get-tuple-element.47), channel_id=1, source_target_pairs={{0,2},{1,3},{2,0},{3,1},{4,6},{5,7},{6,4},{7,5},{8,10},{9,11},{10,... | collective-permute-start | bytes 442376 | tf_op jit(solution)/shard_map/ppermute | solution.py:321
  20.6 7.1 %collective-permute-done.1.refs_2_ = f32[2,3,4,1,24,128]{5,4,3,2,1,0:T(8,128)S(1)} collective-permute-done((f32[2,3,4,1,24,128]{5,4,3,2,1,0:T(8,128)S(1)}, f32[2,3,4,1,24,128]{5,4,3,2,1,0:T(8,128)S(1)}, u32[]{:S(2)}, u32[]{:S(2)}) %collective-permute-start.1) | collective-permute-done | bytes 294944 | tf_op jit(solution)/shard_map/ppermute | solution.py:321
  27.7 1.0 collective-permute-start.3
  28.7 0.7 shard_map.98
  29.3 2.1 %collective-permute-start.4 = (f32[1,2,4,1,24,128]{5,4,2,1,3,0:T(8,128)S(1)}, f32[1,2,4,1,24,128]{5,4,2,1,3,0:T(8,128)S(1)}, u32[]{:S(2)}, u32[]{:S(2)}) collective-permute-start(f32[1,2,4,1,24,128]{5,4,2,1,3,0:T(8,128)S(1)} %bitcast.22), channel_id=1, source_target_pairs={{0,2},{1,3},{2,0},{3,1},{4,6},{5,7},{6,4},{7,5},{8,10},{9,11},{10,... | collective-permute-start | bytes 294920 | tf_op jit(solution)/shard_map/ppermute | solution.py:321
  31.5 7.7 %collective-permute-done.3.refs_6_ = f32[1,3,4,1,24,128]{5,4,3,2,1,0:T(8,128)S(1)} collective-permute-done((f32[1,3,4,1,24,128]{5,4,3,2,1,0:T(8,128)S(1)}, f32[1,3,4,1,24,128]{5,4,3,2,1,0:T(8,128)S(1)}, u32[]{:S(2)}, u32[]{:S(2)}) %collective-permute-start.3) | collective-permute-done | bytes 147488 | tf_op jit(solution)/shard_map/ppermute | solution.py:321
  39.1 0.7 shard_map.99
  39.8 0.1 collective-permute-start.6
  39.9 0.5 collective-permute-done.4
  40.4 1.9 %collective-permute-start.5 = (f32[2,2,4,1,24,128]{5,4,3,2,1,0:T(8,128)S(1)}, f32[2,2,4,1,24,128]{5,4,3,2,1,0:T(8,128)S(1)}, u32[]{:S(2)}, u32[]{:S(2)}) collective-permute-start(f32[2,2,4,1,24,128]{5,4,3,2,1,0:T(8,128)S(1)} %maximum_bitcast_fusion.refs_2_), channel_id=1, source_target_pairs={{0,1},{1,0},{2,3},{3,2},{4,5},{5,4},{6,7},{7,6},{8,9},{9,8},{10,11... | collective-permute-start | bytes 589832 | tf_op jit(solution)/shard_map/ppermute | solution.py:321
  42.3 3.7 %collective-permute-done.6 = f32[1,2,4,1,24,128]{5,4,2,1,3,0:T(8,128)S(1)} collective-permute-done((f32[1,2,4,1,24,128]{5,4,2,1,3,0:T(8,128)S(1)}, f32[1,2,4,1,24,128]{5,4,2,1,3,0:T(8,128)S(1)}, u32[]{:S(2)}, u32[]{:S(2)}) %collective-permute-start.6) | collective-permute-done | bytes 98336 | tf_op jit(solution)/shard_map/ppermute | solution.py:321
  46.0 0.1 collective-permute-start.7
  46.1 1.1 %shard_map.100.refs_0_.refs_6_ = bf16[2,512,2048]{2,1,0:T(8,128)(2,1)S(1)} custom-call(f32[2,4,1,24,128]{4,3,2,1,0:T(8,128)S(1)} %get-tuple-element.53.refs_0_.refs_4_.refs_7_, s32[2]{0:T(128)S(1)} %pad_add_fusion.refs_0_.refs_1_.refs_2_, s32[2,2048]{1,0:T(2,128)S(1)} %copy-done.2), custom_call_target="tpu_custom_call" | custom-call | flops 1048576 | bytes 1024 | tf_op jit(solution)/shard_map/pallas_call | solution.py:33
  47.1 2.4 %collective-permute-done.5.refs_3_ = f32[2,2,4,1,24,128]{5,4,3,2,1,0:T(8,128)S(1)} collective-permute-done((f32[2,2,4,1,24,128]{5,4,3,2,1,0:T(8,128)S(1)}, f32[2,2,4,1,24,128]{5,4,3,2,1,0:T(8,128)S(1)}, u32[]{:S(2)}, u32[]{:S(2)}) %collective-permute-start.5) | collective-permute-done | bytes 196640 | tf_op jit(solution)/shard_map/ppermute | solution.py:321
  49.6 5.4 %shard_map.101 = (f32[2,3,4,1,24,128]{5,4,3,2,1,0:T(8,128)S(1)}, f32[2,3,4,1,24,128]{5,4,3,2,1,0:T(8,128)S(1)}) custom-call(bf16[2,512,2048]{2,1,0:T(8,128)(2,1)S(1)} %shard_map.100.refs_0_.refs_6_, s32[2]{0:T(128)S(1)} %pad_add_fusion.refs_0_.refs_1_.refs_2_, f32[2,2,4,1,24,128]{5,4,3,2,1,0:T(8,128)S(1)} %maximum_bitcast_fusion.refs_2_, ...), custom_call_target="tpu_custom_call" | custom-call | flops 1048576 | bytes 1024 | tf_op jit(solution)/shard_map/pallas_call | solution.py:33
  55.0 0.6 collective-permute-start.8
  55.6 5.2 %shard_map.102 = (f32[2,3,4,1,24,128]{5,4,3,2,1,0:T(8,128)S(1)}, f32[2,3,4,1,24,128]{5,4,3,2,1,0:T(8,128)S(1)}) custom-call(f32[2,3,4,1,24,128]{5,4,3,2,1,0:T(8,128)S(1)} %get-tuple-element.54.refs_0_.refs_1_, s32[2]{0:T(128)S(1)} %pad_add_fusion.refs_0_.refs_1_.refs_2_, f32[2,2,4,1,24,128]{5,4,3,2,1,0:T(8,128)S(1)} %maximum_bitcast_fusion.1.refs_2_, ...), custom_call_target="tpu_custom_call" | custom-call | flops 1048576 | bytes 1024 | tf_op jit(solution)/shard_map/pallas_call | solution.py:33
  60.8 1.5 %collective-permute-start.9 = (f32[2,3,4,1,24,128]{5,4,3,2,1,0:T(8,128)S(1)}, f32[2,3,4,1,24,128]{5,4,3,2,1,0:T(8,128)S(1)}, u32[]{:S(2)}, u32[]{:S(2)}) collective-permute-start(f32[2,3,4,1,24,128]{5,4,3,2,1,0:T(8,128)S(1)} %get-tuple-element.58), channel_id=1, source_target_pairs={{0,1},{1,0},{2,3},{3,2},{4,5},{5,4},{6,7},{7,6},{8,9},{9,8},{10,11... | collective-permute-start | bytes 884744 | tf_op jit(solution)/shard_map/ppermute | solution.py:321
  62.3 0.7 collective-permute-done.8.refs_2_
  63.1 0.5 collective-permute-start.10
  63.6 1.2 %collective-permute-done.11 = f32[2,4,2,4,128]{4,3,2,1,0:T(4,128)S(1)} collective-permute-done((f32[2,4,2,4,128]{4,3,2,1,0:T(4,128)S(1)}, f32[2,4,2,4,128]{4,3,2,1,0:T(4,128)S(1)}, u32[]{:S(2)}, u32[]{:S(2)}) %collective-permute-start.11) | collective-permute-done | bytes 32800 | tf_op jit(solution)/shard_map/ppermute | solution.py:321
  64.8 1.6 %collective-permute-start.12 = (f32[2,4,2,4,128]{4,3,2,1,0:T(4,128)S(1)}, f32[2,4,2,4,128]{4,3,2,1,0:T(4,128)S(1)}, u32[]{:S(2)}, u32[]{:S(2)}) collective-permute-start(f32[2,4,2,4,128]{4,3,2,1,0:T(4,128)S(1)} %add.18), channel_id=1, source_target_pairs={{0,8},{4,12},{8,0},{12,4},{16,24},{20,28},{24,16},{28,20},{1,9},{5... | collective-permute-start | bytes 98312 | tf_op jit(solution)/shard_map/ppermute | solution.py:321
  66.4 5.2 %collective-permute-done.9.refs_2_ = f32[2,3,4,1,24,128]{5,4,3,2,1,0:T(8,128)S(1)} collective-permute-done((f32[2,3,4,1,24,128]{5,4,3,2,1,0:T(8,128)S(1)}, f32[2,3,4,1,24,128]{5,4,3,2,1,0:T(8,128)S(1)}, u32[]{:S(2)}, u32[]{:S(2)}) %collective-permute-start.9) | collective-permute-done | bytes 294944 | tf_op jit(solution)/shard_map/ppermute | solution.py:321
  71.6 0.4 collective-permute-start.16
  72.0 1.8 %collective-permute-start.13 = (f32[2,4,2,4,128]{4,3,2,1,0:T(4,128)S(1)}, f32[2,4,2,4,128]{4,3,2,1,0:T(4,128)S(1)}, u32[]{:S(2)}, u32[]{:S(2)}) collective-permute-start(f32[2,4,2,4,128]{4,3,2,1,0:T(4,128)S(1)} %add.19), channel_id=1, source_target_pairs={{0,16},{4,20},{8,24},{12,28},{16,0},{20,4},{24,8},{28,12},{1,17},{... | collective-permute-start | bytes 98312 | tf_op jit(solution)/shard_map/ppermute | solution.py:321
  73.8 2.2 %collective-permute-done.13 = f32[2,4,2,4,128]{4,3,2,1,0:T(4,128)S(1)} collective-permute-done((f32[2,4,2,4,128]{4,3,2,1,0:T(4,128)S(1)}, f32[2,4,2,4,128]{4,3,2,1,0:T(4,128)S(1)}, u32[]{:S(2)}, u32[]{:S(2)}) %collective-permute-start.13) | collective-permute-done | bytes 32800 | tf_op jit(solution)/shard_map/ppermute | solution.py:321
  76.0 0.7 shard_map.105
  76.7 0.7 shard_map.106
  77.4 2.7 %collective-permute-start.14 = (f32[1,2,4,1,24,128]{5,4,2,1,3,0:T(8,128)S(1)}, f32[1,2,4,1,24,128]{5,4,2,1,3,0:T(8,128)S(1)}, u32[]{:S(2)}, u32[]{:S(2)}) collective-permute-start(f32[1,2,4,1,24,128]{5,4,2,1,3,0:T(8,128)S(1)} %bitcast.26), channel_id=1, source_target_pairs={{0,2},{1,3},{2,0},{3,1},{4,6},{5,7},{6,4},{7,5},{8,10},{9,11},{10,... | collective-permute-start | bytes 294920 | tf_op jit(solution)/shard_map/ppermute | solution.py:321
  80.1 2.3 %collective-permute-done.16.refs_6_ = f32[1,3,4,1,24,128]{5,4,3,2,1,0:T(8,128)S(1)} collective-permute-done((f32[1,3,4,1,24,128]{5,4,3,2,1,0:T(8,128)S(1)}, f32[1,3,4,1,24,128]{5,4,3,2,1,0:T(8,128)S(1)}, u32[]{:S(2)}, u32[]{:S(2)}) %collective-permute-start.16) | collective-permute-done | bytes 147488 | tf_op jit(solution)/shard_map/ppermute | solution.py:321
  82.4 0.7 shard_map.107
  83.1 0.1 collective-permute-start.17
  83.2 1.8 %collective-permute-done.14 = f32[1,2,4,1,24,128]{5,4,2,1,3,0:T(8,128)S(1)} collective-permute-done((f32[1,2,4,1,24,128]{5,4,2,1,3,0:T(8,128)S(1)}, f32[1,2,4,1,24,128]{5,4,2,1,3,0:T(8,128)S(1)}, u32[]{:S(2)}, u32[]{:S(2)}) %collective-permute-start.14) | collective-permute-done | bytes 98336 | tf_op jit(solution)/shard_map/ppermute | solution.py:321
  84.9 1.7 %collective-permute-start.15 = (f32[2,2,4,1,24,128]{5,4,3,2,1,0:T(8,128)S(1)}, f32[2,2,4,1,24,128]{5,4,3,2,1,0:T(8,128)S(1)}, u32[]{:S(2)}, u32[]{:S(2)}) collective-permute-start(f32[2,2,4,1,24,128]{5,4,3,2,1,0:T(8,128)S(1)} %maximum_bitcast_fusion.2.refs_1_), channel_id=1, source_target_pairs={{0,1},{1,0},{2,3},{3,2},{4,5},{5,4},{6,7},{7,6},{8,9},{9,8},{10,11... | collective-permute-start | bytes 589832 | tf_op jit(solution)/shard_map/ppermute | solution.py:321
  86.6 2.3 %collective-permute-done.17 = f32[1,2,4,1,24,128]{5,4,2,1,3,0:T(8,128)S(1)} collective-permute-done((f32[1,2,4,1,24,128]{5,4,2,1,3,0:T(8,128)S(1)}, f32[1,2,4,1,24,128]{5,4,2,1,3,0:T(8,128)S(1)}, u32[]{:S(2)}, u32[]{:S(2)}) %collective-permute-start.17) | collective-permute-done | bytes 98336 | tf_op jit(solution)/shard_map/ppermute | solution.py:321
  89.1 1.2 %collective-permute-done.19 = f32[2,4,2,4,128]{4,3,2,1,0:T(4,128)S(1)} collective-permute-done((f32[2,4,2,4,128]{4,3,2,1,0:T(4,128)S(1)}, f32[2,4,2,4,128]{4,3,2,1,0:T(4,128)S(1)}, u32[]{:S(2)}, u32[]{:S(2)}) %collective-permute-start.19) | collective-permute-done | bytes 32800 | tf_op jit(solution)/shard_map/ppermute | solution.py:321
  90.3 1.7 %collective-permute-start.20 = (f32[2,4,2,4,128]{4,3,2,1,0:T(4,128)S(1)}, f32[2,4,2,4,128]{4,3,2,1,0:T(4,128)S(1)}, u32[]{:S(2)}, u32[]{:S(2)}) collective-permute-start(f32[2,4,2,4,128]{4,3,2,1,0:T(4,128)S(1)} %add.21), channel_id=1, source_target_pairs={{0,8},{4,12},{8,0},{12,4},{16,24},{20,28},{24,16},{28,20},{1,9},{5... | collective-permute-start | bytes 98312 | tf_op jit(solution)/shard_map/ppermute | solution.py:321
  92.1 2.3 %collective-permute-done.20 = f32[2,4,2,4,128]{4,3,2,1,0:T(4,128)S(1)} collective-permute-done((f32[2,4,2,4,128]{4,3,2,1,0:T(4,128)S(1)}, f32[2,4,2,4,128]{4,3,2,1,0:T(4,128)S(1)}, u32[]{:S(2)}, u32[]{:S(2)}) %collective-permute-start.20) | collective-permute-done | bytes 32800 | tf_op jit(solution)/shard_map/ppermute | solution.py:321
  94.3 1.7 %collective-permute-start.21 = (f32[2,4,2,4,128]{4,3,2,1,0:T(4,128)S(1)}, f32[2,4,2,4,128]{4,3,2,1,0:T(4,128)S(1)}, u32[]{:S(2)}, u32[]{:S(2)}) collective-permute-start(f32[2,4,2,4,128]{4,3,2,1,0:T(4,128)S(1)} %add.22), channel_id=1, source_target_pairs={{0,16},{4,20},{8,24},{12,28},{16,0},{20,4},{24,8},{28,12},{1,17},{... | collective-permute-start | bytes 98312 | tf_op jit(solution)/shard_map/ppermute | solution.py:321
  96.0 2.3 %collective-permute-done.21 = f32[2,4,2,4,128]{4,3,2,1,0:T(4,128)S(1)} collective-permute-done((f32[2,4,2,4,128]{4,3,2,1,0:T(4,128)S(1)}, f32[2,4,2,4,128]{4,3,2,1,0:T(4,128)S(1)}, u32[]{:S(2)}, u32[]{:S(2)}) %collective-permute-start.21) | collective-permute-done | bytes 32800 | tf_op jit(solution)/shard_map/ppermute | solution.py:321
  98.3 1.4 %shard_map.109 = (f32[2,4,2,24,128]{4,3,2,1,0:T(8,128)}, f32[2,4,2,24,128]{4,3,2,1,0:T(8,128)}) custom-call(s32[2]{0:T(128)S(1)} %pad_add_fusion.refs_0_.refs_1_.refs_2_, f32[192,4]{1,0:T(8,128)S(1)} %copy-done.1, f32[2,4,2,4,128]{4,3,2,1,0:T(4,128)S(1)} %add.23.refs_2_, f32[2,4,1,24,128]{4,3,2,1,0:T(8,128)S(1)} %get-tuple-element.64.refs_0_.refs_3_, ...), custom_call_target="tpu_custom_call" | custom-call | flops 1048576 | bytes 1024 | tf_op jit(solution)/shard_map/pallas_call | solution.py:33
  99.8 1.5 %shard_map.108 = f32[2,4,2,24,512]{4,3,2,1,0:T(8,128)} custom-call(s32[2]{0:T(128)S(1)} %pad_add_fusion.refs_0_.refs_1_.refs_2_, f32[2,2,4,1,24,128]{5,4,3,2,1,0:T(8,128)S(1)} %maximum_bitcast_fusion.2.refs_1_, f32[2,2,4,1,24,128]{5,4,3,2,1,0:T(8,128)S(1)} %collective-permute-done.15.refs_2_, f32[2,2,4,1,24,128]{5,4,3,2,1,0:T(8,128)S(1)} %maximum_bitcast_fusion.3.refs_3_, ...), custom_call_target="tpu_custom_call" | custom-call | flops 1048576 | bytes 1024 | tf_op jit(solution)/shard_map/pallas_call | solution.py:33
  (32 shorter events, 0.4 us)
Async XLA Ops:
  7.6 10.3 %collective-permute-start = (f32[2,3,4,1,24,128]{5,4,3,2,1,0:T(8,128)S(1)}, f32[2,3,4,1,24,128]{5,4,3,2,1,0:T(8,128)S(1)}, u32[]{:S(2)}, u32[]{:S(2)}) collective-permute-start(f32[2,3,4,1,24,128]{5,4,3,2,1,0:T(8,128)S(1)} %get-tuple-element.43), channel_id=1, source_target_pairs={{0,1},{1,0},{2,3},{3,2},{4,5},{5,4},{6,7},{7,6},{8,9},{9,8},{10,11... | collective-permute-start | bytes 884744 | tf_op jit(solution)/shard_map/ppermute | solution.py:321
  10.7 17.9 %copy-start = (f32[192,4]{1,0:T(8,128)S(1)}, f32[192,4]{1,0:T(8,128)}, u32[]{:S(2)}) copy-start(f32[192,4]{1,0:T(8,128)} %constant.15.clone.refs_3_) | copy-start | bytes 9220
  10.7 17.9 %copy-start.3 = (f32[4]{0:T(128)S(1)}, f32[4]{0:T(128)}, u32[]{:S(2)}) copy-start(f32[4]{0:T(128)} %refs_1_.11) | copy-start | bytes 52
  10.7 35.3 %copy-start.2 = (s32[2,2048]{1,0:T(2,128)S(1)}, s32[2,2048]{1,0:T(2,128)}, u32[]{:S(2)}) copy-start(s32[2,2048]{1,0:T(2,128)} %refs_2_.3) | copy-start | bytes 49156
  15.9 11.7 %collective-permute-start.1 = (f32[2,3,4,1,24,128]{5,4,3,2,1,0:T(8,128)S(1)}, f32[2,3,4,1,24,128]{5,4,3,2,1,0:T(8,128)S(1)}, u32[]{:S(2)}, u32[]{:S(2)}) collective-permute-start(f32[2,3,4,1,24,128]{5,4,3,2,1,0:T(8,128)S(1)} %get-tuple-element.45), channel_id=1, source_target_pairs={{0,1},{1,0},{2,3},{3,2},{4,5},{5,4},{6,7},{7,6},{8,9},{9,8},{10,11... | collective-permute-start | bytes 884744 | tf_op jit(solution)/shard_map/ppermute | solution.py:321
  18.0 10.7 %collective-permute-start.2 = (f32[1,3,4,1,24,128]{5,4,3,2,1,0:T(8,128)S(1)}, f32[1,3,4,1,24,128]{5,4,3,2,1,0:T(8,128)S(1)}, u32[]{:S(2)}, u32[]{:S(2)}) collective-permute-start(f32[1,3,4,1,24,128]{5,4,3,2,1,0:T(8,128)S(1)} %get-tuple-element.47), channel_id=1, source_target_pairs={{0,2},{1,3},{2,0},{3,1},{4,6},{5,7},{6,4},{7,5},{8,10},{9,11},{10,... | collective-permute-start | bytes 442376 | tf_op jit(solution)/shard_map/ppermute | solution.py:321
  27.7 11.5 %collective-permute-start.3 = (f32[1,3,4,1,24,128]{5,4,3,2,1,0:T(8,128)S(1)}, f32[1,3,4,1,24,128]{5,4,3,2,1,0:T(8,128)S(1)}, u32[]{:S(2)}, u32[]{:S(2)}) collective-permute-start(f32[1,3,4,1,24,128]{5,4,3,2,1,0:T(8,128)S(1)} %get-tuple-element.51), channel_id=1, source_target_pairs={{0,2},{1,3},{2,0},{3,1},{4,6},{5,7},{6,4},{7,5},{8,10},{9,11},{10,... | collective-permute-start | bytes 442376 | tf_op jit(solution)/shard_map/ppermute | solution.py:321
  29.3 11.1 %collective-permute-start.4 = (f32[1,2,4,1,24,128]{5,4,2,1,3,0:T(8,128)S(1)}, f32[1,2,4,1,24,128]{5,4,2,1,3,0:T(8,128)S(1)}, u32[]{:S(2)}, u32[]{:S(2)}) collective-permute-start(f32[1,2,4,1,24,128]{5,4,2,1,3,0:T(8,128)S(1)} %bitcast.22), channel_id=1, source_target_pairs={{0,2},{1,3},{2,0},{3,1},{4,6},{5,7},{6,4},{7,5},{8,10},{9,11},{10,... | collective-permute-start | bytes 294920 | tf_op jit(solution)/shard_map/ppermute | solution.py:321
  39.8 6.2 %collective-permute-start.6 = (f32[1,2,4,1,24,128]{5,4,2,1,3,0:T(8,128)S(1)}, f32[1,2,4,1,24,128]{5,4,2,1,3,0:T(8,128)S(1)}, u32[]{:S(2)}, u32[]{:S(2)}) collective-permute-start(f32[1,2,4,1,24,128]{5,4,2,1,3,0:T(8,128)S(1)} %bitcast.24), channel_id=1, source_target_pairs={{0,2},{1,3},{2,0},{3,1},{4,6},{5,7},{6,4},{7,5},{8,10},{9,11},{10,... | collective-permute-start | bytes 294920 | tf_op jit(solution)/shard_map/ppermute | solution.py:321
  40.4 9.2 %collective-permute-start.5 = (f32[2,2,4,1,24,128]{5,4,3,2,1,0:T(8,128)S(1)}, f32[2,2,4,1,24,128]{5,4,3,2,1,0:T(8,128)S(1)}, u32[]{:S(2)}, u32[]{:S(2)}) collective-permute-start(f32[2,2,4,1,24,128]{5,4,3,2,1,0:T(8,128)S(1)} %maximum_bitcast_fusion.refs_2_), channel_id=1, source_target_pairs={{0,1},{1,0},{2,3},{3,2},{4,5},{5,4},{6,7},{7,6},{8,9},{9,8},{10,11... | collective-permute-start | bytes 589832 | tf_op jit(solution)/shard_map/ppermute | solution.py:321
  46.0 9.6 %collective-permute-start.7 = (f32[2,2,4,1,24,128]{5,4,3,2,1,0:T(8,128)S(1)}, f32[2,2,4,1,24,128]{5,4,3,2,1,0:T(8,128)S(1)}, u32[]{:S(2)}, u32[]{:S(2)}) collective-permute-start(f32[2,2,4,1,24,128]{5,4,3,2,1,0:T(8,128)S(1)} %maximum_bitcast_fusion.1.refs_2_), channel_id=1, source_target_pairs={{0,1},{1,0},{2,3},{3,2},{4,5},{5,4},{6,7},{7,6},{8,9},{9,8},{10,11... | collective-permute-start | bytes 589832 | tf_op jit(solution)/shard_map/ppermute | solution.py:321
  55.0 8.1 %collective-permute-start.8 = (f32[2,3,4,1,24,128]{5,4,3,2,1,0:T(8,128)S(1)}, f32[2,3,4,1,24,128]{5,4,3,2,1,0:T(8,128)S(1)}, u32[]{:S(2)}, u32[]{:S(2)}) collective-permute-start(f32[2,3,4,1,24,128]{5,4,3,2,1,0:T(8,128)S(1)} %get-tuple-element.56), channel_id=1, source_target_pairs={{0,1},{1,0},{2,3},{3,2},{4,5},{5,4},{6,7},{7,6},{8,9},{9,8},{10,11... | collective-permute-start | bytes 884744 | tf_op jit(solution)/shard_map/ppermute | solution.py:321
  55.6 20.4 %copy-start.1 = (f32[192,4]{1,0:T(8,128)S(1)}, f32[192,4]{1,0:T(8,128)}, u32[]{:S(2)}) copy-start(f32[192,4]{1,0:T(8,128)} %constant.16.clone.refs_1_) | copy-start | bytes 9220
  60.8 10.8 %collective-permute-start.9 = (f32[2,3,4,1,24,128]{5,4,3,2,1,0:T(8,128)S(1)}, f32[2,3,4,1,24,128]{5,4,3,2,1,0:T(8,128)S(1)}, u32[]{:S(2)}, u32[]{:S(2)}) collective-permute-start(f32[2,3,4,1,24,128]{5,4,3,2,1,0:T(8,128)S(1)} %get-tuple-element.58), channel_id=1, source_target_pairs={{0,1},{1,0},{2,3},{3,2},{4,5},{5,4},{6,7},{7,6},{8,9},{9,8},{10,11... | collective-permute-start | bytes 884744 | tf_op jit(solution)/shard_map/ppermute | solution.py:321
  63.1 13.6 %collective-permute-start.10 = (f32[1,3,4,1,24,128]{5,4,3,2,1,0:T(8,128)S(1)}, f32[1,3,4,1,24,128]{5,4,3,2,1,0:T(8,128)S(1)}, u32[]{:S(2)}, u32[]{:S(2)}) collective-permute-start(f32[1,3,4,1,24,128]{5,4,3,2,1,0:T(8,128)S(1)} %get-tuple-element.60), channel_id=1, source_target_pairs={{0,2},{1,3},{2,0},{3,1},{4,6},{5,7},{6,4},{7,5},{8,10},{9,11},{10,... | collective-permute-start | bytes 442376 | tf_op jit(solution)/shard_map/ppermute | solution.py:321
  63.6 1.2 %collective-permute-start.11 = (f32[2,4,2,4,128]{4,3,2,1,0:T(4,128)S(1)}, f32[2,4,2,4,128]{4,3,2,1,0:T(4,128)S(1)}, u32[]{:S(2)}, u32[]{:S(2)}) collective-permute-start(f32[2,4,2,4,128]{4,3,2,1,0:T(4,128)S(1)} %get-tuple-element.61), channel_id=1, source_target_pairs={{0,4},{4,0},{8,12},{12,8},{16,20},{20,16},{24,28},{28,24},{1,5},{5... | collective-permute-start | bytes 98312 | tf_op jit(solution)/shard_map/ppermute | solution.py:321
  64.8 7.2 %collective-permute-start.12 = (f32[2,4,2,4,128]{4,3,2,1,0:T(4,128)S(1)}, f32[2,4,2,4,128]{4,3,2,1,0:T(4,128)S(1)}, u32[]{:S(2)}, u32[]{:S(2)}) collective-permute-start(f32[2,4,2,4,128]{4,3,2,1,0:T(4,128)S(1)} %add.18), channel_id=1, source_target_pairs={{0,8},{4,12},{8,0},{12,4},{16,24},{20,28},{24,16},{28,20},{1,9},{5... | collective-permute-start | bytes 98312 | tf_op jit(solution)/shard_map/ppermute | solution.py:321
  71.6 10.8 %collective-permute-start.16 = (f32[1,3,4,1,24,128]{5,4,3,2,1,0:T(8,128)S(1)}, f32[1,3,4,1,24,128]{5,4,3,2,1,0:T(8,128)S(1)}, u32[]{:S(2)}, u32[]{:S(2)}) collective-permute-start(f32[1,3,4,1,24,128]{5,4,3,2,1,0:T(8,128)S(1)} %get-tuple-element.66), channel_id=1, source_target_pairs={{0,2},{1,3},{2,0},{3,1},{4,6},{5,7},{6,4},{7,5},{8,10},{9,11},{10,... | collective-permute-start | bytes 442376 | tf_op jit(solution)/shard_map/ppermute | solution.py:321
  72.0 4.0 %collective-permute-start.13 = (f32[2,4,2,4,128]{4,3,2,1,0:T(4,128)S(1)}, f32[2,4,2,4,128]{4,3,2,1,0:T(4,128)S(1)}, u32[]{:S(2)}, u32[]{:S(2)}) collective-permute-start(f32[2,4,2,4,128]{4,3,2,1,0:T(4,128)S(1)} %add.19), channel_id=1, source_target_pairs={{0,16},{4,20},{8,24},{12,28},{16,0},{20,4},{24,8},{28,12},{1,17},{... | collective-permute-start | bytes 98312 | tf_op jit(solution)/shard_map/ppermute | solution.py:321
  77.4 7.5 %collective-permute-start.14 = (f32[1,2,4,1,24,128]{5,4,2,1,3,0:T(8,128)S(1)}, f32[1,2,4,1,24,128]{5,4,2,1,3,0:T(8,128)S(1)}, u32[]{:S(2)}, u32[]{:S(2)}) collective-permute-start(f32[1,2,4,1,24,128]{5,4,2,1,3,0:T(8,128)S(1)} %bitcast.26), channel_id=1, source_target_pairs={{0,2},{1,3},{2,0},{3,1},{4,6},{5,7},{6,4},{7,5},{8,10},{9,11},{10,... | collective-permute-start | bytes 294920 | tf_op jit(solution)/shard_map/ppermute | solution.py:321
  83.1 5.9 %collective-permute-start.17 = (f32[1,2,4,1,24,128]{5,4,2,1,3,0:T(8,128)S(1)}, f32[1,2,4,1,24,128]{5,4,2,1,3,0:T(8,128)S(1)}, u32[]{:S(2)}, u32[]{:S(2)}) collective-permute-start(f32[1,2,4,1,24,128]{5,4,2,1,3,0:T(8,128)S(1)} %bitcast.28), channel_id=1, source_target_pairs={{0,2},{1,3},{2,0},{3,1},{4,6},{5,7},{6,4},{7,5},{8,10},{9,11},{10,... | collective-permute-start | bytes 294920 | tf_op jit(solution)/shard_map/ppermute | solution.py:321
  84.9 14.8 %collective-permute-start.15 = (f32[2,2,4,1,24,128]{5,4,3,2,1,0:T(8,128)S(1)}, f32[2,2,4,1,24,128]{5,4,3,2,1,0:T(8,128)S(1)}, u32[]{:S(2)}, u32[]{:S(2)}) collective-permute-start(f32[2,2,4,1,24,128]{5,4,3,2,1,0:T(8,128)S(1)} %maximum_bitcast_fusion.2.refs_1_), channel_id=1, source_target_pairs={{0,1},{1,0},{2,3},{3,2},{4,5},{5,4},{6,7},{7,6},{8,9},{9,8},{10,11... | collective-permute-start | bytes 589832 | tf_op jit(solution)/shard_map/ppermute | solution.py:321
  89.0 10.8 %collective-permute-start.18 = (f32[2,2,4,1,24,128]{5,4,3,2,1,0:T(8,128)S(1)}, f32[2,2,4,1,24,128]{5,4,3,2,1,0:T(8,128)S(1)}, u32[]{:S(2)}, u32[]{:S(2)}) collective-permute-start(f32[2,2,4,1,24,128]{5,4,3,2,1,0:T(8,128)S(1)} %maximum_bitcast_fusion.3.refs_3_), channel_id=1, source_target_pairs={{0,1},{1,0},{2,3},{3,2},{4,5},{5,4},{6,7},{7,6},{8,9},{9,8},{10,11... | collective-permute-start | bytes 589832 | tf_op jit(solution)/shard_map/ppermute | solution.py:321
  89.1 1.3 %collective-permute-start.19 = (f32[2,4,2,4,128]{4,3,2,1,0:T(4,128)S(1)}, f32[2,4,2,4,128]{4,3,2,1,0:T(4,128)S(1)}, u32[]{:S(2)}, u32[]{:S(2)}) collective-permute-start(f32[2,4,2,4,128]{4,3,2,1,0:T(4,128)S(1)} %get-tuple-element.68), channel_id=1, source_target_pairs={{0,4},{4,0},{8,12},{12,8},{16,20},{20,16},{24,28},{28,24},{1,5},{5... | collective-permute-start | bytes 98312 | tf_op jit(solution)/shard_map/ppermute | solution.py:321
  90.3 4.0 %collective-permute-start.20 = (f32[2,4,2,4,128]{4,3,2,1,0:T(4,128)S(1)}, f32[2,4,2,4,128]{4,3,2,1,0:T(4,128)S(1)}, u32[]{:S(2)}, u32[]{:S(2)}) collective-permute-start(f32[2,4,2,4,128]{4,3,2,1,0:T(4,128)S(1)} %add.21), channel_id=1, source_target_pairs={{0,8},{4,12},{8,0},{12,4},{16,24},{20,28},{24,16},{28,20},{1,9},{5... | collective-permute-start | bytes 98312 | tf_op jit(solution)/shard_map/ppermute | solution.py:321
  94.3 4.0 %collective-permute-start.21 = (f32[2,4,2,4,128]{4,3,2,1,0:T(4,128)S(1)}, f32[2,4,2,4,128]{4,3,2,1,0:T(4,128)S(1)}, u32[]{:S(2)}, u32[]{:S(2)}) collective-permute-start(f32[2,4,2,4,128]{4,3,2,1,0:T(4,128)S(1)} %add.22), channel_id=1, source_target_pairs={{0,16},{4,20},{8,24},{12,28},{16,0},{20,4},{24,8},{28,12},{1,17},{... | collective-permute-start | bytes 98312 | tf_op jit(solution)/shard_map/ppermute | solution.py:321

commit v4 on v3

--- a/solution.py
+++ b/solution.py
@@ -13,11 +13,8 @@
 ITERS = 2
 LANES = 128
 SUBLANES = 8
-DIRECT_SUM = False
-EARLY = False
-STEP_BEFORE = 99
-DIRECT_SPREAD = (False, False)
-CHUNKING = "times"
+JOIN_AFTER = ((0, 0), (1, 2))
+ADD_AFTER = 2
 ROWS_BY_COLS = (((1,), (0,)), ((), ()))
 ROWS_BY_ROWS = (((1,), (1,)), ((), ()))
 VMEM = pltpu.MemorySpace.VMEM
@@ -57,8 +54,6 @@
 
 
 def chunks_of(times, chans):
-    if CHUNKING == "channels" and chans % SUBLANES == 0:
-        return [(0, times, f, f + SUBLANES) for f in range(0, chans, SUBLANES)]
     return [(t, t + 1, 0, chans) for t in range(times)]
 
 
@@ -72,7 +67,7 @@
     place_ref = refs.pop(0)
     gain_refs = [refs.pop(0) for _ in range(sources)]
     vis_ref, coh_ref, pick_ref = [refs.pop(0) for _ in range(3)]
-    outs = [refs.pop(0) for _ in range(line if DIRECT_SUM else 2)]
+    outs = [refs.pop(0) for _ in range(2)]
     own_ref = refs.pop(0) if start else None
     dirs, links = coh_ref.shape[1], coh_ref.shape[4]
     rows = (t1 - t0) * (f1 - f0)
@@ -93,9 +88,9 @@
         for copy in copies:
             copy.start()
         copies[0].wait()
-        build_picks(line, share, offsets, station_ref, pick_ref)
         for t in range(t0, t1):
             copies[1 + 3 * t].wait()
+        build_picks(line, share, offsets, station_ref, pick_ref)
     if start:
         if share % LANES:
             offsets = [r * share for r in range(line)]
@@ -107,10 +102,10 @@
         blocks = [block_of(gain_refs, r) for r in range(line)]
     blocks = [block.reshape(2 * dirs * rows, share) for block in blocks]
     dot = functools.partial(lax.dot_general, preferred_element_type=jnp.float32)
-    upper, lower = split(jnp.concatenate(blocks, axis=1))
-    first, second = [
-        dot(upper, pick_ref[end], ROWS_BY_COLS) + dot(lower, pick_ref[end], ROWS_BY_COLS) for end in range(2)
-    ]
+    both = jnp.concatenate(split(jnp.concatenate(blocks, axis=1)), axis=0)
+    wide = [dot(both, pick_ref[end], ROWS_BY_COLS) for end in range(2)]
+    height = 2 * dirs * rows
+    first, second = [values[:height] + values[height:] for values in wide]
 
     def row(values, part, k):
         begin = (part * dirs + k) * rows
@@ -146,17 +141,15 @@
     terms[1] += [rest_real * c + rest_imag * d for _, _, c, d in sides]
     terms[1] += [rest_real * d - rest_imag * c for _, _, c, d in sides]
     terms[1] += [c * c + d * d for _, _, c, d in sides]
+    pieces = [split(jnp.concatenate(terms[end], axis=0)) for end in range(2)]
+    wide = jnp.concatenate([pick_ref[0], pick_ref[1]], axis=1)
     total = None
-    for end in range(2):
-        for piece in split(jnp.concatenate(terms[end], axis=0)):
-            value = dot(piece, pick_ref[end], ROWS_BY_ROWS)
-            total = value if total is None else total + value
+    for part in range(2):
+        value = dot(jnp.concatenate([pieces[0][part], pieces[1][part]], axis=1), wide, ROWS_BY_ROWS)
+        total = value if total is None else total + value
     for r in range(line):
         piece = total[:, r * share : (r + 1) * share].reshape(3, dirs, t1 - t0, f1 - f0, share)
-        if DIRECT_SUM:
-            outs[r][0] = piece
-        else:
-            outs[r % 2][r // 2] = piece
+        outs[r % 2][r // 2] = piece
     for t in range(vis_ref.shape[1] if fill else 0):
         if not t0 <= t < t1:
             for copy in copies[1 + 3 * t : 4 + 3 * t]:
@@ -192,8 +185,7 @@
     count = gains[0].shape[-1] if start else gains[0].shape[-1] * line
     share = count // line
     piece = (dirs, t1 - t0, f1 - f0, share)
-    lead = [1] * line if DIRECT_SUM else [line // 2] * 2
-    shapes = [jax.ShapeDtypeStruct((n, 3) + piece, jnp.float32) for n in lead]
+    shapes = [jax.ShapeDtypeStruct((line // 2, 3) + piece, jnp.float32)] * 2
     scratch = []
     if start:
         shapes.append(jax.ShapeDtypeStruct((2,) + piece, jnp.float32))
@@ -219,6 +211,17 @@
 def add_parts(keep, got, token):
     shape = jax.ShapeDtypeStruct((keep.shape[0] // 2,) + keep.shape[1:], keep.dtype)
     return run(add_kernel, token, [WHOLE] * 2, [shape] * 2, [keep, got])
+
+
+def join_kernel(blocks_ref, got_ref, out_ref):
+    for i in range(blocks_ref.shape[0]):
+        out_ref[2 * i] = blocks_ref[i]
+        out_ref[2 * i + 1] = got_ref[i]
+
+
+def join(blocks, got, token):
+    shape = jax.ShapeDtypeStruct((2 * blocks.shape[0],) + blocks.shape[1:], blocks.dtype)
+    return run(join_kernel, token, [WHOLE] * 2, [shape], [blocks, got])[0]
 
 
 def update_kernel(chunk, parts, first, chans, penalty_ref, place_ref, basis_ref, before_ref, *refs):
@@ -283,13 +286,14 @@
     return run(kernel, token, [SCALARS] + [WHOLE] * len(operands), shapes, [place, *operands])
 
 
-def assemble_kernel(chunks, line, share, place_ref, *refs):
+def assemble_kernel(chunks, sizes, line, share, place_ref, *refs):
     out_ref = refs[-1]
-    each = (len(refs) - 1) // len(chunks)
-    for i, (t0, t1, f0, f1) in enumerate(chunks):
+    refs = list(refs)
+    for size, (t0, t1, f0, f1) in zip(sizes, chunks):
+        blocks = [refs.pop(0) for _ in range(size)]
         for r in range(line):
             offset = pl.multiple_of((place_ref[0] ^ r) * share, LANES)
-            out_ref[:, :, t0:t1, f0:f1, pl.ds(offset, share)] = block_of(refs[i * each : (i + 1) * each], r)
+            out_ref[:, :, t0:t1, f0:f1, pl.ds(offset, share)] = block_of(blocks, r)
 
 
 def assemble(chunks, line, place, gains, dims):
@@ -302,7 +306,7 @@
             whole = whole.at[:, :, t0:t1, f0:f1].set(jnp.concatenate(parts, axis=-1))
         return whole
     flat = [block for blocks in gains for block in blocks]
-    kernel = functools.partial(assemble_kernel, chunks, line, share)
+    kernel = functools.partial(assemble_kernel, chunks, [len(blocks) for blocks in gains], line, share)
     shapes = [jax.ShapeDtypeStruct(dims, jnp.float32)]
     return run(kernel, [], [SCALARS] + [WHOLE] * len(flat), shapes, [place, *flat])[0]
 
@@ -337,74 +341,64 @@
     token = []
     gains = own = targets = duals = projected = None
 
-    def spread(values, direct):
-        blocks, bit, arrived = values[None], line // 2, None
-        if direct:
-            blocks = [blocks] + [swap(blocks, "bl", line, r) for r in range(1, line)]
-            return blocks, blocks[1]
-        while bit > 1:
-            got = swap(blocks, "bl", line, bit)
-            arrived = got if arrived is None else arrived
-            blocks = jnp.stack([blocks, got], axis=1).reshape((2 * blocks.shape[0],) + blocks.shape[1:])
-            bit //= 2
-        return [blocks, swap(blocks, "bl", line, 1)], arrived
-
+    direct_order = list(range(1, line))
+    zeros = jnp.zeros((times, POLY, 2, dirs, share), jnp.float32)
     for iteration in range(ITERS):
         first = iteration == 0
         parts, fresh = [], []
         if not first:
             picks = make_picks(line, count, place, stations, token)
             token = [picks]
-            steps = chan_steps(projected)
         for c, chunk in enumerate(chunks):
             fill = first and c == 0
-            if not first and c + STEP_BEFORE < len(steps):
-                token = token + [steps[c + STEP_BEFORE]]
-            out = normals(
-                chunk,
-                line,
-                first,
-                fill,
-                place,
-                [ordered] if first else gains[c],
-                visibilities,
-                coherencies,
-                stations if fill else picks,
-                token,
-            )
+            source = [ordered] if first else gains[c]
+            ends = stations if fill else picks
+            out = normals(chunk, line, first, fill, place, source, visibilities, coherencies, ends, token)
             token = [out[0]]
-            count_sent = line if DIRECT_SUM else 2
-            if DIRECT_SUM:
-                parts.append([out[0]] + [swap(out[r], "bl", line, r) for r in range(1, line)])
-            else:
-                parts.append([out[0], swap(out[1], "bl", line, 1)])
-            rest = list(out[count_sent:])
+            parts.append([out[0], swap(out[1], "bl", line, 1)])
+            rest = list(out[2:])
             if first:
                 fresh.append(rest.pop(0))
             if fill:
                 picks, ordered, visibilities, coherencies = rest
         if first:
             own = fresh
-        else:
-            targets, duals = smooth(chunks, True, place, solved, steps[-1], own, [], own_dims, [])
         bit = 2
-        while bit < line and not DIRECT_SUM:
+        while bit < line:
             for c in range(len(chunks)):
-                keep, send = add_parts(*parts[c], token)
+                waits = [steps[ADD_AFTER]] if ADD_AFTER and c and not first else []
+                keep, send = add_parts(*parts[c], token + waits)
                 parts[c] = [keep, swap(send, "bl", line, bit)]
                 token = [keep]
             bit *= 2
-        gains, fresh = [], []
-        projected = jnp.zeros((times, POLY, 2, dirs, share), jnp.float32)
+        fresh, arrived = [], []
+        projected = zeros
         for c, chunk in enumerate(chunks):
             extra = [own[c]] if first else [own[c], targets, duals]
             new, projected = update(chunk, first, chans, penalty, place, basis, projected, parts[c], extra, token)
-            pair, arrived = spread(new, DIRECT_SPREAD[iteration])
-            token = [new] if first or not EARLY else [new, arrived]
-            gains.append(pair)
+            token = [new]
             fresh.append(new)
+            direct = not first and c == len(chunks) - 1
+            arrived.append([swap(new[None], "bl", line, r) for r in (direct_order if direct else [line // 2])])
         own = fresh
-    steps = chan_steps(projected)
+        steps = chan_steps(projected)
+        gains = []
+        for c in range(len(chunks)):
+            blocks, got, bit = own[c][None], arrived[c][0], line // 2
+            if len(arrived[c]) > 1:
+                gains.append([blocks] + [arrived[c][direct_order.index(r)] for r in range(1, line)])
+                continue
+            after = JOIN_AFTER[iteration][min(c, 1)]
+            while bit > 1:
+                if after:
+                    blocks = join(blocks, got, [steps[after]])
+                else:
+                    blocks = jnp.stack([blocks, got], axis=1).reshape((2 * blocks.shape[0],) + blocks.shape[1:])
+                bit //= 2
+                got = swap(blocks, "bl", line, bit)
+            gains.append([blocks, got])
+        if first:
+            targets, duals = smooth(chunks, True, place, solved, steps[-1], own, [], own_dims, [])
     consensus, dual = smooth(chunks, False, place, solved, steps[-1], own, [duals], own_dims, [])
     return assemble(chunks, line, place, gains, dims), consensus, dual
 

time: 102 us -> 99.9 us (0.979)
  waiting for transfers between devices: 44.7 us -> 39.7 us
  starting transfers between devices: 25.3 us -> 29.4 us
    ppermute x22 -> x23, waiting for transfers between devices: 44.7 us -> 39.7 us  [swap(): return lax.ppermute(values, axis, [(i, i ^ bit) for i in range(size)])]
    ppermute x22 -> x23, starting transfers between devices: 25.3 us -> 29.4 us  [swap(): return lax.ppermute(values, axis, [(i, i ^ bit) for i in range(size)])]
    pallas_call x16 -> x17, Pallas kernels: 30.2 us -> 29.5 us  [run(): pl.pallas_call(lambda *refs: kernel(*refs[count:]), in_specs=[OUTSIDE] *...]
  transfers between devices with their start and end apart: 22 -> 23, of which waited for: 16 -> 14; matrix products, arithmetic and copies ran while one was open for 0% -> 0% of each run, Pallas kernels for 22% -> 21%
where the time goes in v4:
time: 99.9 us; the launch traced here: 99.7 us
  waiting for transfers between devices  39.7 us (40%)
  Pallas kernels  29.5 us (30%)
  starting transfers between devices  29.4 us (29%)
    ppermute x23, waiting for transfers between devices, swap(): return lax.ppermute(values, axis, [(i, i ^ bit) for i in range(size)])  39.7 us
    pallas_call x17, Pallas kernels, run(): pl.pallas_call(lambda *refs: kernel(*refs[count:]), in_specs=[OUTSIDE] *...  29.5 us
    ppermute x23, starting transfers between devices, swap(): return lax.ppermute(values, axis, [(i, i ^ bit) for i in range(size)])  29.4 us
  transfers between devices with their start and end apart: 23, of which 14 were waited for; matrix products, arithmetic and copies ran while one was open for 0% of the time, Pallas kernels for 21%

profile of v4, /device:TPU:0, one launch (start us, length us, event | category | flops | bytes accessed | tf_op | source)
XLA Modules:
  0.0 99.7 jit_solution(6221032105016344898)
XLA Ops:
  0.6 0.1 pad_add_fusion.refs_0_.refs_1_.refs_2_
  0.7 6.9 %shard_map.94 = (f32[2,3,4,1,24,128]{5,4,3,2,1,0:T(8,128)S(1)}, f32[2,3,4,1,24,128]{5,4,3,2,1,0:T(8,128)S(1)}, f32[2,4,1,24,128]{4,3,2,1,0:T(8,128)S(1)}, bf16[2...) custom-call(s32[2]{0:T(128)S(1)} %pad_add_fusion.refs_0_.refs_1_.ref, ...), custom_call_target="tpu_custom_call" | custom-call | flops 1048576 | bytes 1024 | tf_op jit(solution)/shard_map/pallas_call | solution.py:30
  7.6 3.1 %collective-permute-start = (f32[2,3,4,1,24,128]{5,4,3,2,1,0:T(8,128)S(1)}, f32[2,3,4,1,24,128]{5,4,3,2,1,0:T(8,128)S(1)}, u32[]{:S(2)}, u32[]{:S(2)}) collective-permute-start(f32[2,3,4,1,24,128]{5,4,3,2,1,0:T(8,128)S(1)} %get-tuple-element.43), channel_id=1, source_target_pairs={{0,1},{1,0},{2,3},{3,2},{4,5},{5,4},{6,7},{7,6},{8,9},{9,8},{10,11... | collective-permute-start | bytes 884744 | tf_op jit(solution)/shard_map/ppermute | solution.py:325
  10.7 5.0 %shard_map.95 = (f32[2,3,4,1,24,128]{5,4,3,2,1,0:T(8,128)S(1)}, f32[2,3,4,1,24,128]{5,4,3,2,1,0:T(8,128)S(1)}, f32[2,4,1,24,128]{4,3,2,1,0:T(8,128)S(1)}) custom-call(f32[2,3,4,1,24,128]{5,4,3,2,1,0:T(8,128)S(1)} %get-tuple-element.37.refs_0_.refs_1_, s32[2]{0:T(128)S(1)} %pad_add_fusion.refs_0_.refs_1_.refs_2_, ...), custom_call_target="tpu_custom_call" | custom-call | flops 1048576 | bytes 1024 | tf_op jit(solution)/shard_map/pallas_call | solution.py:30
  15.7 0.1 collective-permute-start.1
  15.8 2.3 %collective-permute-done.refs_2_ = f32[2,3,4,1,24,128]{5,4,3,2,1,0:T(8,128)S(1)} collective-permute-done((f32[2,3,4,1,24,128]{5,4,3,2,1,0:T(8,128)S(1)}, f32[2,3,4,1,24,128]{5,4,3,2,1,0:T(8,128)S(1)}, u32[]{:S(2)}, u32[]{:S(2)}) %collective-permute-start) | collective-permute-done | bytes 294944 | tf_op jit(solution)/shard_map/ppermute | solution.py:325
  18.1 2.5 %collective-permute-start.2 = (f32[1,3,4,1,24,128]{5,4,3,2,1,0:T(8,128)S(1)}, f32[1,3,4,1,24,128]{5,4,3,2,1,0:T(8,128)S(1)}, u32[]{:S(2)}, u32[]{:S(2)}) collective-permute-start(f32[1,3,4,1,24,128]{5,4,3,2,1,0:T(8,128)S(1)} %get-tuple-element.47), channel_id=1, source_target_pairs={{0,2},{1,3},{2,0},{3,1},{4,6},{5,7},{6,4},{7,5},{8,10},{9,11},{10,... | collective-permute-start | bytes 442376 | tf_op jit(solution)/shard_map/ppermute | solution.py:325
  20.6 6.7 %collective-permute-done.1.refs_2_ = f32[2,3,4,1,24,128]{5,4,3,2,1,0:T(8,128)S(1)} collective-permute-done((f32[2,3,4,1,24,128]{5,4,3,2,1,0:T(8,128)S(1)}, f32[2,3,4,1,24,128]{5,4,3,2,1,0:T(8,128)S(1)}, u32[]{:S(2)}, u32[]{:S(2)}) %collective-permute-start.1) | collective-permute-done | bytes 294944 | tf_op jit(solution)/shard_map/ppermute | solution.py:325
  27.4 1.1 %collective-permute-start.3 = (f32[1,3,4,1,24,128]{5,4,3,2,1,0:T(8,128)S(1)}, f32[1,3,4,1,24,128]{5,4,3,2,1,0:T(8,128)S(1)}, u32[]{:S(2)}, u32[]{:S(2)}) collective-permute-start(f32[1,3,4,1,24,128]{5,4,3,2,1,0:T(8,128)S(1)} %get-tuple-element.51), channel_id=1, source_target_pairs={{0,2},{1,3},{2,0},{3,1},{4,6},{5,7},{6,4},{7,5},{8,10},{9,11},{10,... | collective-permute-start | bytes 442376 | tf_op jit(solution)/shard_map/ppermute | solution.py:325
  28.5 0.7 shard_map.98
  29.2 2.0 %collective-permute-start.4 = (f32[1,2,4,1,24,128]{5,4,2,1,3,0:T(8,128)S(1)}, f32[1,2,4,1,24,128]{5,4,2,1,3,0:T(8,128)S(1)}, u32[]{:S(2)}, u32[]{:S(2)}) collective-permute-start(f32[1,2,4,1,24,128]{5,4,2,1,3,0:T(8,128)S(1)} %bitcast.14), channel_id=1, source_target_pairs={{0,2},{1,3},{2,0},{3,1},{4,6},{5,7},{6,4},{7,5},{8,10},{9,11},{10,... | collective-permute-start | bytes 294920 | tf_op jit(solution)/shard_map/ppermute | solution.py:325
  31.2 7.7 %collective-permute-done.3.refs_6_ = f32[1,3,4,1,24,128]{5,4,3,2,1,0:T(8,128)S(1)} collective-permute-done((f32[1,3,4,1,24,128]{5,4,3,2,1,0:T(8,128)S(1)}, f32[1,3,4,1,24,128]{5,4,3,2,1,0:T(8,128)S(1)}, u32[]{:S(2)}, u32[]{:S(2)}) %collective-permute-start.3) | collective-permute-done | bytes 147488 | tf_op jit(solution)/shard_map/ppermute | solution.py:325
  38.9 0.7 shard_map.99
  39.6 0.1 collective-permute-start.6
  39.7 0.5 collective-permute-done.4
  40.2 2.0 %collective-permute-start.5 = (f32[2,2,4,1,24,128]{5,4,3,2,1,0:T(8,128)S(1)}, f32[2,2,4,1,24,128]{5,4,3,2,1,0:T(8,128)S(1)}, u32[]{:S(2)}, u32[]{:S(2)}) collective-permute-start(f32[2,2,4,1,24,128]{5,4,3,2,1,0:T(8,128)S(1)} %maximum_bitcast_fusion.refs_2_), channel_id=1, source_target_pairs={{0,1},{1,0},{2,3},{3,2},{4,5},{5,4},{6,7},{7,6},{8,9},{9,8},{10,11... | collective-permute-start | bytes 589832 | tf_op jit(solution)/shard_map/ppermute | solution.py:325
  42.1 3.6 %collective-permute-done.6 = f32[1,2,4,1,24,128]{5,4,2,1,3,0:T(8,128)S(1)} collective-permute-done((f32[1,2,4,1,24,128]{5,4,2,1,3,0:T(8,128)S(1)}, f32[1,2,4,1,24,128]{5,4,2,1,3,0:T(8,128)S(1)}, u32[]{:S(2)}, u32[]{:S(2)}) %collective-permute-start.6) | collective-permute-done | bytes 98336 | tf_op jit(solution)/shard_map/ppermute | solution.py:325
  45.8 0.1 collective-permute-start.7
  45.8 1.1 %shard_map.100.refs_0_.refs_6_ = bf16[2,512,2048]{2,1,0:T(8,128)(2,1)S(1)} custom-call(f32[2,4,1,24,128]{4,3,2,1,0:T(8,128)S(1)} %get-tuple-element.53.refs_0_.refs_4_.refs_7_, s32[2]{0:T(128)S(1)} %pad_add_fusion.refs_0_.refs_1_.refs_2_, s32[2,2048]{1,0:T(2,128)S(1)} %copy-done.2), custom_call_target="tpu_custom_call" | custom-call | flops 1048576 | bytes 1024 | tf_op jit(solution)/shard_map/pallas_call | solution.py:30
  46.9 2.4 %collective-permute-done.5.refs_3_ = f32[2,2,4,1,24,128]{5,4,3,2,1,0:T(8,128)S(1)} collective-permute-done((f32[2,2,4,1,24,128]{5,4,3,2,1,0:T(8,128)S(1)}, f32[2,2,4,1,24,128]{5,4,3,2,1,0:T(8,128)S(1)}, u32[]{:S(2)}, u32[]{:S(2)}) %collective-permute-start.5) | collective-permute-done | bytes 196640 | tf_op jit(solution)/shard_map/ppermute | solution.py:325
  49.3 5.2 %shard_map.101 = (f32[2,3,4,1,24,128]{5,4,3,2,1,0:T(8,128)S(1)}, f32[2,3,4,1,24,128]{5,4,3,2,1,0:T(8,128)S(1)}) custom-call(bf16[2,512,2048]{2,1,0:T(8,128)(2,1)S(1)} %shard_map.100.refs_0_.refs_6_, s32[2]{0:T(128)S(1)} %pad_add_fusion.refs_0_.refs_1_.refs_2_, f32[2,2,4,1,24,128]{5,4,3,2,1,0:T(8,128)S(1)} %maximum_bitcast_fusion.refs_2_, ...), custom_call_target="tpu_custom_call" | custom-call | flops 1048576 | bytes 1024 | tf_op jit(solution)/shard_map/pallas_call | solution.py:30
  54.5 0.8 collective-permute-start.8
  55.2 5.0 %shard_map.102 = (f32[2,3,4,1,24,128]{5,4,3,2,1,0:T(8,128)S(1)}, f32[2,3,4,1,24,128]{5,4,3,2,1,0:T(8,128)S(1)}) custom-call(f32[2,3,4,1,24,128]{5,4,3,2,1,0:T(8,128)S(1)} %get-tuple-element.54.refs_0_.refs_1_, s32[2]{0:T(128)S(1)} %pad_add_fusion.refs_0_.refs_1_.refs_2_, f32[2,2,4,1,24,128]{5,4,3,2,1,0:T(8,128)S(1)} %maximum_bitcast_fusion.1.refs_2_, ...), custom_call_target="tpu_custom_call" | custom-call | flops 1048576 | bytes 1024 | tf_op jit(solution)/shard_map/pallas_call | solution.py:30
  60.2 1.4 %collective-permute-start.11 = (f32[2,3,4,1,24,128]{5,4,3,2,1,0:T(8,128)S(1)}, f32[2,3,4,1,24,128]{5,4,3,2,1,0:T(8,128)S(1)}, u32[]{:S(2)}, u32[]{:S(2)}) collective-permute-start(f32[2,3,4,1,24,128]{5,4,3,2,1,0:T(8,128)S(1)} %get-tuple-element.59), channel_id=1, source_target_pairs={{0,1},{1,0},{2,3},{3,2},{4,5},{5,4},{6,7},{7,6},{8,9},{9,8},{10,11... | collective-permute-start | bytes 884744 | tf_op jit(solution)/shard_map/ppermute | solution.py:325
  61.6 1.2 %collective-permute-done.8.refs_2_ = f32[2,3,4,1,24,128]{5,4,3,2,1,0:T(8,128)S(1)} collective-permute-done((f32[2,3,4,1,24,128]{5,4,3,2,1,0:T(8,128)S(1)}, f32[2,3,4,1,24,128]{5,4,3,2,1,0:T(8,128)S(1)}, u32[]{:S(2)}, u32[]{:S(2)}) %collective-permute-start.8) | collective-permute-done | bytes 294944 | tf_op jit(solution)/shard_map/ppermute | solution.py:325
  62.9 0.3 collective-permute-start.12
  63.2 1.5 %collective-permute-start.10 = (f32[2,4,2,4,128]{4,3,2,1,0:T(4,128)S(1)}, f32[2,4,2,4,128]{4,3,2,1,0:T(4,128)S(1)}, u32[]{:S(2)}, u32[]{:S(2)}) collective-permute-start(f32[2,4,2,4,128]{4,3,2,1,0:T(4,128)S(1)} %add.18), channel_id=1, source_target_pairs={{0,8},{4,12},{8,0},{12,4},{16,24},{20,28},{24,16},{28,20},{1,9},{5... | collective-permute-start | bytes 98312 | tf_op jit(solution)/shard_map/ppermute | solution.py:325
  64.7 2.5 %collective-permute-done.10 = f32[2,4,2,4,128]{4,3,2,1,0:T(4,128)S(1)} collective-permute-done((f32[2,4,2,4,128]{4,3,2,1,0:T(4,128)S(1)}, f32[2,4,2,4,128]{4,3,2,1,0:T(4,128)S(1)}, u32[]{:S(2)}, u32[]{:S(2)}) %collective-permute-start.10) | collective-permute-done | bytes 32800 | tf_op jit(solution)/shard_map/ppermute | solution.py:325
  67.2 3.8 %collective-permute-done.11.refs_3_ = f32[2,3,4,1,24,128]{5,4,3,2,1,0:T(8,128)S(1)} collective-permute-done((f32[2,3,4,1,24,128]{5,4,3,2,1,0:T(8,128)S(1)}, f32[2,3,4,1,24,128]{5,4,3,2,1,0:T(8,128)S(1)}, u32[]{:S(2)}, u32[]{:S(2)}) %collective-permute-start.11) | collective-permute-done | bytes 294944 | tf_op jit(solution)/shard_map/ppermute | solution.py:325
  71.0 0.1 collective-permute-start.14
  71.1 1.7 %collective-permute-start.13 = (f32[2,4,2,4,128]{4,3,2,1,0:T(4,128)S(1)}, f32[2,4,2,4,128]{4,3,2,1,0:T(4,128)S(1)}, u32[]{:S(2)}, u32[]{:S(2)}) collective-permute-start(f32[2,4,2,4,128]{4,3,2,1,0:T(4,128)S(1)} %add.19.refs_1_), channel_id=1, source_target_pairs={{0,16},{4,20},{8,24},{12,28},{16,0},{20,4},{24,8},{28,12},{1,17},{... | collective-permute-start | bytes 98312 | tf_op jit(solution)/shard_map/ppermute | solution.py:325
  72.8 2.2 %collective-permute-done.13 = f32[2,4,2,4,128]{4,3,2,1,0:T(4,128)S(1)} collective-permute-done((f32[2,4,2,4,128]{4,3,2,1,0:T(4,128)S(1)}, f32[2,4,2,4,128]{4,3,2,1,0:T(4,128)S(1)}, u32[]{:S(2)}, u32[]{:S(2)}) %collective-permute-start.13) | collective-permute-done | bytes 32800 | tf_op jit(solution)/shard_map/ppermute | solution.py:325
  75.1 0.7 shard_map.105
  75.8 0.7 shard_map.106
  76.5 2.9 %collective-permute-start.16 = (f32[1,2,4,1,24,128]{5,4,3,2,1,0:T(8,128)S(1)}, f32[1,2,4,1,24,128]{5,4,3,2,1,0:T(8,128)S(1)}, u32[]{:S(2)}, u32[]{:S(2)}) collective-permute-start(f32[1,2,4,1,24,128]{5,4,3,2,1,0:T(8,128)S(1)} %bitcast.18), channel_id=1, source_target_pairs={{0,2},{1,3},{2,0},{3,1},{4,6},{5,7},{6,4},{7,5},{8,10},{9,11},{10,... | collective-permute-start | bytes 294920 | tf_op jit(solution)/shard_map/ppermute | solution.py:325
  79.4 1.1 %collective-permute-done.14.refs_6_ = f32[1,3,4,1,24,128]{5,4,3,2,1,0:T(8,128)S(1)} collective-permute-done((f32[1,3,4,1,24,128]{5,4,3,2,1,0:T(8,128)S(1)}, f32[1,3,4,1,24,128]{5,4,3,2,1,0:T(8,128)S(1)}, u32[]{:S(2)}, u32[]{:S(2)}) %collective-permute-start.14) | collective-permute-done | bytes 147488 | tf_op jit(solution)/shard_map/ppermute | solution.py:325
  80.5 0.7 shard_map.107
  81.2 1.2 %collective-permute-done.15 = f32[2,4,2,4,128]{4,3,2,1,0:T(4,128)S(1)} collective-permute-done((f32[2,4,2,4,128]{4,3,2,1,0:T(4,128)S(1)}, f32[2,4,2,4,128]{4,3,2,1,0:T(4,128)S(1)}, u32[]{:S(2)}, u32[]{:S(2)}) %collective-permute-start.15) | collective-permute-done | bytes 32800 | tf_op jit(solution)/shard_map/ppermute | solution.py:325
  82.5 1.9 %collective-permute-start.17 = (f32[2,2,4,1,24,128]{5,4,3,2,1,0:T(8,128)S(1)}, f32[2,2,4,1,24,128]{5,4,3,2,1,0:T(8,128)S(1)}, u32[]{:S(2)}, u32[]{:S(2)}) collective-permute-start(f32[2,2,4,1,24,128]{5,4,3,2,1,0:T(8,128)S(1)} %shard_map.108.refs_1_), channel_id=1, source_target_pairs={{0,1},{1,0},{2,3},{3,2},{4,5},{5,4},{6,7},{7,6},{8,9},{9,8},{10,11... | collective-permute-start | bytes 589832 | tf_op jit(solution)/shard_map/ppermute | solution.py:325
  84.4 0.1 collective-permute-start.18
  84.6 2.4 %collective-permute-start.19 = (f32[1,2,4,1,24,128]{5,4,3,2,1,0:T(8,128)S(1)}, f32[1,2,4,1,24,128]{5,4,3,2,1,0:T(8,128)S(1)}, u32[]{:S(2)}, u32[]{:S(2)}) collective-permute-start(f32[1,2,4,1,24,128]{5,4,3,2,1,0:T(8,128)S(1)} %bitcast.21), channel_id=1, source_target_pairs={{0,2},{1,3},{2,0},{3,1},{4,6},{5,7},{6,4},{7,5},{8,10},{9,11},{10,... | collective-permute-start | bytes 294920 | tf_op jit(solution)/shard_map/ppermute | solution.py:325
  87.0 1.8 %collective-permute-start.20 = (f32[1,2,4,1,24,128]{5,4,3,2,1,0:T(8,128)S(1)}, f32[1,2,4,1,24,128]{5,4,3,2,1,0:T(8,128)S(1)}, u32[]{:S(2)}, u32[]{:S(2)}) collective-permute-start(f32[1,2,4,1,24,128]{5,4,3,2,1,0:T(8,128)S(1)} %bitcast.22), channel_id=1, source_target_pairs={{0,3},{1,2},{2,1},{3,0},{4,7},{5,6},{6,5},{7,4},{8,11},{9,10},{10,... | collective-permute-start | bytes 294920 | tf_op jit(solution)/shard_map/ppermute | solution.py:325
  88.8 1.7 %collective-permute-start.21 = (f32[2,4,2,4,128]{4,3,2,1,0:T(4,128)S(1)}, f32[2,4,2,4,128]{4,3,2,1,0:T(4,128)S(1)}, u32[]{:S(2)}, u32[]{:S(2)}) collective-permute-start(f32[2,4,2,4,128]{4,3,2,1,0:T(4,128)S(1)} %add.21.refs_0_), channel_id=1, source_target_pairs={{0,8},{4,12},{8,0},{12,4},{16,24},{20,28},{24,16},{28,20},{1,9},{5... | collective-permute-start | bytes 98312 | tf_op jit(solution)/shard_map/ppermute | solution.py:325
  90.5 2.2 %collective-permute-done.21 = f32[2,4,2,4,128]{4,3,2,1,0:T(4,128)S(1)} collective-permute-done((f32[2,4,2,4,128]{4,3,2,1,0:T(4,128)S(1)}, f32[2,4,2,4,128]{4,3,2,1,0:T(4,128)S(1)}, u32[]{:S(2)}, u32[]{:S(2)}) %collective-permute-start.21) | collective-permute-done | bytes 32800 | tf_op jit(solution)/shard_map/ppermute | solution.py:325
  92.7 1.8 %collective-permute-start.22 = (f32[2,4,2,4,128]{4,3,2,1,0:T(4,128)S(1)}, f32[2,4,2,4,128]{4,3,2,1,0:T(4,128)S(1)}, u32[]{:S(2)}, u32[]{:S(2)}) collective-permute-start(f32[2,4,2,4,128]{4,3,2,1,0:T(4,128)S(1)} %add.22), channel_id=1, source_target_pairs={{0,16},{4,20},{8,24},{12,28},{16,0},{20,4},{24,8},{28,12},{1,17},{... | collective-permute-start | bytes 98312 | tf_op jit(solution)/shard_map/ppermute | solution.py:325
  94.5 2.2 %collective-permute-done.22 = f32[2,4,2,4,128]{4,3,2,1,0:T(4,128)S(1)} collective-permute-done((f32[2,4,2,4,128]{4,3,2,1,0:T(4,128)S(1)}, f32[2,4,2,4,128]{4,3,2,1,0:T(4,128)S(1)}, u32[]{:S(2)}, u32[]{:S(2)}) %collective-permute-start.22) | collective-permute-done | bytes 32800 | tf_op jit(solution)/shard_map/ppermute | solution.py:325
  96.7 1.4 %shard_map.110 = (f32[2,4,2,24,128]{4,3,2,1,0:T(8,128)}, f32[2,4,2,24,128]{4,3,2,1,0:T(8,128)}) custom-call(s32[2]{0:T(128)S(1)} %pad_add_fusion.refs_0_.refs_1_.refs_2_, f32[192,4]{1,0:T(8,128)S(1)} %copy-done.1, f32[2,4,2,4,128]{4,3,2,1,0:T(4,128)S(1)} %add.23.refs_2_, f32[2,4,1,24,128]{4,3,2,1,0:T(8,128)S(1)} %get-tuple-element.64.refs_0_.refs_3_, ...), custom_call_target="tpu_custom_call" | custom-call | flops 1048576 | bytes 1024 | tf_op jit(solution)/shard_map/pallas_call | solution.py:30
  98.2 1.5 %shard_map.109 = f32[2,4,2,24,512]{4,3,2,1,0:T(8,128)} custom-call(s32[2]{0:T(128)S(1)} %pad_add_fusion.refs_0_.refs_1_.refs_2_, f32[2,2,4,1,24,128]{5,4,3,2,1,0:T(8,128)S(1)} %shard_map.108.refs_1_, f32[2,2,4,1,24,128]{5,4,3,2,1,0:T(8,128)S(1)} %collective-permute-done.17.refs_2_, f32[1,2,4,1,24,128]{5,4,3,2,1,0:T(8,128)S(1)} %bitcast.23, ...), custom_call_target="tpu_custom_call" | custom-call | flops 1048576 | bytes 1024 | tf_op jit(solution)/shard_map/pallas_call | solution.py:30
  (33 shorter events, 0.3 us)
Async XLA Ops:
  7.6 10.5 %collective-permute-start = (f32[2,3,4,1,24,128]{5,4,3,2,1,0:T(8,128)S(1)}, f32[2,3,4,1,24,128]{5,4,3,2,1,0:T(8,128)S(1)}, u32[]{:S(2)}, u32[]{:S(2)}) collective-permute-start(f32[2,3,4,1,24,128]{5,4,3,2,1,0:T(8,128)S(1)} %get-tuple-element.43), channel_id=1, source_target_pairs={{0,1},{1,0},{2,3},{3,2},{4,5},{5,4},{6,7},{7,6},{8,9},{9,8},{10,11... | collective-permute-start | bytes 884744 | tf_op jit(solution)/shard_map/ppermute | solution.py:325
  10.7 17.8 %copy-start = (f32[192,4]{1,0:T(8,128)S(1)}, f32[192,4]{1,0:T(8,128)}, u32[]{:S(2)}) copy-start(f32[192,4]{1,0:T(8,128)} %constant.15.clone.refs_3_) | copy-start | bytes 9220
  10.7 17.8 %copy-start.3 = (f32[4]{0:T(128)S(1)}, f32[4]{0:T(128)}, u32[]{:S(2)}) copy-start(f32[4]{0:T(128)} %refs_1_.11) | copy-start | bytes 52
  10.7 35.2 %copy-start.2 = (s32[2,2048]{1,0:T(2,128)S(1)}, s32[2,2048]{1,0:T(2,128)}, u32[]{:S(2)}) copy-start(s32[2,2048]{1,0:T(2,128)} %refs_2_.3) | copy-start | bytes 49156
  15.7 11.7 %collective-permute-start.1 = (f32[2,3,4,1,24,128]{5,4,3,2,1,0:T(8,128)S(1)}, f32[2,3,4,1,24,128]{5,4,3,2,1,0:T(8,128)S(1)}, u32[]{:S(2)}, u32[]{:S(2)}) collective-permute-start(f32[2,3,4,1,24,128]{5,4,3,2,1,0:T(8,128)S(1)} %get-tuple-element.45), channel_id=1, source_target_pairs={{0,1},{1,0},{2,3},{3,2},{4,5},{5,4},{6,7},{7,6},{8,9},{9,8},{10,11... | collective-permute-start | bytes 884744 | tf_op jit(solution)/shard_map/ppermute | solution.py:325
  18.1 10.3 %collective-permute-start.2 = (f32[1,3,4,1,24,128]{5,4,3,2,1,0:T(8,128)S(1)}, f32[1,3,4,1,24,128]{5,4,3,2,1,0:T(8,128)S(1)}, u32[]{:S(2)}, u32[]{:S(2)}) collective-permute-start(f32[1,3,4,1,24,128]{5,4,3,2,1,0:T(8,128)S(1)} %get-tuple-element.47), channel_id=1, source_target_pairs={{0,2},{1,3},{2,0},{3,1},{4,6},{5,7},{6,4},{7,5},{8,10},{9,11},{10,... | collective-permute-start | bytes 442376 | tf_op jit(solution)/shard_map/ppermute | solution.py:325
  27.4 11.5 %collective-permute-start.3 = (f32[1,3,4,1,24,128]{5,4,3,2,1,0:T(8,128)S(1)}, f32[1,3,4,1,24,128]{5,4,3,2,1,0:T(8,128)S(1)}, u32[]{:S(2)}, u32[]{:S(2)}) collective-permute-start(f32[1,3,4,1,24,128]{5,4,3,2,1,0:T(8,128)S(1)} %get-tuple-element.51), channel_id=1, source_target_pairs={{0,2},{1,3},{2,0},{3,1},{4,6},{5,7},{6,4},{7,5},{8,10},{9,11},{10,... | collective-permute-start | bytes 442376 | tf_op jit(solution)/shard_map/ppermute | solution.py:325
  29.2 11.0 %collective-permute-start.4 = (f32[1,2,4,1,24,128]{5,4,2,1,3,0:T(8,128)S(1)}, f32[1,2,4,1,24,128]{5,4,2,1,3,0:T(8,128)S(1)}, u32[]{:S(2)}, u32[]{:S(2)}) collective-permute-start(f32[1,2,4,1,24,128]{5,4,2,1,3,0:T(8,128)S(1)} %bitcast.14), channel_id=1, source_target_pairs={{0,2},{1,3},{2,0},{3,1},{4,6},{5,7},{6,4},{7,5},{8,10},{9,11},{10,... | collective-permute-start | bytes 294920 | tf_op jit(solution)/shard_map/ppermute | solution.py:325
  39.6 6.1 %collective-permute-start.6 = (f32[1,2,4,1,24,128]{5,4,2,1,3,0:T(8,128)S(1)}, f32[1,2,4,1,24,128]{5,4,2,1,3,0:T(8,128)S(1)}, u32[]{:S(2)}, u32[]{:S(2)}) collective-permute-start(f32[1,2,4,1,24,128]{5,4,2,1,3,0:T(8,128)S(1)} %bitcast.16), channel_id=1, source_target_pairs={{0,2},{1,3},{2,0},{3,1},{4,6},{5,7},{6,4},{7,5},{8,10},{9,11},{10,... | collective-permute-start | bytes 294920 | tf_op jit(solution)/shard_map/ppermute | solution.py:325
  40.2 9.1 %collective-permute-start.5 = (f32[2,2,4,1,24,128]{5,4,3,2,1,0:T(8,128)S(1)}, f32[2,2,4,1,24,128]{5,4,3,2,1,0:T(8,128)S(1)}, u32[]{:S(2)}, u32[]{:S(2)}) collective-permute-start(f32[2,2,4,1,24,128]{5,4,3,2,1,0:T(8,128)S(1)} %maximum_bitcast_fusion.refs_2_), channel_id=1, source_target_pairs={{0,1},{1,0},{2,3},{3,2},{4,5},{5,4},{6,7},{7,6},{8,9},{9,8},{10,11... | collective-permute-start | bytes 589832 | tf_op jit(solution)/shard_map/ppermute | solution.py:325
  45.8 9.5 %collective-permute-start.7 = (f32[2,2,4,1,24,128]{5,4,3,2,1,0:T(8,128)S(1)}, f32[2,2,4,1,24,128]{5,4,3,2,1,0:T(8,128)S(1)}, u32[]{:S(2)}, u32[]{:S(2)}) collective-permute-start(f32[2,2,4,1,24,128]{5,4,3,2,1,0:T(8,128)S(1)} %maximum_bitcast_fusion.1.refs_2_), channel_id=1, source_target_pairs={{0,1},{1,0},{2,3},{3,2},{4,5},{5,4},{6,7},{7,6},{8,9},{9,8},{10,11... | collective-permute-start | bytes 589832 | tf_op jit(solution)/shard_map/ppermute | solution.py:325
  54.5 8.4 %collective-permute-start.8 = (f32[2,3,4,1,24,128]{5,4,3,2,1,0:T(8,128)S(1)}, f32[2,3,4,1,24,128]{5,4,3,2,1,0:T(8,128)S(1)}, u32[]{:S(2)}, u32[]{:S(2)}) collective-permute-start(f32[2,3,4,1,24,128]{5,4,3,2,1,0:T(8,128)S(1)} %get-tuple-element.56), channel_id=1, source_target_pairs={{0,1},{1,0},{2,3},{3,2},{4,5},{5,4},{6,7},{7,6},{8,9},{9,8},{10,11... | collective-permute-start | bytes 884744 | tf_op jit(solution)/shard_map/ppermute | solution.py:325
  55.2 19.8 %copy-start.1 = (f32[192,4]{1,0:T(8,128)S(1)}, f32[192,4]{1,0:T(8,128)}, u32[]{:S(2)}) copy-start(f32[192,4]{1,0:T(8,128)} %constant.16.clone.refs_1_) | copy-start | bytes 9220
  60.2 10.7 %collective-permute-start.11 = (f32[2,3,4,1,24,128]{5,4,3,2,1,0:T(8,128)S(1)}, f32[2,3,4,1,24,128]{5,4,3,2,1,0:T(8,128)S(1)}, u32[]{:S(2)}, u32[]{:S(2)}) collective-permute-start(f32[2,3,4,1,24,128]{5,4,3,2,1,0:T(8,128)S(1)} %get-tuple-element.59), channel_id=1, source_target_pairs={{0,1},{1,0},{2,3},{3,2},{4,5},{5,4},{6,7},{7,6},{8,9},{9,8},{10,11... | collective-permute-start | bytes 884744 | tf_op jit(solution)/shard_map/ppermute | solution.py:325
  61.6 1.5 %collective-permute-start.9 = (f32[2,4,2,4,128]{4,3,2,1,0:T(4,128)S(1)}, f32[2,4,2,4,128]{4,3,2,1,0:T(4,128)S(1)}, u32[]{:S(2)}, u32[]{:S(2)}) collective-permute-start(f32[2,4,2,4,128]{4,3,2,1,0:T(4,128)S(1)} %get-tuple-element.58), channel_id=1, source_target_pairs={{0,4},{4,0},{8,12},{12,8},{16,20},{20,16},{24,28},{28,24},{1,5},{5... | collective-permute-start | bytes 98312 | tf_op jit(solution)/shard_map/ppermute | solution.py:325
  62.9 12.9 %collective-permute-start.12 = (f32[1,3,4,1,24,128]{5,4,3,2,1,0:T(8,128)S(1)}, f32[1,3,4,1,24,128]{5,4,3,2,1,0:T(8,128)S(1)}, u32[]{:S(2)}, u32[]{:S(2)}) collective-permute-start(f32[1,3,4,1,24,128]{5,4,3,2,1,0:T(8,128)S(1)} %get-tuple-element.61), channel_id=1, source_target_pairs={{0,2},{1,3},{2,0},{3,1},{4,6},{5,7},{6,4},{7,5},{8,10},{9,11},{10,... | collective-permute-start | bytes 442376 | tf_op jit(solution)/shard_map/ppermute | solution.py:325
  63.2 4.0 %collective-permute-start.10 = (f32[2,4,2,4,128]{4,3,2,1,0:T(4,128)S(1)}, f32[2,4,2,4,128]{4,3,2,1,0:T(4,128)S(1)}, u32[]{:S(2)}, u32[]{:S(2)}) collective-permute-start(f32[2,4,2,4,128]{4,3,2,1,0:T(4,128)S(1)} %add.18), channel_id=1, source_target_pairs={{0,8},{4,12},{8,0},{12,4},{16,24},{20,28},{24,16},{28,20},{1,9},{5... | collective-permute-start | bytes 98312 | tf_op jit(solution)/shard_map/ppermute | solution.py:325
  71.0 9.5 %collective-permute-start.14 = (f32[1,3,4,1,24,128]{5,4,3,2,1,0:T(8,128)S(1)}, f32[1,3,4,1,24,128]{5,4,3,2,1,0:T(8,128)S(1)}, u32[]{:S(2)}, u32[]{:S(2)}) collective-permute-start(f32[1,3,4,1,24,128]{5,4,3,2,1,0:T(8,128)S(1)} %get-tuple-element.66), channel_id=1, source_target_pairs={{0,2},{1,3},{2,0},{3,1},{4,6},{5,7},{6,4},{7,5},{8,10},{9,11},{10,... | collective-permute-start | bytes 442376 | tf_op jit(solution)/shard_map/ppermute | solution.py:325
  71.1 4.0 %collective-permute-start.13 = (f32[2,4,2,4,128]{4,3,2,1,0:T(4,128)S(1)}, f32[2,4,2,4,128]{4,3,2,1,0:T(4,128)S(1)}, u32[]{:S(2)}, u32[]{:S(2)}) collective-permute-start(f32[2,4,2,4,128]{4,3,2,1,0:T(4,128)S(1)} %add.19.refs_1_), channel_id=1, source_target_pairs={{0,16},{4,20},{8,24},{12,28},{16,0},{20,4},{24,8},{28,12},{1,17},{... | collective-permute-start | bytes 98312 | tf_op jit(solution)/shard_map/ppermute | solution.py:325
  76.5 6.0 %collective-permute-start.16 = (f32[1,2,4,1,24,128]{5,4,3,2,1,0:T(8,128)S(1)}, f32[1,2,4,1,24,128]{5,4,3,2,1,0:T(8,128)S(1)}, u32[]{:S(2)}, u32[]{:S(2)}) collective-permute-start(f32[1,2,4,1,24,128]{5,4,3,2,1,0:T(8,128)S(1)} %bitcast.18), channel_id=1, source_target_pairs={{0,2},{1,3},{2,0},{3,1},{4,6},{5,7},{6,4},{7,5},{8,10},{9,11},{10,... | collective-permute-start | bytes 294920 | tf_op jit(solution)/shard_map/ppermute | solution.py:325
  81.1 1.3 %collective-permute-start.15 = (f32[2,4,2,4,128]{4,3,2,1,0:T(4,128)S(1)}, f32[2,4,2,4,128]{4,3,2,1,0:T(4,128)S(1)}, u32[]{:S(2)}, u32[]{:S(2)}) collective-permute-start(f32[2,4,2,4,128]{4,3,2,1,0:T(4,128)S(1)} %get-tuple-element.67), channel_id=1, source_target_pairs={{0,4},{4,0},{8,12},{12,8},{16,20},{20,16},{24,28},{28,24},{1,5},{5... | collective-permute-start | bytes 98312 | tf_op jit(solution)/shard_map/ppermute | solution.py:325
  82.5 15.7 %collective-permute-start.17 = (f32[2,2,4,1,24,128]{5,4,3,2,1,0:T(8,128)S(1)}, f32[2,2,4,1,24,128]{5,4,3,2,1,0:T(8,128)S(1)}, u32[]{:S(2)}, u32[]{:S(2)}) collective-permute-start(f32[2,2,4,1,24,128]{5,4,3,2,1,0:T(8,128)S(1)} %shard_map.108.refs_1_), channel_id=1, source_target_pairs={{0,1},{1,0},{2,3},{3,2},{4,5},{5,4},{6,7},{7,6},{8,9},{9,8},{10,11... | collective-permute-start | bytes 589832 | tf_op jit(solution)/shard_map/ppermute | solution.py:325
  84.4 13.7 %collective-permute-start.18 = (f32[1,2,4,1,24,128]{5,4,3,2,1,0:T(8,128)S(1)}, f32[1,2,4,1,24,128]{5,4,3,2,1,0:T(8,128)S(1)}, u32[]{:S(2)}, u32[]{:S(2)}) collective-permute-start(f32[1,2,4,1,24,128]{5,4,3,2,1,0:T(8,128)S(1)} %bitcast.20), channel_id=1, source_target_pairs={{0,1},{1,0},{2,3},{3,2},{4,5},{5,4},{6,7},{7,6},{8,9},{9,8},{10,11... | collective-permute-start | bytes 294920 | tf_op jit(solution)/shard_map/ppermute | solution.py:325
  84.6 13.6 %collective-permute-start.19 = (f32[1,2,4,1,24,128]{5,4,3,2,1,0:T(8,128)S(1)}, f32[1,2,4,1,24,128]{5,4,3,2,1,0:T(8,128)S(1)}, u32[]{:S(2)}, u32[]{:S(2)}) collective-permute-start(f32[1,2,4,1,24,128]{5,4,3,2,1,0:T(8,128)S(1)} %bitcast.21), channel_id=1, source_target_pairs={{0,2},{1,3},{2,0},{3,1},{4,6},{5,7},{6,4},{7,5},{8,10},{9,11},{10,... | collective-permute-start | bytes 294920 | tf_op jit(solution)/shard_map/ppermute | solution.py:325
  87.0 11.2 %collective-permute-start.20 = (f32[1,2,4,1,24,128]{5,4,3,2,1,0:T(8,128)S(1)}, f32[1,2,4,1,24,128]{5,4,3,2,1,0:T(8,128)S(1)}, u32[]{:S(2)}, u32[]{:S(2)}) collective-permute-start(f32[1,2,4,1,24,128]{5,4,3,2,1,0:T(8,128)S(1)} %bitcast.22), channel_id=1, source_target_pairs={{0,3},{1,2},{2,1},{3,0},{4,7},{5,6},{6,5},{7,4},{8,11},{9,10},{10,... | collective-permute-start | bytes 294920 | tf_op jit(solution)/shard_map/ppermute | solution.py:325
  88.8 3.9 %collective-permute-start.21 = (f32[2,4,2,4,128]{4,3,2,1,0:T(4,128)S(1)}, f32[2,4,2,4,128]{4,3,2,1,0:T(4,128)S(1)}, u32[]{:S(2)}, u32[]{:S(2)}) collective-permute-start(f32[2,4,2,4,128]{4,3,2,1,0:T(4,128)S(1)} %add.21.refs_0_), channel_id=1, source_target_pairs={{0,8},{4,12},{8,0},{12,4},{16,24},{20,28},{24,16},{28,20},{1,9},{5... | collective-permute-start | bytes 98312 | tf_op jit(solution)/shard_map/ppermute | solution.py:325
  92.7 4.0 %collective-permute-start.22 = (f32[2,4,2,4,128]{4,3,2,1,0:T(4,128)S(1)}, f32[2,4,2,4,128]{4,3,2,1,0:T(4,128)S(1)}, u32[]{:S(2)}, u32[]{:S(2)}) collective-permute-start(f32[2,4,2,4,128]{4,3,2,1,0:T(4,128)S(1)} %add.22), channel_id=1, source_target_pairs={{0,16},{4,20},{8,24},{12,28},{16,0},{20,4},{24,8},{28,12},{1,17},{... | collective-permute-start | bytes 98312 | tf_op jit(solution)/shard_map/ppermute | solution.py:325

commit v5 on v4

--- a/solution.py
+++ b/solution.py
@@ -21,7 +21,6 @@
 HBM = pltpu.MemorySpace.HBM
 WHOLE = pl.BlockSpec(memory_space=VMEM)
 OUTSIDE = pl.BlockSpec(memory_space=pl.ANY)
-SCALARS = pl.BlockSpec(memory_space=pltpu.MemorySpace.SMEM)
 CHEAP = pl.CostEstimate(flops=2**20, bytes_accessed=2**10, transcendentals=0)
 
 
@@ -64,39 +63,38 @@
 def normals_kernel(chunk, line, share, start, fill, sources, *refs):
     t0, t1, f0, f1 = chunk
     refs = list(refs)
-    place_ref = refs.pop(0)
     gain_refs = [refs.pop(0) for _ in range(sources)]
     vis_ref, coh_ref, pick_ref = [refs.pop(0) for _ in range(3)]
     outs = [refs.pop(0) for _ in range(2)]
     own_ref = refs.pop(0) if start else None
     dirs, links = coh_ref.shape[1], coh_ref.shape[4]
     rows = (t1 - t0) * (f1 - f0)
-    offsets = [(place_ref[0] ^ r) * share for r in range(line)]
     copies = []
     if fill:
+        offsets = block_offsets(line, share)
+        moves = [(r * share, share, pl.multiple_of(offsets[r], LANES)) for r in range(line)]
+        if share % LANES:
+            moves = [(0, line * share, 0)]
         station_hbm, pick_ref = pick_ref, refs.pop(0)
         station_ref, sems = refs[-2:]
         pairs = [(station_hbm, station_ref)]
         for t in range(vis_ref.shape[1]):
-            pairs += [
-                (gain_refs[0].at[:, :, t], refs[0].at[:, :, t]),
-                (vis_ref.at[:, t], refs[1].at[:, t]),
-                (coh_ref.at[:, :, t], refs[2].at[:, :, t]),
-            ]
+            for to, size, at in moves:
+                gain_from = gain_refs[0].at[:, :, t, :, pl.ds(at, size)]
+                pairs.append((gain_from, refs[0].at[:, :, t, :, pl.ds(to, size)]))
+            pairs += [(vis_ref.at[:, t], refs[1].at[:, t]), (coh_ref.at[:, :, t], refs[2].at[:, :, t])]
+        each = len(moves) + 2
         gain_refs, vis_ref, coh_ref = [refs[0]], refs[1], refs[2]
         copies = [pltpu.make_async_copy(src, dst, sems.at[i]) for i, (src, dst) in enumerate(pairs)]
         for copy in copies:
             copy.start()
         copies[0].wait()
         for t in range(t0, t1):
-            copies[1 + 3 * t].wait()
+            for copy in copies[1 + each * t : each * t + each - 1]:
+                copy.wait()
         build_picks(line, share, offsets, station_ref, pick_ref)
     if start:
-        if share % LANES:
-            offsets = [r * share for r in range(line)]
-        else:
-            offsets = [pl.multiple_of(offset, LANES) for offset in offsets]
-        blocks = [gain_refs[0][:, :, t0:t1, f0:f1, pl.ds(offset, share)] for offset in offsets]
+        blocks = [gain_refs[0][:, :, t0:t1, f0:f1, r * share : (r + 1) * share] for r in range(line)]
         own_ref[...] = blocks[0]
     else:
         blocks = [block_of(gain_refs, r) for r in range(line)]
@@ -118,8 +116,8 @@
         return values[:, f0 - low : f1 - low].reshape(rows, links)
 
     for t in range(t0, t1 if fill else t0):
-        copies[2 + 3 * t].wait()
-        copies[3 + 3 * t].wait()
+        copies[each * t + each - 1].wait()
+        copies[each * t + each].wait()
     rest_real = vis_ref[0, t0:t1, f0:f1].reshape(rows, links)
     rest_imag = vis_ref[1, t0:t1, f0:f1].reshape(rows, links)
     sides = []
@@ -152,8 +150,13 @@
         outs[r % 2][r // 2] = piece
     for t in range(vis_ref.shape[1] if fill else 0):
         if not t0 <= t < t1:
-            for copy in copies[1 + 3 * t : 4 + 3 * t]:
+            for copy in copies[1 + each * t : 1 + each * t + each]:
                 copy.wait()
+
+
+def block_offsets(line, share):
+    place = lax.axis_index("bl")
+    return [(place ^ r) * share for r in range(line)]
 
 
 def build_picks(line, share, offsets, station_ref, pick_ref):
@@ -168,18 +171,17 @@
             pick_ref[end, r * share : (r + 1) * share] = jnp.where(ids == number, one, zero)
 
 
-def picks_kernel(line, share, place_ref, station_ref, pick_ref):
-    offsets = [(place_ref[0] ^ r) * share for r in range(line)]
-    build_picks(line, share, offsets, station_ref, pick_ref)
-
-
-def make_picks(line, count, place, stations, token):
+def picks_kernel(line, share, station_ref, pick_ref):
+    build_picks(line, share, block_offsets(line, share), station_ref, pick_ref)
+
+
+def make_picks(line, count, stations, token):
     shapes = [VMEM((2, count, stations.shape[1]), jnp.bfloat16)]
     kernel = functools.partial(picks_kernel, line, count // line)
-    return run(kernel, token, [SCALARS, WHOLE], shapes, [place, stations], (), 8)[0]
-
-
-def normals(chunk, line, start, fill, place, gains, visibilities, coherencies, picks, token):
+    return run(kernel, token, [WHOLE], shapes, [stations], (), 8)[0]
+
+
+def normals(chunk, line, start, fill, gains, visibilities, coherencies, picks, token):
     t0, t1, f0, f1 = chunk
     dirs, links = coherencies.shape[1], coherencies.shape[4]
     count = gains[0].shape[-1] if start else gains[0].shape[-1] * line
@@ -192,14 +194,14 @@
     if fill:
         shapes.append(VMEM((2, count, links), jnp.bfloat16))
         times = visibilities.shape[1]
-        scratch = [pltpu.VMEM((2, links), jnp.int32), pltpu.SemaphoreType.DMA((1 + 3 * times,))]
+        scratch = [pltpu.VMEM((2, links), jnp.int32), pltpu.SemaphoreType.DMA((1 + (line + 2) * times,))]
         shapes += [VMEM(x.shape, x.dtype) for x in (gains[0], visibilities, coherencies)]
     spaces = [HBM if fill else VMEM] * (len(gains) + 3)
     sources = [*gains, visibilities, coherencies, picks]
     sources = [pltpu.with_memory_space_constraint(x, space) for x, space in zip(sources, spaces)]
     specs = [OUTSIDE if space is HBM else WHOLE for space in spaces]
     kernel = functools.partial(normals_kernel, chunk, line, share, start, fill, len(gains))
-    return run(kernel, token, [SCALARS] + specs, shapes, [place, *sources], scratch, 32)
+    return run(kernel, token, specs, shapes, sources, scratch, 32)
 
 
 def add_kernel(keep_ref, got_ref, own_ref, send_ref):
@@ -224,15 +226,15 @@
     return run(join_kernel, token, [WHOLE] * 2, [shape], [blocks, got])[0]
 
 
-def update_kernel(chunk, parts, first, chans, penalty_ref, place_ref, basis_ref, before_ref, *refs):
+def update_kernel(chunk, parts, first, penalty_ref, table_ref, before_ref, *refs):
     t0, t1, f0, f1 = chunk
     part_refs = refs[:parts]
     extra = refs[parts:-2]
     new_ref, sum_ref = refs[-2:]
     sum_ref[...] = before_ref[...]
-    basis = basis_ref[pl.ds(place_ref[1] * chans + f0, f1 - f0)]
+    basis = table_ref[f0:f1]
     for k in range(new_ref.shape[1]):
-        load = penalty_ref[k]
+        load = penalty_ref[k : k + 1]
         for t in range(t0, t1):
             weight = sum(ref[0, 2, k, t - t0] for ref in part_refs)
             divisor = weight + load
@@ -248,19 +250,19 @@
                     sum_ref[t, j, part, k : k + 1] += row
 
 
-def update(chunk, first, chans, penalty, place, basis, before, parts, extra, token):
+def update(chunk, first, penalty, table, before, parts, extra, token):
     shapes = [
         jax.ShapeDtypeStruct((2,) + parts[0].shape[2:], jnp.float32),
         jax.ShapeDtypeStruct(before.shape, jnp.float32),
     ]
-    operands = [basis, before, *parts, *extra]
-    kernel = functools.partial(update_kernel, chunk, len(parts), first, chans)
-    return run(kernel, token, [SCALARS] * 2 + [WHOLE] * len(operands), shapes, [penalty, place, *operands])
-
-
-def smooth_kernel(chunks, first, chans, place_ref, solved_ref, sum_ref, *refs):
+    operands = [penalty, table, before, *parts, *extra]
+    kernel = functools.partial(update_kernel, chunk, len(parts), first)
+    return run(kernel, token, [WHOLE] * len(operands), shapes, operands)
+
+
+def smooth_kernel(chunks, first, table_ref, sum_ref, *refs):
     one_ref, two_ref = refs[-2:]
-    solved = solved_ref[pl.ds(place_ref[1] * chans, chans)]
+    solved = table_ref[:, POLY:]
     for (t0, t1, f0, f1), gain_ref in zip(chunks, refs):
         for part in range(2):
             for k in range(one_ref.shape[1]):
@@ -279,20 +281,21 @@
                     two_ref[at] = dual
 
 
-def smooth(chunks, first, place, solved, sums, gains, extra, dims, token):
-    operands = [solved, sums, *gains, *extra]
+def smooth(chunks, first, table, sums, gains, extra, dims, token):
+    operands = [table, sums, *gains, *extra]
     shapes = [jax.ShapeDtypeStruct(dims, jnp.float32)] * 2
-    kernel = functools.partial(smooth_kernel, chunks, first, dims[3])
-    return run(kernel, token, [SCALARS] + [WHOLE] * len(operands), shapes, [place, *operands])
-
-
-def assemble_kernel(chunks, sizes, line, share, place_ref, *refs):
+    kernel = functools.partial(smooth_kernel, chunks, first)
+    return run(kernel, token, [WHOLE] * len(operands), shapes, operands)
+
+
+def assemble_kernel(chunks, sizes, line, share, *refs):
     out_ref = refs[-1]
     refs = list(refs)
+    offsets = block_offsets(line, share)
     for size, (t0, t1, f0, f1) in zip(sizes, chunks):
         blocks = [refs.pop(0) for _ in range(size)]
         for r in range(line):
-            offset = pl.multiple_of((place_ref[0] ^ r) * share, LANES)
+            offset = pl.multiple_of(offsets[r], LANES)
             out_ref[:, :, t0:t1, f0:f1, pl.ds(offset, share)] = block_of(blocks, r)
 
 
@@ -302,13 +305,13 @@
         whole = jnp.zeros(dims, jnp.float32)
         for (t0, t1, f0, f1), blocks in zip(chunks, gains):
             stacked = jnp.stack([block_of(blocks, r) for r in range(line)])
-            parts = [lax.dynamic_index_in_dim(stacked, place[0] ^ r, 0, False) for r in range(line)]
+            parts = [lax.dynamic_index_in_dim(stacked, place ^ r, 0, False) for r in range(line)]
             whole = whole.at[:, :, t0:t1, f0:f1].set(jnp.concatenate(parts, axis=-1))
         return whole
     flat = [block for blocks in gains for block in blocks]
     kernel = functools.partial(assemble_kernel, chunks, [len(blocks) for blocks in gains], line, share)
     shapes = [jax.ShapeDtypeStruct(dims, jnp.float32)]
-    return run(kernel, [], [SCALARS] + [WHOLE] * len(flat), shapes, [place, *flat])[0]
+    return run(kernel, [], [WHOLE] * len(flat), shapes, flat)[0]
 
 
 def shards(visibilities, coherencies, start_gains, penalty, stations):
@@ -316,10 +319,11 @@
     _, dirs, times, chans, count = dims
     line = lax.axis_size("bl")
     index = lax.axis_index("bl")
-    place = jnp.stack([index, lax.axis_index("chan")]).astype(jnp.int32)
     groups = lax.axis_size("chan")
     share = count // line
-    basis, solved = [jnp.asarray(table) for table in bernstein_tables(chans * groups)]
+    tables = jnp.asarray(np.concatenate(bernstein_tables(chans * groups), axis=1))
+    table = lax.dynamic_slice_in_dim(tables, lax.axis_index("chan") * chans, chans, 0)
+    loads = jnp.broadcast_to(penalty[:, None], (dirs, share))
 
     def swap(values, axis, size, bit):
         return lax.ppermute(values, axis, [(i, i ^ bit) for i in range(size)])
@@ -347,13 +351,13 @@
         first = iteration == 0
         parts, fresh = [], []
         if not first:
-            picks = make_picks(line, count, place, stations, token)
+            picks = make_picks(line, count, stations, token)
             token = [picks]
         for c, chunk in enumerate(chunks):
             fill = first and c == 0
             source = [ordered] if first else gains[c]
             ends = stations if fill else picks
-            out = normals(chunk, line, first, fill, place, source, visibilities, coherencies, ends, token)
+            out = normals(chunk, line, first, fill, source, visibilities, coherencies, ends, token)
             token = [out[0]]
             parts.append([out[0], swap(out[1], "bl", line, 1)])
             rest = list(out[2:])
@@ -375,7 +379,7 @@
         projected = zeros
         for c, chunk in enumerate(chunks):
             extra = [own[c]] if first else [own[c], targets, duals]
-            new, projected = update(chunk, first, chans, penalty, place, basis, projected, parts[c], extra, token)
+            new, projected = update(chunk, first, loads, table, projected, parts[c], extra, token)
             token = [new]
             fresh.append(new)
             direct = not first and c == len(chunks) - 1
@@ -398,9 +402,9 @@
                 got = swap(blocks, "bl", line, bit)
             gains.append([blocks, got])
         if first:
-            targets, duals = smooth(chunks, True, place, solved, steps[-1], own, [], own_dims, [])
-    consensus, dual = smooth(chunks, False, place, solved, steps[-1], own, [duals], own_dims, [])
-    return assemble(chunks, line, place, gains, dims), consensus, dual
+            targets, duals = smooth(chunks, True, table, steps[-1], own, [], own_dims, [])
+    consensus, dual = smooth(chunks, False, table, steps[-1], own, [duals], own_dims, [])
+    return assemble(chunks, line, index, gains, dims), consensus, dual
 
 
 def solution(mesh):

time: 99.9 us -> 96.6 us (0.967)
  Pallas kernels: 29.5 us -> 24.3 us
    pallas_call x17, Pallas kernels: 29.5 us -> 24.3 us  [run(): pl.pallas_call(lambda *refs: kernel(*refs[count:]), in_specs=[OUTSIDE] *...]
  transfers between devices with their start and end apart: 23 -> 23, of which waited for: 14 -> 14; matrix products, arithmetic and copies ran while one was open for 0% -> 1% of each run, Pallas kernels for 21% -> 18%
where the time goes in v5:
time: 96.6 us; the launch traced here: 96.3 us
  waiting for transfers between devices  40.3 us (42%)
  starting transfers between devices  30 us (31%)
  Pallas kernels  24.3 us (25%)
    ppermute x23, waiting for transfers between devices, swap(): return lax.ppermute(values, axis, [(i, i ^ bit) for i in range(size)])  40.3 us
    ppermute x23, starting transfers between devices, swap(): return lax.ppermute(values, axis, [(i, i ^ bit) for i in range(size)])  30 us
    pallas_call x17, Pallas kernels, run(): pl.pallas_call(lambda *refs: kernel(*refs[count:]), in_specs=[OUTSIDE] *...  24.3 us
  transfers between devices with their start and end apart: 23, of which 14 were waited for; matrix products, arithmetic and copies ran while one was open for 1% of the time, Pallas kernels for 18%

profile of v5, /device:TPU:0, one launch (start us, length us, event | category | flops | bytes accessed | tf_op | source)
XLA Modules:
  0.0 96.3 jit_solution(8749056389255366490)
XLA Ops:
  0.6 6.4 %shard_map.85 = (f32[2,3,4,1,24,128]{5,4,3,2,1,0:T(8,128)S(1)}, f32[2,3,4,1,24,128]{5,4,3,2,1,0:T(8,128)S(1)}, f32[2,4,1,24,128]{4,3,2,1,0:T(8,128)S(1)}, bf16[2...) custom-call(f32[2,4,2,24,512]{4,3,2,1,0:T(8,128)} %refs_0_.1, ...), custom_call_target="tpu_custom_call" | custom-call | flops 1048576 | bytes 1024 | tf_op jit(solution)/shard_map/pallas_call | solution.py:29
  7.0 3.1 %collective-permute-start = (f32[2,3,4,1,24,128]{5,4,3,2,1,0:T(8,128)S(1)}, f32[2,3,4,1,24,128]{5,4,3,2,1,0:T(8,128)S(1)}, u32[]{:S(2)}, u32[]{:S(2)}) collective-permute-start(f32[2,3,4,1,24,128]{5,4,3,2,1,0:T(8,128)S(1)} %get-tuple-element.43), channel_id=1, source_target_pairs={{0,1},{1,0},{2,3},{3,2},{4,5},{5,4},{6,7},{7,6},{8,9},{9,8},{10,11... | collective-permute-start | bytes 884744 | tf_op jit(solution)/shard_map/ppermute | solution.py:329
  10.1 5.1 %shard_map.86 = (f32[2,3,4,1,24,128]{5,4,3,2,1,0:T(8,128)S(1)}, f32[2,3,4,1,24,128]{5,4,3,2,1,0:T(8,128)}, f32[2,4,1,24,128]{4,3,2,1,0:T(8,128)S(1)}) custom-call(f32[2,3,4,1,24,128]{5,4,3,2,1,0:T(8,128)S(1)} %get-tuple-element.37.refs_0_.refs_1_, f32[2,4,2,24,512]{4,3,2,1,0:T(8,128)S(1)} %get-tuple-element.38.refs_1_, ...), custom_call_target="tpu_custom_call" | custom-call | flops 1048576 | bytes 1024 | tf_op jit(solution)/shard_map/pallas_call | solution.py:29
  15.2 2.0 %collective-permute-done.refs_2_ = f32[2,3,4,1,24,128]{5,4,3,2,1,0:T(8,128)S(1)} collective-permute-done((f32[2,3,4,1,24,128]{5,4,3,2,1,0:T(8,128)S(1)}, f32[2,3,4,1,24,128]{5,4,3,2,1,0:T(8,128)S(1)}, u32[]{:S(2)}, u32[]{:S(2)}) %collective-permute-start) | collective-permute-done | bytes 294944 | tf_op jit(solution)/shard_map/ppermute | solution.py:329
  17.3 0.7 shard_map.87
  18.0 2.6 %collective-permute-start.2 = (f32[1,3,4,1,24,128]{5,4,3,2,1,0:T(8,128)}, f32[1,3,4,1,24,128]{5,4,3,2,1,0:T(8,128)S(1)}, u32[]{:S(2)}, u32[]{:S(2)}) collective-permute-start(f32[1,3,4,1,24,128]{5,4,3,2,1,0:T(8,128)} %get-tuple-element.47), channel_id=1, source_target_pairs={{0,2},{1,3},{2,0},{3,1},{4,6},{5,7},{6,4},{7,5},{8,10},{9,11},{10,... | collective-permute-start | bytes 442376 | tf_op jit(solution)/shard_map/ppermute | solution.py:329
  20.6 6.5 %collective-permute-done.1.refs_2_ = f32[2,3,4,1,24,128]{5,4,3,2,1,0:T(8,128)S(1)} collective-permute-done((f32[2,3,4,1,24,128]{5,4,3,2,1,0:T(8,128)}, f32[2,3,4,1,24,128]{5,4,3,2,1,0:T(8,128)S(1)}, u32[]{:S(2)}, u32[]{:S(2)}) %collective-permute-start.1) | collective-permute-done | bytes 294944 | tf_op jit(solution)/shard_map/ppermute | solution.py:329
  27.1 1.0 collective-permute-start.3
  28.1 0.7 constant_dynamic-slice_fusion.refs_2_.refs_0_
  28.8 0.1 shard_map.89
  29.0 2.1 %collective-permute-start.4 = (f32[1,2,4,1,24,128]{5,4,2,1,3,0:T(8,128)S(1)}, f32[1,2,4,1,24,128]{5,4,2,1,3,0:T(8,128)S(1)}, u32[]{:S(2)}, u32[]{:S(2)}) collective-permute-start(f32[1,2,4,1,24,128]{5,4,2,1,3,0:T(8,128)S(1)} %bitcast.14), channel_id=1, source_target_pairs={{0,2},{1,3},{2,0},{3,1},{4,6},{5,7},{6,4},{7,5},{8,10},{9,11},{10,... | collective-permute-start | bytes 294920 | tf_op jit(solution)/shard_map/ppermute | solution.py:329
  31.1 7.1 %collective-permute-done.3.refs_5_ = f32[1,3,4,1,24,128]{5,4,3,2,1,0:T(8,128)S(1)} collective-permute-done((f32[1,3,4,1,24,128]{5,4,3,2,1,0:T(8,128)S(1)}, f32[1,3,4,1,24,128]{5,4,3,2,1,0:T(8,128)S(1)}, u32[]{:S(2)}, u32[]{:S(2)}) %collective-permute-start.3) | collective-permute-done | bytes 147488 | tf_op jit(solution)/shard_map/ppermute | solution.py:329
  38.2 0.1 shard_map.90
  38.3 0.1 collective-permute-start.6
  38.4 1.4 %collective-permute-done.4 = f32[1,2,4,1,24,128]{5,4,2,1,3,0:T(8,128)S(1)} collective-permute-done((f32[1,2,4,1,24,128]{5,4,2,1,3,0:T(8,128)S(1)}, f32[1,2,4,1,24,128]{5,4,2,1,3,0:T(8,128)S(1)}, u32[]{:S(2)}, u32[]{:S(2)}) %collective-permute-start.4) | collective-permute-done | bytes 98336 | tf_op jit(solution)/shard_map/ppermute | solution.py:329
  39.8 1.4 %collective-permute-start.5 = (f32[2,2,4,1,24,128]{5,4,3,2,1,0:T(8,128)S(1)}, f32[2,2,4,1,24,128]{5,4,3,2,1,0:T(8,128)S(1)}, u32[]{:S(2)}, u32[]{:S(2)}) collective-permute-start(f32[2,2,4,1,24,128]{5,4,3,2,1,0:T(8,128)S(1)} %maximum_bitcast_fusion.refs_1_), channel_id=1, source_target_pairs={{0,1},{1,0},{2,3},{3,2},{4,5},{5,4},{6,7},{7,6},{8,9},{9,8},{10,11... | collective-permute-start | bytes 589832 | tf_op jit(solution)/shard_map/ppermute | solution.py:329
  41.3 3.3 %collective-permute-done.6 = f32[1,2,4,1,24,128]{5,4,2,1,3,0:T(8,128)S(1)} collective-permute-done((f32[1,2,4,1,24,128]{5,4,2,1,3,0:T(8,128)S(1)}, f32[1,2,4,1,24,128]{5,4,2,1,3,0:T(8,128)S(1)}, u32[]{:S(2)}, u32[]{:S(2)}) %collective-permute-start.6) | collective-permute-done | bytes 98336 | tf_op jit(solution)/shard_map/ppermute | solution.py:329
  44.6 0.2 collective-permute-start.7
  44.8 0.5 shard_map.91.refs_0_.refs_5_
  45.3 3.2 %collective-permute-done.5.refs_2_ = f32[2,2,4,1,24,128]{5,4,3,2,1,0:T(8,128)S(1)} collective-permute-done((f32[2,2,4,1,24,128]{5,4,3,2,1,0:T(8,128)S(1)}, f32[2,2,4,1,24,128]{5,4,3,2,1,0:T(8,128)S(1)}, u32[]{:S(2)}, u32[]{:S(2)}) %collective-permute-start.5) | collective-permute-done | bytes 196640 | tf_op jit(solution)/shard_map/ppermute | solution.py:329
  48.5 4.6 %shard_map.92 = (f32[2,3,4,1,24,128]{5,4,3,2,1,0:T(8,128)S(1)}, f32[2,3,4,1,24,128]{5,4,3,2,1,0:T(8,128)S(1)}) custom-call(bf16[2,512,2048]{2,1,0:T(8,128)(2,1)S(1)} %shard_map.91.refs_0_.refs_5_, f32[2,2,4,1,24,128]{5,4,3,2,1,0:T(8,128)S(1)} %maximum_bitcast_fusion.refs_1_, f32[2,2,4,1,24,128]{5,4,3,2,1,0:T(8,128)S(1)} %collective-permute-done.5.refs_2_, ...), custom_call_target="tpu_custom_call" | custom-call | flops 1048576 | bytes 1024 | tf_op jit(solution)/shard_map/pallas_call | solution.py:29
  53.1 0.7 collective-permute-start.8
  53.8 4.4 %shard_map.93 = (f32[2,3,4,1,24,128]{5,4,3,2,1,0:T(8,128)S(1)}, f32[2,3,4,1,24,128]{5,4,3,2,1,0:T(8,128)S(1)}) custom-call(f32[2,3,4,1,24,128]{5,4,3,2,1,0:T(8,128)S(1)} %get-tuple-element.54.refs_0_.refs_1_, f32[2,2,4,1,24,128]{5,4,3,2,1,0:T(8,128)S(1)} %maximum_bitcast_fusion.1.refs_1_, f32[2,2,4,1,24,128]{5,4,3,2,1,0:T(8,128)S(1)} %collective-permute-done.7.refs_2_, ...), custom_call_target="tpu_custom_call" | custom-call | flops 1048576 | bytes 1024 | tf_op jit(solution)/shard_map/pallas_call | solution.py:29
  58.1 1.5 %collective-permute-start.11 = (f32[2,3,4,1,24,128]{5,4,3,2,1,0:T(8,128)S(1)}, f32[2,3,4,1,24,128]{5,4,3,2,1,0:T(8,128)S(1)}, u32[]{:S(2)}, u32[]{:S(2)}) collective-permute-start(f32[2,3,4,1,24,128]{5,4,3,2,1,0:T(8,128)S(1)} %get-tuple-element.59), channel_id=1, source_target_pairs={{0,1},{1,0},{2,3},{3,2},{4,5},{5,4},{6,7},{7,6},{8,9},{9,8},{10,11... | collective-permute-start | bytes 884744 | tf_op jit(solution)/shard_map/ppermute | solution.py:329
  59.6 2.4 %collective-permute-done.8.refs_2_ = f32[2,3,4,1,24,128]{5,4,3,2,1,0:T(8,128)S(1)} collective-permute-done((f32[2,3,4,1,24,128]{5,4,3,2,1,0:T(8,128)S(1)}, f32[2,3,4,1,24,128]{5,4,3,2,1,0:T(8,128)S(1)}, u32[]{:S(2)}, u32[]{:S(2)}) %collective-permute-start.8) | collective-permute-done | bytes 294944 | tf_op jit(solution)/shard_map/ppermute | solution.py:329
  62.1 0.3 collective-permute-start.12
  62.4 2.0 %collective-permute-start.10 = (f32[2,4,2,4,128]{4,3,2,1,0:T(4,128)S(1)}, f32[2,4,2,4,128]{4,3,2,1,0:T(4,128)S(1)}, u32[]{:S(2)}, u32[]{:S(2)}) collective-permute-start(f32[2,4,2,4,128]{4,3,2,1,0:T(4,128)S(1)} %add.22), channel_id=1, source_target_pairs={{0,8},{4,12},{8,0},{12,4},{16,24},{20,28},{24,16},{28,20},{1,9},{5... | collective-permute-start | bytes 98312 | tf_op jit(solution)/shard_map/ppermute | solution.py:329
  64.4 2.0 %collective-permute-done.10 = f32[2,4,2,4,128]{4,3,2,1,0:T(4,128)S(1)} collective-permute-done((f32[2,4,2,4,128]{4,3,2,1,0:T(4,128)S(1)}, f32[2,4,2,4,128]{4,3,2,1,0:T(4,128)S(1)}, u32[]{:S(2)}, u32[]{:S(2)}) %collective-permute-start.10) | collective-permute-done | bytes 32800 | tf_op jit(solution)/shard_map/ppermute | solution.py:329
  66.4 3.3 %collective-permute-done.11.refs_3_ = f32[2,3,4,1,24,128]{5,4,3,2,1,0:T(8,128)S(1)} collective-permute-done((f32[2,3,4,1,24,128]{5,4,3,2,1,0:T(8,128)S(1)}, f32[2,3,4,1,24,128]{5,4,3,2,1,0:T(8,128)S(1)}, u32[]{:S(2)}, u32[]{:S(2)}) %collective-permute-start.11) | collective-permute-done | bytes 294944 | tf_op jit(solution)/shard_map/ppermute | solution.py:329
  69.8 0.1 collective-permute-start.14
  69.9 1.9 %collective-permute-start.13 = (f32[2,4,2,4,128]{4,3,2,1,0:T(4,128)S(1)}, f32[2,4,2,4,128]{4,3,2,1,0:T(4,128)S(1)}, u32[]{:S(2)}, u32[]{:S(2)}) collective-permute-start(f32[2,4,2,4,128]{4,3,2,1,0:T(4,128)S(1)} %add.23.refs_1_), channel_id=1, source_target_pairs={{0,16},{4,20},{8,24},{12,28},{16,0},{20,4},{24,8},{28,12},{1,17},{... | collective-permute-start | bytes 98312 | tf_op jit(solution)/shard_map/ppermute | solution.py:329
  71.7 2.1 %collective-permute-done.13 = f32[2,4,2,4,128]{4,3,2,1,0:T(4,128)S(1)} collective-permute-done((f32[2,4,2,4,128]{4,3,2,1,0:T(4,128)S(1)}, f32[2,4,2,4,128]{4,3,2,1,0:T(4,128)S(1)}, u32[]{:S(2)}, u32[]{:S(2)}) %collective-permute-start.13) | collective-permute-done | bytes 32800 | tf_op jit(solution)/shard_map/ppermute | solution.py:329
  73.9 0.1 shard_map.96
  74.0 0.1 shard_map.97
  74.1 2.9 %collective-permute-start.16 = (f32[1,2,4,1,24,128]{5,4,3,2,1,0:T(8,128)S(1)}, f32[1,2,4,1,24,128]{5,4,3,2,1,0:T(8,128)S(1)}, u32[]{:S(2)}, u32[]{:S(2)}) collective-permute-start(f32[1,2,4,1,24,128]{5,4,3,2,1,0:T(8,128)S(1)} %bitcast.16), channel_id=1, source_target_pairs={{0,2},{1,3},{2,0},{3,1},{4,6},{5,7},{6,4},{7,5},{8,10},{9,11},{10,... | collective-permute-start | bytes 294920 | tf_op jit(solution)/shard_map/ppermute | solution.py:329
  77.1 1.6 %collective-permute-done.14.refs_5_ = f32[1,3,4,1,24,128]{5,4,3,2,1,0:T(8,128)S(1)} collective-permute-done((f32[1,3,4,1,24,128]{5,4,3,2,1,0:T(8,128)S(1)}, f32[1,3,4,1,24,128]{5,4,3,2,1,0:T(8,128)S(1)}, u32[]{:S(2)}, u32[]{:S(2)}) %collective-permute-start.14) | collective-permute-done | bytes 147488 | tf_op jit(solution)/shard_map/ppermute | solution.py:329
  78.6 0.1 shard_map.98
  78.8 1.2 %collective-permute-done.15 = f32[2,4,2,4,128]{4,3,2,1,0:T(4,128)S(1)} collective-permute-done((f32[2,4,2,4,128]{4,3,2,1,0:T(4,128)S(1)}, f32[2,4,2,4,128]{4,3,2,1,0:T(4,128)S(1)}, u32[]{:S(2)}, u32[]{:S(2)}) %collective-permute-start.15) | collective-permute-done | bytes 32800 | tf_op jit(solution)/shard_map/ppermute | solution.py:329
  80.1 2.1 %collective-permute-start.17 = (f32[2,2,4,1,24,128]{5,4,3,2,1,0:T(8,128)S(1)}, f32[2,2,4,1,24,128]{5,4,3,2,1,0:T(8,128)S(1)}, u32[]{:S(2)}, u32[]{:S(2)}) collective-permute-start(f32[2,2,4,1,24,128]{5,4,3,2,1,0:T(8,128)S(1)} %shard_map.99.refs_0_), channel_id=1, source_target_pairs={{0,1},{1,0},{2,3},{3,2},{4,5},{5,4},{6,7},{7,6},{8,9},{9,8},{10,11... | collective-permute-start | bytes 589832 | tf_op jit(solution)/shard_map/ppermute | solution.py:329
  82.1 0.1 collective-permute-start.18
  82.2 2.5 %collective-permute-start.19 = (f32[1,2,4,1,24,128]{5,4,3,2,1,0:T(8,128)S(1)}, f32[1,2,4,1,24,128]{5,4,3,2,1,0:T(8,128)S(1)}, u32[]{:S(2)}, u32[]{:S(2)}) collective-permute-start(f32[1,2,4,1,24,128]{5,4,3,2,1,0:T(8,128)S(1)} %bitcast.19), channel_id=1, source_target_pairs={{0,2},{1,3},{2,0},{3,1},{4,6},{5,7},{6,4},{7,5},{8,10},{9,11},{10,... | collective-permute-start | bytes 294920 | tf_op jit(solution)/shard_map/ppermute | solution.py:329
  84.7 1.8 %collective-permute-start.20 = (f32[1,2,4,1,24,128]{5,4,3,2,1,0:T(8,128)S(1)}, f32[1,2,4,1,24,128]{5,4,3,2,1,0:T(8,128)S(1)}, u32[]{:S(2)}, u32[]{:S(2)}) collective-permute-start(f32[1,2,4,1,24,128]{5,4,3,2,1,0:T(8,128)S(1)} %bitcast.20), channel_id=1, source_target_pairs={{0,3},{1,2},{2,1},{3,0},{4,7},{5,6},{6,5},{7,4},{8,11},{9,10},{10,... | collective-permute-start | bytes 294920 | tf_op jit(solution)/shard_map/ppermute | solution.py:329
  86.5 1.9 %collective-permute-start.21 = (f32[2,4,2,4,128]{4,3,2,1,0:T(4,128)S(1)}, f32[2,4,2,4,128]{4,3,2,1,0:T(4,128)S(1)}, u32[]{:S(2)}, u32[]{:S(2)}) collective-permute-start(f32[2,4,2,4,128]{4,3,2,1,0:T(4,128)S(1)} %add.25.refs_0_), channel_id=1, source_target_pairs={{0,8},{4,12},{8,0},{12,4},{16,24},{20,28},{24,16},{28,20},{1,9},{5... | collective-permute-start | bytes 98312 | tf_op jit(solution)/shard_map/ppermute | solution.py:329
  88.4 2.0 %collective-permute-done.21 = f32[2,4,2,4,128]{4,3,2,1,0:T(4,128)S(1)} collective-permute-done((f32[2,4,2,4,128]{4,3,2,1,0:T(4,128)S(1)}, f32[2,4,2,4,128]{4,3,2,1,0:T(4,128)S(1)}, u32[]{:S(2)}, u32[]{:S(2)}) %collective-permute-start.21) | collective-permute-done | bytes 32800 | tf_op jit(solution)/shard_map/ppermute | solution.py:329
  90.4 1.9 %collective-permute-start.22 = (f32[2,4,2,4,128]{4,3,2,1,0:T(4,128)S(1)}, f32[2,4,2,4,128]{4,3,2,1,0:T(4,128)S(1)}, u32[]{:S(2)}, u32[]{:S(2)}) collective-permute-start(f32[2,4,2,4,128]{4,3,2,1,0:T(4,128)S(1)} %add.26), channel_id=1, source_target_pairs={{0,16},{4,20},{8,24},{12,28},{16,0},{20,4},{24,8},{28,12},{1,17},{... | collective-permute-start | bytes 98312 | tf_op jit(solution)/shard_map/ppermute | solution.py:329
  92.4 2.1 %collective-permute-done.22 = f32[2,4,2,4,128]{4,3,2,1,0:T(4,128)S(1)} collective-permute-done((f32[2,4,2,4,128]{4,3,2,1,0:T(4,128)S(1)}, f32[2,4,2,4,128]{4,3,2,1,0:T(4,128)S(1)}, u32[]{:S(2)}, u32[]{:S(2)}) %collective-permute-start.22) | collective-permute-done | bytes 32800 | tf_op jit(solution)/shard_map/ppermute | solution.py:329
  94.4 0.9 shard_map.101
  95.3 1.0 %shard_map.100 = f32[2,4,2,24,512]{4,3,2,1,0:T(8,128)} custom-call(f32[2,2,4,1,24,128]{5,4,3,2,1,0:T(8,128)S(1)} %shard_map.99.refs_0_, f32[2,2,4,1,24,128]{5,4,3,2,1,0:T(8,128)S(1)} %collective-permute-done.17.refs_1_, f32[1,2,4,1,24,128]{5,4,3,2,1,0:T(8,128)S(1)} %bitcast.21, f32[1,2,4,1,24,128]{5,4,3,2,1,0:T(8,128)S(1)} %collective-permute-done.18.refs_3_, ...), custom_call_target="tpu_custom_call" | custom-call | flops 1048576 | bytes 1024 | tf_op jit(solution)/shard_map/pallas_call | solution.py:29
  (30 shorter events, 0.4 us)
Async XLA Ops:
  7.0 10.3 %collective-permute-start = (f32[2,3,4,1,24,128]{5,4,3,2,1,0:T(8,128)S(1)}, f32[2,3,4,1,24,128]{5,4,3,2,1,0:T(8,128)S(1)}, u32[]{:S(2)}, u32[]{:S(2)}) collective-permute-start(f32[2,3,4,1,24,128]{5,4,3,2,1,0:T(8,128)S(1)} %get-tuple-element.43), channel_id=1, source_target_pairs={{0,1},{1,0},{2,3},{3,2},{4,5},{5,4},{6,7},{7,6},{8,9},{9,8},{10,11... | collective-permute-start | bytes 884744 | tf_op jit(solution)/shard_map/ppermute | solution.py:329
  10.1 18.7 %copy-start.1 = (f32[4]{0:T(128)S(1)}, f32[4]{0:T(128)}, u32[]{:S(2)}) copy-start(f32[4]{0:T(128)} %param.9) | copy-start | bytes 52
  10.1 34.6 %copy-start = (s32[2,2048]{1,0:T(2,128)S(1)}, s32[2,2048]{1,0:T(2,128)}, u32[]{:S(2)}) copy-start(s32[2,2048]{1,0:T(2,128)} %refs_1_.3) | copy-start | bytes 49156
  15.2 11.8 %collective-permute-start.1 = (f32[2,3,4,1,24,128]{5,4,3,2,1,0:T(8,128)}, f32[2,3,4,1,24,128]{5,4,3,2,1,0:T(8,128)S(1)}, u32[]{:S(2)}, u32[]{:S(2)}) collective-permute-start(f32[2,3,4,1,24,128]{5,4,3,2,1,0:T(8,128)} %get-tuple-element.45), channel_id=1, source_target_pairs={{0,1},{1,0},{2,3},{3,2},{4,5},{5,4},{6,7},{7,6},{8,9},{9,8},{10,11... | collective-permute-start | bytes 884744 | tf_op jit(solution)/shard_map/ppermute | solution.py:329
  18.0 10.8 %collective-permute-start.2 = (f32[1,3,4,1,24,128]{5,4,3,2,1,0:T(8,128)}, f32[1,3,4,1,24,128]{5,4,3,2,1,0:T(8,128)S(1)}, u32[]{:S(2)}, u32[]{:S(2)}) collective-permute-start(f32[1,3,4,1,24,128]{5,4,3,2,1,0:T(8,128)} %get-tuple-element.47), channel_id=1, source_target_pairs={{0,2},{1,3},{2,0},{3,1},{4,6},{5,7},{6,4},{7,5},{8,10},{9,11},{10,... | collective-permute-start | bytes 442376 | tf_op jit(solution)/shard_map/ppermute | solution.py:329
  27.1 11.1 %collective-permute-start.3 = (f32[1,3,4,1,24,128]{5,4,3,2,1,0:T(8,128)S(1)}, f32[1,3,4,1,24,128]{5,4,3,2,1,0:T(8,128)S(1)}, u32[]{:S(2)}, u32[]{:S(2)}) collective-permute-start(f32[1,3,4,1,24,128]{5,4,3,2,1,0:T(8,128)S(1)} %get-tuple-element.51), channel_id=1, source_target_pairs={{0,2},{1,3},{2,0},{3,1},{4,6},{5,7},{6,4},{7,5},{8,10},{9,11},{10,... | collective-permute-start | bytes 442376 | tf_op jit(solution)/shard_map/ppermute | solution.py:329
  29.0 10.9 %collective-permute-start.4 = (f32[1,2,4,1,24,128]{5,4,2,1,3,0:T(8,128)S(1)}, f32[1,2,4,1,24,128]{5,4,2,1,3,0:T(8,128)S(1)}, u32[]{:S(2)}, u32[]{:S(2)}) collective-permute-start(f32[1,2,4,1,24,128]{5,4,2,1,3,0:T(8,128)S(1)} %bitcast.14), channel_id=1, source_target_pairs={{0,2},{1,3},{2,0},{3,1},{4,6},{5,7},{6,4},{7,5},{8,10},{9,11},{10,... | collective-permute-start | bytes 294920 | tf_op jit(solution)/shard_map/ppermute | solution.py:329
  38.3 6.3 %collective-permute-start.6 = (f32[1,2,4,1,24,128]{5,4,2,1,3,0:T(8,128)S(1)}, f32[1,2,4,1,24,128]{5,4,2,1,3,0:T(8,128)S(1)}, u32[]{:S(2)}, u32[]{:S(2)}) collective-permute-start(f32[1,2,4,1,24,128]{5,4,2,1,3,0:T(8,128)S(1)} %bitcast.12), channel_id=1, source_target_pairs={{0,2},{1,3},{2,0},{3,1},{4,6},{5,7},{6,4},{7,5},{8,10},{9,11},{10,... | collective-permute-start | bytes 294920 | tf_op jit(solution)/shard_map/ppermute | solution.py:329
  39.8 8.6 %collective-permute-start.5 = (f32[2,2,4,1,24,128]{5,4,3,2,1,0:T(8,128)S(1)}, f32[2,2,4,1,24,128]{5,4,3,2,1,0:T(8,128)S(1)}, u32[]{:S(2)}, u32[]{:S(2)}) collective-permute-start(f32[2,2,4,1,24,128]{5,4,3,2,1,0:T(8,128)S(1)} %maximum_bitcast_fusion.refs_1_), channel_id=1, source_target_pairs={{0,1},{1,0},{2,3},{3,2},{4,5},{5,4},{6,7},{7,6},{8,9},{9,8},{10,11... | collective-permute-start | bytes 589832 | tf_op jit(solution)/shard_map/ppermute | solution.py:329
  44.6 9.2 %collective-permute-start.7 = (f32[2,2,4,1,24,128]{5,4,3,2,1,0:T(8,128)S(1)}, f32[2,2,4,1,24,128]{5,4,3,2,1,0:T(8,128)S(1)}, u32[]{:S(2)}, u32[]{:S(2)}) collective-permute-start(f32[2,2,4,1,24,128]{5,4,3,2,1,0:T(8,128)S(1)} %maximum_bitcast_fusion.1.refs_1_), channel_id=1, source_target_pairs={{0,1},{1,0},{2,3},{3,2},{4,5},{5,4},{6,7},{7,6},{8,9},{9,8},{10,11... | collective-permute-start | bytes 589832 | tf_op jit(solution)/shard_map/ppermute | solution.py:329
  53.1 9.0 %collective-permute-start.8 = (f32[2,3,4,1,24,128]{5,4,3,2,1,0:T(8,128)S(1)}, f32[2,3,4,1,24,128]{5,4,3,2,1,0:T(8,128)S(1)}, u32[]{:S(2)}, u32[]{:S(2)}) collective-permute-start(f32[2,3,4,1,24,128]{5,4,3,2,1,0:T(8,128)S(1)} %get-tuple-element.56), channel_id=1, source_target_pairs={{0,1},{1,0},{2,3},{3,2},{4,5},{5,4},{6,7},{7,6},{8,9},{9,8},{10,11... | collective-permute-start | bytes 884744 | tf_op jit(solution)/shard_map/ppermute | solution.py:329
  58.1 11.6 %collective-permute-start.11 = (f32[2,3,4,1,24,128]{5,4,3,2,1,0:T(8,128)S(1)}, f32[2,3,4,1,24,128]{5,4,3,2,1,0:T(8,128)S(1)}, u32[]{:S(2)}, u32[]{:S(2)}) collective-permute-start(f32[2,3,4,1,24,128]{5,4,3,2,1,0:T(8,128)S(1)} %get-tuple-element.59), channel_id=1, source_target_pairs={{0,1},{1,0},{2,3},{3,2},{4,5},{5,4},{6,7},{7,6},{8,9},{9,8},{10,11... | collective-permute-start | bytes 884744 | tf_op jit(solution)/shard_map/ppermute | solution.py:329
  59.6 2.8 %collective-permute-start.9 = (f32[2,4,2,4,128]{4,3,2,1,0:T(4,128)S(1)}, f32[2,4,2,4,128]{4,3,2,1,0:T(4,128)S(1)}, u32[]{:S(2)}, u32[]{:S(2)}) collective-permute-start(f32[2,4,2,4,128]{4,3,2,1,0:T(4,128)S(1)} %get-tuple-element.58), channel_id=1, source_target_pairs={{0,4},{4,0},{8,12},{12,8},{16,20},{20,16},{24,28},{28,24},{1,5},{5... | collective-permute-start | bytes 98312 | tf_op jit(solution)/shard_map/ppermute | solution.py:329
  62.1 11.9 %collective-permute-start.12 = (f32[1,3,4,1,24,128]{5,4,3,2,1,0:T(8,128)S(1)}, f32[1,3,4,1,24,128]{5,4,3,2,1,0:T(8,128)S(1)}, u32[]{:S(2)}, u32[]{:S(2)}) collective-permute-start(f32[1,3,4,1,24,128]{5,4,3,2,1,0:T(8,128)S(1)} %get-tuple-element.61), channel_id=1, source_target_pairs={{0,2},{1,3},{2,0},{3,1},{4,6},{5,7},{6,4},{7,5},{8,10},{9,11},{10,... | collective-permute-start | bytes 442376 | tf_op jit(solution)/shard_map/ppermute | solution.py:329
  62.4 4.0 %collective-permute-start.10 = (f32[2,4,2,4,128]{4,3,2,1,0:T(4,128)S(1)}, f32[2,4,2,4,128]{4,3,2,1,0:T(4,128)S(1)}, u32[]{:S(2)}, u32[]{:S(2)}) collective-permute-start(f32[2,4,2,4,128]{4,3,2,1,0:T(4,128)S(1)} %add.22), channel_id=1, source_target_pairs={{0,8},{4,12},{8,0},{12,4},{16,24},{20,28},{24,16},{28,20},{1,9},{5... | collective-permute-start | bytes 98312 | tf_op jit(solution)/shard_map/ppermute | solution.py:329
  69.8 8.8 %collective-permute-start.14 = (f32[1,3,4,1,24,128]{5,4,3,2,1,0:T(8,128)S(1)}, f32[1,3,4,1,24,128]{5,4,3,2,1,0:T(8,128)S(1)}, u32[]{:S(2)}, u32[]{:S(2)}) collective-permute-start(f32[1,3,4,1,24,128]{5,4,3,2,1,0:T(8,128)S(1)} %get-tuple-element.66), channel_id=1, source_target_pairs={{0,2},{1,3},{2,0},{3,1},{4,6},{5,7},{6,4},{7,5},{8,10},{9,11},{10,... | collective-permute-start | bytes 442376 | tf_op jit(solution)/shard_map/ppermute | solution.py:329
  69.9 4.0 %collective-permute-start.13 = (f32[2,4,2,4,128]{4,3,2,1,0:T(4,128)S(1)}, f32[2,4,2,4,128]{4,3,2,1,0:T(4,128)S(1)}, u32[]{:S(2)}, u32[]{:S(2)}) collective-permute-start(f32[2,4,2,4,128]{4,3,2,1,0:T(4,128)S(1)} %add.23.refs_1_), channel_id=1, source_target_pairs={{0,16},{4,20},{8,24},{12,28},{16,0},{20,4},{24,8},{28,12},{1,17},{... | collective-permute-start | bytes 98312 | tf_op jit(solution)/shard_map/ppermute | solution.py:329
  74.1 5.9 %collective-permute-start.16 = (f32[1,2,4,1,24,128]{5,4,3,2,1,0:T(8,128)S(1)}, f32[1,2,4,1,24,128]{5,4,3,2,1,0:T(8,128)S(1)}, u32[]{:S(2)}, u32[]{:S(2)}) collective-permute-start(f32[1,2,4,1,24,128]{5,4,3,2,1,0:T(8,128)S(1)} %bitcast.16), channel_id=1, source_target_pairs={{0,2},{1,3},{2,0},{3,1},{4,6},{5,7},{6,4},{7,5},{8,10},{9,11},{10,... | collective-permute-start | bytes 294920 | tf_op jit(solution)/shard_map/ppermute | solution.py:329
  78.7 1.3 %collective-permute-start.15 = (f32[2,4,2,4,128]{4,3,2,1,0:T(4,128)S(1)}, f32[2,4,2,4,128]{4,3,2,1,0:T(4,128)S(1)}, u32[]{:S(2)}, u32[]{:S(2)}) collective-permute-start(f32[2,4,2,4,128]{4,3,2,1,0:T(4,128)S(1)} %get-tuple-element.67), channel_id=1, source_target_pairs={{0,4},{4,0},{8,12},{12,8},{16,20},{20,16},{24,28},{28,24},{1,5},{5... | collective-permute-start | bytes 98312 | tf_op jit(solution)/shard_map/ppermute | solution.py:329
  80.1 15.3 %collective-permute-start.17 = (f32[2,2,4,1,24,128]{5,4,3,2,1,0:T(8,128)S(1)}, f32[2,2,4,1,24,128]{5,4,3,2,1,0:T(8,128)S(1)}, u32[]{:S(2)}, u32[]{:S(2)}) collective-permute-start(f32[2,2,4,1,24,128]{5,4,3,2,1,0:T(8,128)S(1)} %shard_map.99.refs_0_), channel_id=1, source_target_pairs={{0,1},{1,0},{2,3},{3,2},{4,5},{5,4},{6,7},{7,6},{8,9},{9,8},{10,11... | collective-permute-start | bytes 589832 | tf_op jit(solution)/shard_map/ppermute | solution.py:329
  82.1 13.2 %collective-permute-start.18 = (f32[1,2,4,1,24,128]{5,4,3,2,1,0:T(8,128)S(1)}, f32[1,2,4,1,24,128]{5,4,3,2,1,0:T(8,128)S(1)}, u32[]{:S(2)}, u32[]{:S(2)}) collective-permute-start(f32[1,2,4,1,24,128]{5,4,3,2,1,0:T(8,128)S(1)} %bitcast.18), channel_id=1, source_target_pairs={{0,1},{1,0},{2,3},{3,2},{4,5},{5,4},{6,7},{7,6},{8,9},{9,8},{10,11... | collective-permute-start | bytes 294920 | tf_op jit(solution)/shard_map/ppermute | solution.py:329
  82.2 13.1 %collective-permute-start.19 = (f32[1,2,4,1,24,128]{5,4,3,2,1,0:T(8,128)S(1)}, f32[1,2,4,1,24,128]{5,4,3,2,1,0:T(8,128)S(1)}, u32[]{:S(2)}, u32[]{:S(2)}) collective-permute-start(f32[1,2,4,1,24,128]{5,4,3,2,1,0:T(8,128)S(1)} %bitcast.19), channel_id=1, source_target_pairs={{0,2},{1,3},{2,0},{3,1},{4,6},{5,7},{6,4},{7,5},{8,10},{9,11},{10,... | collective-permute-start | bytes 294920 | tf_op jit(solution)/shard_map/ppermute | solution.py:329
  84.7 10.6 %collective-permute-start.20 = (f32[1,2,4,1,24,128]{5,4,3,2,1,0:T(8,128)S(1)}, f32[1,2,4,1,24,128]{5,4,3,2,1,0:T(8,128)S(1)}, u32[]{:S(2)}, u32[]{:S(2)}) collective-permute-start(f32[1,2,4,1,24,128]{5,4,3,2,1,0:T(8,128)S(1)} %bitcast.20), channel_id=1, source_target_pairs={{0,3},{1,2},{2,1},{3,0},{4,7},{5,6},{6,5},{7,4},{8,11},{9,10},{10,... | collective-permute-start | bytes 294920 | tf_op jit(solution)/shard_map/ppermute | solution.py:329
  86.5 3.9 %collective-permute-start.21 = (f32[2,4,2,4,128]{4,3,2,1,0:T(4,128)S(1)}, f32[2,4,2,4,128]{4,3,2,1,0:T(4,128)S(1)}, u32[]{:S(2)}, u32[]{:S(2)}) collective-permute-start(f32[2,4,2,4,128]{4,3,2,1,0:T(4,128)S(1)} %add.25.refs_0_), channel_id=1, source_target_pairs={{0,8},{4,12},{8,0},{12,4},{16,24},{20,28},{24,16},{28,20},{1,9},{5... | collective-permute-start | bytes 98312 | tf_op jit(solution)/shard_map/ppermute | solution.py:329
  90.4 4.0 %collective-permute-start.22 = (f32[2,4,2,4,128]{4,3,2,1,0:T(4,128)S(1)}, f32[2,4,2,4,128]{4,3,2,1,0:T(4,128)S(1)}, u32[]{:S(2)}, u32[]{:S(2)}) collective-permute-start(f32[2,4,2,4,128]{4,3,2,1,0:T(4,128)S(1)} %add.26), channel_id=1, source_target_pairs={{0,16},{4,20},{8,24},{12,28},{16,0},{20,4},{24,8},{28,12},{1,17},{... | collective-permute-start | bytes 98312 | tf_op jit(solution)/shard_map/ppermute | solution.py:329

commit v6 on v5

--- a/solution.py
+++ b/solution.py
@@ -382,7 +382,7 @@
             new, projected = update(chunk, first, loads, table, projected, parts[c], extra, token)
             token = [new]
             fresh.append(new)
-            direct = not first and c == len(chunks) - 1
+            direct = c == len(chunks) - 1
             arrived.append([swap(new[None], "bl", line, r) for r in (direct_order if direct else [line // 2])])
         own = fresh
         steps = chan_steps(projected)

time: 96.6 us -> 94.9 us (0.982)
  waiting for transfers between devices: 40.3 us -> 35.6 us
  starting transfers between devices: 30 us -> 33 us
    ppermute x23 -> x24, waiting for transfers between devices: 40.3 us -> 35.6 us  [swap(): return lax.ppermute(values, axis, [(i, i ^ bit) for i in range(size)])]
    ppermute x23 -> x24, starting transfers between devices: 30 us -> 33 us  [swap(): return lax.ppermute(values, axis, [(i, i ^ bit) for i in range(size)])]
  transfers between devices with their start and end apart: 23 -> 24, of which waited for: 14 -> 12; matrix products, arithmetic and copies ran while one was open for 1% -> 1% of each run, Pallas kernels for 18% -> 18%
where the time goes in v6:
time: 94.9 us; the launch traced here: 94.6 us
  waiting for transfers between devices  35.6 us (38%)
  starting transfers between devices  33 us (35%)
  Pallas kernels  24.3 us (26%)
    ppermute x24, waiting for transfers between devices, swap(): return lax.ppermute(values, axis, [(i, i ^ bit) for i in range(size)])  35.6 us
    ppermute x24, starting transfers between devices, swap(): return lax.ppermute(values, axis, [(i, i ^ bit) for i in range(size)])  33 us
    pallas_call x17, Pallas kernels, run(): pl.pallas_call(lambda *refs: kernel(*refs[count:]), in_specs=[OUTSIDE] *...  24.3 us
  transfers between devices with their start and end apart: 24, of which 12 were waited for; matrix products, arithmetic and copies ran while one was open for 1% of the time, Pallas kernels for 18%

profile of v6, /device:TPU:0, one launch (start us, length us, event | category | flops | bytes accessed | tf_op | source)
XLA Modules:
  0.0 94.6 jit_solution(17348764571370415628)
XLA Ops:
  0.6 6.4 %shard_map.85 = (f32[2,3,4,1,24,128]{5,4,3,2,1,0:T(8,128)S(1)}, f32[2,3,4,1,24,128]{5,4,3,2,1,0:T(8,128)S(1)}, f32[2,4,1,24,128]{4,3,2,1,0:T(8,128)S(1)}, bf16[2...) custom-call(f32[2,4,2,24,512]{4,3,2,1,0:T(8,128)} %refs_0_.1, ...), custom_call_target="tpu_custom_call" | custom-call | flops 1048576 | bytes 1024 | tf_op jit(solution)/shard_map/pallas_call | solution.py:29
  7.0 3.1 %collective-permute-start = (f32[2,3,4,1,24,128]{5,4,3,2,1,0:T(8,128)S(1)}, f32[2,3,4,1,24,128]{5,4,3,2,1,0:T(8,128)S(1)}, u32[]{:S(2)}, u32[]{:S(2)}) collective-permute-start(f32[2,3,4,1,24,128]{5,4,3,2,1,0:T(8,128)S(1)} %get-tuple-element.43), channel_id=1, source_target_pairs={{0,1},{1,0},{2,3},{3,2},{4,5},{5,4},{6,7},{7,6},{8,9},{9,8},{10,11... | collective-permute-start | bytes 884744 | tf_op jit(solution)/shard_map/ppermute | solution.py:329
  10.1 5.1 %shard_map.86 = (f32[2,3,4,1,24,128]{5,4,3,2,1,0:T(8,128)S(1)}, f32[2,3,4,1,24,128]{5,4,3,2,1,0:T(8,128)}, f32[2,4,1,24,128]{4,3,2,1,0:T(8,128)S(1)}) custom-call(f32[2,3,4,1,24,128]{5,4,3,2,1,0:T(8,128)S(1)} %get-tuple-element.37.refs_0_.refs_1_, f32[2,4,2,24,512]{4,3,2,1,0:T(8,128)S(1)} %get-tuple-element.38.refs_1_, ...), custom_call_target="tpu_custom_call" | custom-call | flops 1048576 | bytes 1024 | tf_op jit(solution)/shard_map/pallas_call | solution.py:29
  15.2 2.0 %collective-permute-done.refs_2_ = f32[2,3,4,1,24,128]{5,4,3,2,1,0:T(8,128)S(1)} collective-permute-done((f32[2,3,4,1,24,128]{5,4,3,2,1,0:T(8,128)S(1)}, f32[2,3,4,1,24,128]{5,4,3,2,1,0:T(8,128)S(1)}, u32[]{:S(2)}, u32[]{:S(2)}) %collective-permute-start) | collective-permute-done | bytes 294944 | tf_op jit(solution)/shard_map/ppermute | solution.py:329
  17.3 0.7 shard_map.87
  18.0 2.6 %collective-permute-start.2 = (f32[1,3,4,1,24,128]{5,4,3,2,1,0:T(8,128)}, f32[1,3,4,1,24,128]{5,4,3,2,1,0:T(8,128)S(1)}, u32[]{:S(2)}, u32[]{:S(2)}) collective-permute-start(f32[1,3,4,1,24,128]{5,4,3,2,1,0:T(8,128)} %get-tuple-element.47), channel_id=1, source_target_pairs={{0,2},{1,3},{2,0},{3,1},{4,6},{5,7},{6,4},{7,5},{8,10},{9,11},{10,... | collective-permute-start | bytes 442376 | tf_op jit(solution)/shard_map/ppermute | solution.py:329
  20.6 0.7 constant_dynamic-slice_fusion.refs_2_.refs_0_
  21.3 5.8 %collective-permute-done.1.refs_2_ = f32[2,3,4,1,24,128]{5,4,3,2,1,0:T(8,128)S(1)} collective-permute-done((f32[2,3,4,1,24,128]{5,4,3,2,1,0:T(8,128)}, f32[2,3,4,1,24,128]{5,4,3,2,1,0:T(8,128)S(1)}, u32[]{:S(2)}, u32[]{:S(2)}) %collective-permute-start.1) | collective-permute-done | bytes 294944 | tf_op jit(solution)/shard_map/ppermute | solution.py:329
  27.2 0.1 shard_map.89
  27.3 2.3 %collective-permute-start.4 = (f32[1,2,4,1,24,128]{5,4,2,1,3,0:T(8,128)S(1)}, f32[1,2,4,1,24,128]{5,4,2,1,3,0:T(8,128)S(1)}, u32[]{:S(2)}, u32[]{:S(2)}) collective-permute-start(f32[1,2,4,1,24,128]{5,4,2,1,3,0:T(8,128)S(1)} %bitcast.12), channel_id=1, source_target_pairs={{0,2},{1,3},{2,0},{3,1},{4,6},{5,7},{6,4},{7,5},{8,10},{9,11},{10,... | collective-permute-start | bytes 294920 | tf_op jit(solution)/shard_map/ppermute | solution.py:329
  29.6 4.0 %collective-permute-done.4 = f32[1,2,4,1,24,128]{5,4,2,1,3,0:T(8,128)S(1)} collective-permute-done((f32[1,2,4,1,24,128]{5,4,2,1,3,0:T(8,128)S(1)}, f32[1,2,4,1,24,128]{5,4,2,1,3,0:T(8,128)S(1)}, u32[]{:S(2)}, u32[]{:S(2)}) %collective-permute-start.4) | collective-permute-done | bytes 98336 | tf_op jit(solution)/shard_map/ppermute | solution.py:329
  33.6 1.9 %collective-permute-start.5 = (f32[2,2,4,1,24,128]{5,4,3,2,1,0:T(8,128)S(1)}, f32[2,2,4,1,24,128]{5,4,3,2,1,0:T(8,128)S(1)}, u32[]{:S(2)}, u32[]{:S(2)}) collective-permute-start(f32[2,2,4,1,24,128]{5,4,3,2,1,0:T(8,128)S(1)} %maximum_bitcast_fusion.refs_1_), channel_id=1, source_target_pairs={{0,1},{1,0},{2,3},{3,2},{4,5},{5,4},{6,7},{7,6},{8,9},{9,8},{10,11... | collective-permute-start | bytes 589832 | tf_op jit(solution)/shard_map/ppermute | solution.py:329
  35.5 2.2 %collective-permute-start.3 = (f32[1,3,4,1,24,128]{5,4,3,2,1,0:T(8,128)S(1)}, f32[1,3,4,1,24,128]{5,4,3,2,1,0:T(8,128)S(1)}, u32[]{:S(2)}, u32[]{:S(2)}) collective-permute-start(f32[1,3,4,1,24,128]{5,4,3,2,1,0:T(8,128)S(1)} %get-tuple-element.51), channel_id=1, source_target_pairs={{0,2},{1,3},{2,0},{3,1},{4,6},{5,7},{6,4},{7,5},{8,10},{9,11},{10,... | collective-permute-start | bytes 442376 | tf_op jit(solution)/shard_map/ppermute | solution.py:329
  37.7 5.5 %collective-permute-done.3.refs_5_ = f32[1,3,4,1,24,128]{5,4,3,2,1,0:T(8,128)S(1)} collective-permute-done((f32[1,3,4,1,24,128]{5,4,3,2,1,0:T(8,128)S(1)}, f32[1,3,4,1,24,128]{5,4,3,2,1,0:T(8,128)S(1)}, u32[]{:S(2)}, u32[]{:S(2)}) %collective-permute-start.3) | collective-permute-done | bytes 147488 | tf_op jit(solution)/shard_map/ppermute | solution.py:329
  43.2 0.1 shard_map.90
  43.4 0.4 collective-permute-start.6
  43.7 1.0 %collective-permute-start.7 = (f32[1,2,4,1,24,128]{5,4,3,2,1,0:T(8,128)S(1)}, f32[1,2,4,1,24,128]{5,4,3,2,1,0:T(8,128)S(1)}, u32[]{:S(2)}, u32[]{:S(2)}) collective-permute-start(f32[1,2,4,1,24,128]{5,4,3,2,1,0:T(8,128)S(1)} %bitcast.9), channel_id=1, source_target_pairs={{0,2},{1,3},{2,0},{3,1},{4,6},{5,7},{6,4},{7,5},{8,10},{9,11},{10,... | collective-permute-start | bytes 294920 | tf_op jit(solution)/shard_map/ppermute | solution.py:329
  44.7 3.1 %collective-permute-start.8 = (f32[1,2,4,1,24,128]{5,4,3,2,1,0:T(8,128)S(1)}, f32[1,2,4,1,24,128]{5,4,3,2,1,0:T(8,128)S(1)}, u32[]{:S(2)}, u32[]{:S(2)}) collective-permute-start(f32[1,2,4,1,24,128]{5,4,3,2,1,0:T(8,128)S(1)} %bitcast.10), channel_id=1, source_target_pairs={{0,3},{1,2},{2,1},{3,0},{4,7},{5,6},{6,5},{7,4},{8,11},{9,10},{10,... | collective-permute-start | bytes 294920 | tf_op jit(solution)/shard_map/ppermute | solution.py:329
  47.8 0.5 shard_map.91.refs_0_.refs_5_.refs_7_
  48.3 4.6 %shard_map.92 = (f32[2,3,4,1,24,128]{5,4,3,2,1,0:T(8,128)S(1)}, f32[2,3,4,1,24,128]{5,4,3,2,1,0:T(8,128)S(1)}) custom-call(bf16[2,512,2048]{2,1,0:T(8,128)(2,1)S(1)} %shard_map.91.refs_0_.refs_5_.refs_7_, f32[2,2,4,1,24,128]{5,4,3,2,1,0:T(8,128)S(1)} %maximum_bitcast_fusion.refs_1_, f32[2,2,4,1,24,128]{5,4,3,2,1,0:T(8,128)S(1)} %collective-permute-done.5.refs_2_, ...), custom_call_target="tpu_custom_call" | custom-call | flops 1048576 | bytes 1024 | tf_op jit(solution)/shard_map/pallas_call | solution.py:29
  52.9 0.1 collective-permute-start.9
  53.1 4.4 %shard_map.93 = (f32[2,3,4,1,24,128]{5,4,3,2,1,0:T(8,128)S(1)}, f32[2,3,4,1,24,128]{5,4,3,2,1,0:T(8,128)S(1)}) custom-call(f32[2,3,4,1,24,128]{5,4,3,2,1,0:T(8,128)S(1)} %get-tuple-element.54.refs_0_.refs_1_, f32[1,2,4,1,24,128]{5,4,3,2,1,0:T(8,128)S(1)} %bitcast.11, f32[1,2,4,1,24,128]{5,4,3,2,1,0:T(8,128)S(1)} %collective-permute-done.6.refs_2_, ...), custom_call_target="tpu_custom_call" | custom-call | flops 1048576 | bytes 1024 | tf_op jit(solution)/shard_map/pallas_call | solution.py:29
  57.4 2.1 %collective-permute-start.12 = (f32[2,3,4,1,24,128]{5,4,3,2,1,0:T(8,128)S(1)}, f32[2,3,4,1,24,128]{5,4,3,2,1,0:T(8,128)S(1)}, u32[]{:S(2)}, u32[]{:S(2)}) collective-permute-start(f32[2,3,4,1,24,128]{5,4,3,2,1,0:T(8,128)S(1)} %get-tuple-element.59), channel_id=1, source_target_pairs={{0,1},{1,0},{2,3},{3,2},{4,5},{5,4},{6,7},{7,6},{8,9},{9,8},{10,11... | collective-permute-start | bytes 884744 | tf_op jit(solution)/shard_map/ppermute | solution.py:329
  59.5 2.2 %collective-permute-done.9.refs_2_ = f32[2,3,4,1,24,128]{5,4,3,2,1,0:T(8,128)S(1)} collective-permute-done((f32[2,3,4,1,24,128]{5,4,3,2,1,0:T(8,128)S(1)}, f32[2,3,4,1,24,128]{5,4,3,2,1,0:T(8,128)S(1)}, u32[]{:S(2)}, u32[]{:S(2)}) %collective-permute-start.9) | collective-permute-done | bytes 294944 | tf_op jit(solution)/shard_map/ppermute | solution.py:329
  61.7 1.3 %collective-permute-start.13 = (f32[1,3,4,1,24,128]{5,4,3,2,1,0:T(8,128)S(1)}, f32[1,3,4,1,24,128]{5,4,3,2,1,0:T(8,128)S(1)}, u32[]{:S(2)}, u32[]{:S(2)}) collective-permute-start(f32[1,3,4,1,24,128]{5,4,3,2,1,0:T(8,128)S(1)} %get-tuple-element.61), channel_id=1, source_target_pairs={{0,2},{1,3},{2,0},{3,1},{4,6},{5,7},{6,4},{7,5},{8,10},{9,11},{10,... | collective-permute-start | bytes 442376 | tf_op jit(solution)/shard_map/ppermute | solution.py:329
  63.1 1.3 %collective-permute-start.11 = (f32[2,4,2,4,128]{4,3,2,1,0:T(4,128)S(1)}, f32[2,4,2,4,128]{4,3,2,1,0:T(4,128)S(1)}, u32[]{:S(2)}, u32[]{:S(2)}) collective-permute-start(f32[2,4,2,4,128]{4,3,2,1,0:T(4,128)S(1)} %add.22), channel_id=1, source_target_pairs={{0,8},{4,12},{8,0},{12,4},{16,24},{20,28},{24,16},{28,20},{1,9},{5... | collective-permute-start | bytes 98312 | tf_op jit(solution)/shard_map/ppermute | solution.py:329
  64.4 2.6 %collective-permute-done.11 = f32[2,4,2,4,128]{4,3,2,1,0:T(4,128)S(1)} collective-permute-done((f32[2,4,2,4,128]{4,3,2,1,0:T(4,128)S(1)}, f32[2,4,2,4,128]{4,3,2,1,0:T(4,128)S(1)}, u32[]{:S(2)}, u32[]{:S(2)}) %collective-permute-start.11) | collective-permute-done | bytes 32800 | tf_op jit(solution)/shard_map/ppermute | solution.py:329
  67.1 1.8 %collective-permute-start.15 = (f32[1,3,4,1,24,128]{5,4,3,2,1,0:T(8,128)S(1)}, f32[1,3,4,1,24,128]{5,4,3,2,1,0:T(8,128)S(1)}, u32[]{:S(2)}, u32[]{:S(2)}) collective-permute-start(f32[1,3,4,1,24,128]{5,4,3,2,1,0:T(8,128)S(1)} %get-tuple-element.66), channel_id=1, source_target_pairs={{0,2},{1,3},{2,0},{3,1},{4,6},{5,7},{6,4},{7,5},{8,10},{9,11},{10,... | collective-permute-start | bytes 442376 | tf_op jit(solution)/shard_map/ppermute | solution.py:329
  68.9 1.3 %collective-permute-start.14 = (f32[2,4,2,4,128]{4,3,2,1,0:T(4,128)S(1)}, f32[2,4,2,4,128]{4,3,2,1,0:T(4,128)S(1)}, u32[]{:S(2)}, u32[]{:S(2)}) collective-permute-start(f32[2,4,2,4,128]{4,3,2,1,0:T(4,128)S(1)} %add.23.refs_1_), channel_id=1, source_target_pairs={{0,16},{4,20},{8,24},{12,28},{16,0},{20,4},{24,8},{28,12},{1,17},{... | collective-permute-start | bytes 98312 | tf_op jit(solution)/shard_map/ppermute | solution.py:329
  70.2 2.6 %collective-permute-done.14 = f32[2,4,2,4,128]{4,3,2,1,0:T(4,128)S(1)} collective-permute-done((f32[2,4,2,4,128]{4,3,2,1,0:T(4,128)S(1)}, f32[2,4,2,4,128]{4,3,2,1,0:T(4,128)S(1)}, u32[]{:S(2)}, u32[]{:S(2)}) %collective-permute-start.14) | collective-permute-done | bytes 32800 | tf_op jit(solution)/shard_map/ppermute | solution.py:329
  72.8 0.1 shard_map.96
  72.9 0.1 shard_map.97
  73.1 1.3 %collective-permute-start.17 = (f32[1,2,4,1,24,128]{5,4,3,2,1,0:T(8,128)S(1)}, f32[1,2,4,1,24,128]{5,4,3,2,1,0:T(8,128)S(1)}, u32[]{:S(2)}, u32[]{:S(2)}) collective-permute-start(f32[1,2,4,1,24,128]{5,4,3,2,1,0:T(8,128)S(1)} %bitcast.14), channel_id=1, source_target_pairs={{0,2},{1,3},{2,0},{3,1},{4,6},{5,7},{6,4},{7,5},{8,10},{9,11},{10,... | collective-permute-start | bytes 294920 | tf_op jit(solution)/shard_map/ppermute | solution.py:329
  74.4 3.3 %collective-permute-done.15.refs_5_ = f32[1,3,4,1,24,128]{5,4,3,2,1,0:T(8,128)S(1)} collective-permute-done((f32[1,3,4,1,24,128]{5,4,3,2,1,0:T(8,128)S(1)}, f32[1,3,4,1,24,128]{5,4,3,2,1,0:T(8,128)S(1)}, u32[]{:S(2)}, u32[]{:S(2)}) %collective-permute-start.15) | collective-permute-done | bytes 147488 | tf_op jit(solution)/shard_map/ppermute | solution.py:329
  77.7 0.1 shard_map.98
  77.8 0.1 collective-permute-start.16
  77.9 1.2 %collective-permute-done.16 = f32[2,4,2,4,128]{4,3,2,1,0:T(4,128)S(1)} collective-permute-done((f32[2,4,2,4,128]{4,3,2,1,0:T(4,128)S(1)}, f32[2,4,2,4,128]{4,3,2,1,0:T(4,128)S(1)}, u32[]{:S(2)}, u32[]{:S(2)}) %collective-permute-start.16) | collective-permute-done | bytes 32800 | tf_op jit(solution)/shard_map/ppermute | solution.py:329
  79.1 1.1 %collective-permute-done.17.refs_2_ = f32[1,2,4,1,24,128]{5,4,3,2,1,0:T(8,128)S(1)} collective-permute-done((f32[1,2,4,1,24,128]{5,4,3,2,1,0:T(8,128)S(1)}, f32[1,2,4,1,24,128]{5,4,3,2,1,0:T(8,128)S(1)}, u32[]{:S(2)}, u32[]{:S(2)}) %collective-permute-start.17) | collective-permute-done | bytes 98336 | tf_op jit(solution)/shard_map/ppermute | solution.py:329
  80.3 0.1 collective-permute-start.18
  80.4 2.0 %collective-permute-start.19 = (f32[1,2,4,1,24,128]{5,4,3,2,1,0:T(8,128)S(1)}, f32[1,2,4,1,24,128]{5,4,3,2,1,0:T(8,128)S(1)}, u32[]{:S(2)}, u32[]{:S(2)}) collective-permute-start(f32[1,2,4,1,24,128]{5,4,3,2,1,0:T(8,128)S(1)} %bitcast.16), channel_id=1, source_target_pairs={{0,1},{1,0},{2,3},{3,2},{4,5},{5,4},{6,7},{7,6},{8,9},{9,8},{10,11... | collective-permute-start | bytes 294920 | tf_op jit(solution)/shard_map/ppermute | solution.py:329
  82.4 0.1 collective-permute-start.20
  82.5 2.3 %collective-permute-start.21 = (f32[1,2,4,1,24,128]{5,4,3,2,1,0:T(8,128)S(1)}, f32[1,2,4,1,24,128]{5,4,3,2,1,0:T(8,128)S(1)}, u32[]{:S(2)}, u32[]{:S(2)}) collective-permute-start(f32[1,2,4,1,24,128]{5,4,3,2,1,0:T(8,128)S(1)} %bitcast.18), channel_id=1, source_target_pairs={{0,3},{1,2},{2,1},{3,0},{4,7},{5,6},{6,5},{7,4},{8,11},{9,10},{10,... | collective-permute-start | bytes 294920 | tf_op jit(solution)/shard_map/ppermute | solution.py:329
  84.8 1.3 %collective-permute-start.22 = (f32[2,4,2,4,128]{4,3,2,1,0:T(4,128)S(1)}, f32[2,4,2,4,128]{4,3,2,1,0:T(4,128)S(1)}, u32[]{:S(2)}, u32[]{:S(2)}) collective-permute-start(f32[2,4,2,4,128]{4,3,2,1,0:T(4,128)S(1)} %add.25.refs_0_), channel_id=1, source_target_pairs={{0,8},{4,12},{8,0},{12,4},{16,24},{20,28},{24,16},{28,20},{1,9},{5... | collective-permute-start | bytes 98312 | tf_op jit(solution)/shard_map/ppermute | solution.py:329
  86.1 2.6 %collective-permute-done.22 = f32[2,4,2,4,128]{4,3,2,1,0:T(4,128)S(1)} collective-permute-done((f32[2,4,2,4,128]{4,3,2,1,0:T(4,128)S(1)}, f32[2,4,2,4,128]{4,3,2,1,0:T(4,128)S(1)}, u32[]{:S(2)}, u32[]{:S(2)}) %collective-permute-start.22) | collective-permute-done | bytes 32800 | tf_op jit(solution)/shard_map/ppermute | solution.py:329
  88.7 1.4 %collective-permute-start.23 = (f32[2,4,2,4,128]{4,3,2,1,0:T(4,128)S(1)}, f32[2,4,2,4,128]{4,3,2,1,0:T(4,128)S(1)}, u32[]{:S(2)}, u32[]{:S(2)}) collective-permute-start(f32[2,4,2,4,128]{4,3,2,1,0:T(4,128)S(1)} %add.26), channel_id=1, source_target_pairs={{0,16},{4,20},{8,24},{12,28},{16,0},{20,4},{24,8},{28,12},{1,17},{... | collective-permute-start | bytes 98312 | tf_op jit(solution)/shard_map/ppermute | solution.py:329
  90.1 2.6 %collective-permute-done.23 = f32[2,4,2,4,128]{4,3,2,1,0:T(4,128)S(1)} collective-permute-done((f32[2,4,2,4,128]{4,3,2,1,0:T(4,128)S(1)}, f32[2,4,2,4,128]{4,3,2,1,0:T(4,128)S(1)}, u32[]{:S(2)}, u32[]{:S(2)}) %collective-permute-start.23) | collective-permute-done | bytes 32800 | tf_op jit(solution)/shard_map/ppermute | solution.py:329
  92.7 0.9 shard_map.101
  93.6 1.0 %shard_map.100 = f32[2,4,2,24,512]{4,3,2,1,0:T(8,128)} custom-call(f32[2,2,4,1,24,128]{5,4,3,2,1,0:T(8,128)S(1)} %shard_map.99.refs_0_, f32[2,2,4,1,24,128]{5,4,3,2,1,0:T(8,128)S(1)} %collective-permute-done.18.refs_1_, f32[1,2,4,1,24,128]{5,4,3,2,1,0:T(8,128)S(1)} %bitcast.19, f32[1,2,4,1,24,128]{5,4,3,2,1,0:T(8,128)S(1)} %collective-permute-done.19.refs_3_, ...), custom_call_target="tpu_custom_call" | custom-call | flops 1048576 | bytes 1024 | tf_op jit(solution)/shard_map/pallas_call | solution.py:29
  (31 shorter events, 0.3 us)
Async XLA Ops:
  7.0 10.3 %collective-permute-start = (f32[2,3,4,1,24,128]{5,4,3,2,1,0:T(8,128)S(1)}, f32[2,3,4,1,24,128]{5,4,3,2,1,0:T(8,128)S(1)}, u32[]{:S(2)}, u32[]{:S(2)}) collective-permute-start(f32[2,3,4,1,24,128]{5,4,3,2,1,0:T(8,128)S(1)} %get-tuple-element.43), channel_id=1, source_target_pairs={{0,1},{1,0},{2,3},{3,2},{4,5},{5,4},{6,7},{7,6},{8,9},{9,8},{10,11... | collective-permute-start | bytes 884744 | tf_op jit(solution)/shard_map/ppermute | solution.py:329
  10.1 17.0 %copy-start.1 = (f32[4]{0:T(128)S(1)}, f32[4]{0:T(128)}, u32[]{:S(2)}) copy-start(f32[4]{0:T(128)} %param.9) | copy-start | bytes 52
  10.1 37.7 %copy-start = (s32[2,2048]{1,0:T(2,128)S(1)}, s32[2,2048]{1,0:T(2,128)}, u32[]{:S(2)}) copy-start(s32[2,2048]{1,0:T(2,128)} %refs_1_.3) | copy-start | bytes 49156
  15.2 11.8 %collective-permute-start.1 = (f32[2,3,4,1,24,128]{5,4,3,2,1,0:T(8,128)}, f32[2,3,4,1,24,128]{5,4,3,2,1,0:T(8,128)S(1)}, u32[]{:S(2)}, u32[]{:S(2)}) collective-permute-start(f32[2,3,4,1,24,128]{5,4,3,2,1,0:T(8,128)} %get-tuple-element.45), channel_id=1, source_target_pairs={{0,1},{1,0},{2,3},{3,2},{4,5},{5,4},{6,7},{7,6},{8,9},{9,8},{10,11... | collective-permute-start | bytes 884744 | tf_op jit(solution)/shard_map/ppermute | solution.py:329
  18.0 9.1 %collective-permute-start.2 = (f32[1,3,4,1,24,128]{5,4,3,2,1,0:T(8,128)}, f32[1,3,4,1,24,128]{5,4,3,2,1,0:T(8,128)S(1)}, u32[]{:S(2)}, u32[]{:S(2)}) collective-permute-start(f32[1,3,4,1,24,128]{5,4,3,2,1,0:T(8,128)} %get-tuple-element.47), channel_id=1, source_target_pairs={{0,2},{1,3},{2,0},{3,1},{4,6},{5,7},{6,4},{7,5},{8,10},{9,11},{10,... | collective-permute-start | bytes 442376 | tf_op jit(solution)/shard_map/ppermute | solution.py:329
  27.3 6.3 %collective-permute-start.4 = (f32[1,2,4,1,24,128]{5,4,2,1,3,0:T(8,128)S(1)}, f32[1,2,4,1,24,128]{5,4,2,1,3,0:T(8,128)S(1)}, u32[]{:S(2)}, u32[]{:S(2)}) collective-permute-start(f32[1,2,4,1,24,128]{5,4,2,1,3,0:T(8,128)S(1)} %bitcast.12), channel_id=1, source_target_pairs={{0,2},{1,3},{2,0},{3,1},{4,6},{5,7},{6,4},{7,5},{8,10},{9,11},{10,... | collective-permute-start | bytes 294920 | tf_op jit(solution)/shard_map/ppermute | solution.py:329
  33.6 14.7 %collective-permute-start.5 = (f32[2,2,4,1,24,128]{5,4,3,2,1,0:T(8,128)S(1)}, f32[2,2,4,1,24,128]{5,4,3,2,1,0:T(8,128)S(1)}, u32[]{:S(2)}, u32[]{:S(2)}) collective-permute-start(f32[2,2,4,1,24,128]{5,4,3,2,1,0:T(8,128)S(1)} %maximum_bitcast_fusion.refs_1_), channel_id=1, source_target_pairs={{0,1},{1,0},{2,3},{3,2},{4,5},{5,4},{6,7},{7,6},{8,9},{9,8},{10,11... | collective-permute-start | bytes 589832 | tf_op jit(solution)/shard_map/ppermute | solution.py:329
  35.5 7.7 %collective-permute-start.3 = (f32[1,3,4,1,24,128]{5,4,3,2,1,0:T(8,128)S(1)}, f32[1,3,4,1,24,128]{5,4,3,2,1,0:T(8,128)S(1)}, u32[]{:S(2)}, u32[]{:S(2)}) collective-permute-start(f32[1,3,4,1,24,128]{5,4,3,2,1,0:T(8,128)S(1)} %get-tuple-element.51), channel_id=1, source_target_pairs={{0,2},{1,3},{2,0},{3,1},{4,6},{5,7},{6,4},{7,5},{8,10},{9,11},{10,... | collective-permute-start | bytes 442376 | tf_op jit(solution)/shard_map/ppermute | solution.py:329
  43.4 9.7 %collective-permute-start.6 = (f32[1,2,4,1,24,128]{5,4,3,2,1,0:T(8,128)S(1)}, f32[1,2,4,1,24,128]{5,4,3,2,1,0:T(8,128)S(1)}, u32[]{:S(2)}, u32[]{:S(2)}) collective-permute-start(f32[1,2,4,1,24,128]{5,4,3,2,1,0:T(8,128)S(1)} %bitcast.8), channel_id=1, source_target_pairs={{0,1},{1,0},{2,3},{3,2},{4,5},{5,4},{6,7},{7,6},{8,9},{9,8},{10,11... | collective-permute-start | bytes 294920 | tf_op jit(solution)/shard_map/ppermute | solution.py:329
  43.7 9.3 %collective-permute-start.7 = (f32[1,2,4,1,24,128]{5,4,3,2,1,0:T(8,128)S(1)}, f32[1,2,4,1,24,128]{5,4,3,2,1,0:T(8,128)S(1)}, u32[]{:S(2)}, u32[]{:S(2)}) collective-permute-start(f32[1,2,4,1,24,128]{5,4,3,2,1,0:T(8,128)S(1)} %bitcast.9), channel_id=1, source_target_pairs={{0,2},{1,3},{2,0},{3,1},{4,6},{5,7},{6,4},{7,5},{8,10},{9,11},{10,... | collective-permute-start | bytes 294920 | tf_op jit(solution)/shard_map/ppermute | solution.py:329
  44.7 8.3 %collective-permute-start.8 = (f32[1,2,4,1,24,128]{5,4,3,2,1,0:T(8,128)S(1)}, f32[1,2,4,1,24,128]{5,4,3,2,1,0:T(8,128)S(1)}, u32[]{:S(2)}, u32[]{:S(2)}) collective-permute-start(f32[1,2,4,1,24,128]{5,4,3,2,1,0:T(8,128)S(1)} %bitcast.10), channel_id=1, source_target_pairs={{0,3},{1,2},{2,1},{3,0},{4,7},{5,6},{6,5},{7,4},{8,11},{9,10},{10,... | collective-permute-start | bytes 294920 | tf_op jit(solution)/shard_map/ppermute | solution.py:329
  52.9 8.8 %collective-permute-start.9 = (f32[2,3,4,1,24,128]{5,4,3,2,1,0:T(8,128)S(1)}, f32[2,3,4,1,24,128]{5,4,3,2,1,0:T(8,128)S(1)}, u32[]{:S(2)}, u32[]{:S(2)}) collective-permute-start(f32[2,3,4,1,24,128]{5,4,3,2,1,0:T(8,128)S(1)} %get-tuple-element.56), channel_id=1, source_target_pairs={{0,1},{1,0},{2,3},{3,2},{4,5},{5,4},{6,7},{7,6},{8,9},{9,8},{10,11... | collective-permute-start | bytes 884744 | tf_op jit(solution)/shard_map/ppermute | solution.py:329
  57.4 9.6 %collective-permute-start.12 = (f32[2,3,4,1,24,128]{5,4,3,2,1,0:T(8,128)S(1)}, f32[2,3,4,1,24,128]{5,4,3,2,1,0:T(8,128)S(1)}, u32[]{:S(2)}, u32[]{:S(2)}) collective-permute-start(f32[2,3,4,1,24,128]{5,4,3,2,1,0:T(8,128)S(1)} %get-tuple-element.59), channel_id=1, source_target_pairs={{0,1},{1,0},{2,3},{3,2},{4,5},{5,4},{6,7},{7,6},{8,9},{9,8},{10,11... | collective-permute-start | bytes 884744 | tf_op jit(solution)/shard_map/ppermute | solution.py:329
  59.5 3.5 %collective-permute-start.10 = (f32[2,4,2,4,128]{4,3,2,1,0:T(4,128)S(1)}, f32[2,4,2,4,128]{4,3,2,1,0:T(4,128)S(1)}, u32[]{:S(2)}, u32[]{:S(2)}) collective-permute-start(f32[2,4,2,4,128]{4,3,2,1,0:T(4,128)S(1)} %get-tuple-element.58), channel_id=1, source_target_pairs={{0,4},{4,0},{8,12},{12,8},{16,20},{20,16},{24,28},{28,24},{1,5},{5... | collective-permute-start | bytes 98312 | tf_op jit(solution)/shard_map/ppermute | solution.py:329
  61.7 11.2 %collective-permute-start.13 = (f32[1,3,4,1,24,128]{5,4,3,2,1,0:T(8,128)S(1)}, f32[1,3,4,1,24,128]{5,4,3,2,1,0:T(8,128)S(1)}, u32[]{:S(2)}, u32[]{:S(2)}) collective-permute-start(f32[1,3,4,1,24,128]{5,4,3,2,1,0:T(8,128)S(1)} %get-tuple-element.61), channel_id=1, source_target_pairs={{0,2},{1,3},{2,0},{3,1},{4,6},{5,7},{6,4},{7,5},{8,10},{9,11},{10,... | collective-permute-start | bytes 442376 | tf_op jit(solution)/shard_map/ppermute | solution.py:329
  63.1 4.0 %collective-permute-start.11 = (f32[2,4,2,4,128]{4,3,2,1,0:T(4,128)S(1)}, f32[2,4,2,4,128]{4,3,2,1,0:T(4,128)S(1)}, u32[]{:S(2)}, u32[]{:S(2)}) collective-permute-start(f32[2,4,2,4,128]{4,3,2,1,0:T(4,128)S(1)} %add.22), channel_id=1, source_target_pairs={{0,8},{4,12},{8,0},{12,4},{16,24},{20,28},{24,16},{28,20},{1,9},{5... | collective-permute-start | bytes 98312 | tf_op jit(solution)/shard_map/ppermute | solution.py:329
  67.1 10.6 %collective-permute-start.15 = (f32[1,3,4,1,24,128]{5,4,3,2,1,0:T(8,128)S(1)}, f32[1,3,4,1,24,128]{5,4,3,2,1,0:T(8,128)S(1)}, u32[]{:S(2)}, u32[]{:S(2)}) collective-permute-start(f32[1,3,4,1,24,128]{5,4,3,2,1,0:T(8,128)S(1)} %get-tuple-element.66), channel_id=1, source_target_pairs={{0,2},{1,3},{2,0},{3,1},{4,6},{5,7},{6,4},{7,5},{8,10},{9,11},{10,... | collective-permute-start | bytes 442376 | tf_op jit(solution)/shard_map/ppermute | solution.py:329
  68.9 3.9 %collective-permute-start.14 = (f32[2,4,2,4,128]{4,3,2,1,0:T(4,128)S(1)}, f32[2,4,2,4,128]{4,3,2,1,0:T(4,128)S(1)}, u32[]{:S(2)}, u32[]{:S(2)}) collective-permute-start(f32[2,4,2,4,128]{4,3,2,1,0:T(4,128)S(1)} %add.23.refs_1_), channel_id=1, source_target_pairs={{0,16},{4,20},{8,24},{12,28},{16,0},{20,4},{24,8},{28,12},{1,17},{... | collective-permute-start | bytes 98312 | tf_op jit(solution)/shard_map/ppermute | solution.py:329
  73.1 7.2 %collective-permute-start.17 = (f32[1,2,4,1,24,128]{5,4,3,2,1,0:T(8,128)S(1)}, f32[1,2,4,1,24,128]{5,4,3,2,1,0:T(8,128)S(1)}, u32[]{:S(2)}, u32[]{:S(2)}) collective-permute-start(f32[1,2,4,1,24,128]{5,4,3,2,1,0:T(8,128)S(1)} %bitcast.14), channel_id=1, source_target_pairs={{0,2},{1,3},{2,0},{3,1},{4,6},{5,7},{6,4},{7,5},{8,10},{9,11},{10,... | collective-permute-start | bytes 294920 | tf_op jit(solution)/shard_map/ppermute | solution.py:329
  77.8 1.3 %collective-permute-start.16 = (f32[2,4,2,4,128]{4,3,2,1,0:T(4,128)S(1)}, f32[2,4,2,4,128]{4,3,2,1,0:T(4,128)S(1)}, u32[]{:S(2)}, u32[]{:S(2)}) collective-permute-start(f32[2,4,2,4,128]{4,3,2,1,0:T(4,128)S(1)} %get-tuple-element.67), channel_id=1, source_target_pairs={{0,4},{4,0},{8,12},{12,8},{16,20},{20,16},{24,28},{28,24},{1,5},{5... | collective-permute-start | bytes 98312 | tf_op jit(solution)/shard_map/ppermute | solution.py:329
  80.3 13.3 %collective-permute-start.18 = (f32[2,2,4,1,24,128]{5,4,3,2,1,0:T(8,128)S(1)}, f32[2,2,4,1,24,128]{5,4,3,2,1,0:T(8,128)S(1)}, u32[]{:S(2)}, u32[]{:S(2)}) collective-permute-start(f32[2,2,4,1,24,128]{5,4,3,2,1,0:T(8,128)S(1)} %shard_map.99.refs_0_), channel_id=1, source_target_pairs={{0,1},{1,0},{2,3},{3,2},{4,5},{5,4},{6,7},{7,6},{8,9},{9,8},{10,11... | collective-permute-start | bytes 589832 | tf_op jit(solution)/shard_map/ppermute | solution.py:329
  80.4 13.3 %collective-permute-start.19 = (f32[1,2,4,1,24,128]{5,4,3,2,1,0:T(8,128)S(1)}, f32[1,2,4,1,24,128]{5,4,3,2,1,0:T(8,128)S(1)}, u32[]{:S(2)}, u32[]{:S(2)}) collective-permute-start(f32[1,2,4,1,24,128]{5,4,3,2,1,0:T(8,128)S(1)} %bitcast.16), channel_id=1, source_target_pairs={{0,1},{1,0},{2,3},{3,2},{4,5},{5,4},{6,7},{7,6},{8,9},{9,8},{10,11... | collective-permute-start | bytes 294920 | tf_op jit(solution)/shard_map/ppermute | solution.py:329
  82.4 11.2 %collective-permute-start.20 = (f32[1,2,4,1,24,128]{5,4,3,2,1,0:T(8,128)S(1)}, f32[1,2,4,1,24,128]{5,4,3,2,1,0:T(8,128)S(1)}, u32[]{:S(2)}, u32[]{:S(2)}) collective-permute-start(f32[1,2,4,1,24,128]{5,4,3,2,1,0:T(8,128)S(1)} %bitcast.17), channel_id=1, source_target_pairs={{0,2},{1,3},{2,0},{3,1},{4,6},{5,7},{6,4},{7,5},{8,10},{9,11},{10,... | collective-permute-start | bytes 294920 | tf_op jit(solution)/shard_map/ppermute | solution.py:329
  82.5 11.1 %collective-permute-start.21 = (f32[1,2,4,1,24,128]{5,4,3,2,1,0:T(8,128)S(1)}, f32[1,2,4,1,24,128]{5,4,3,2,1,0:T(8,128)S(1)}, u32[]{:S(2)}, u32[]{:S(2)}) collective-permute-start(f32[1,2,4,1,24,128]{5,4,3,2,1,0:T(8,128)S(1)} %bitcast.18), channel_id=1, source_target_pairs={{0,3},{1,2},{2,1},{3,0},{4,7},{5,6},{6,5},{7,4},{8,11},{9,10},{10,... | collective-permute-start | bytes 294920 | tf_op jit(solution)/shard_map/ppermute | solution.py:329
  84.8 3.9 %collective-permute-start.22 = (f32[2,4,2,4,128]{4,3,2,1,0:T(4,128)S(1)}, f32[2,4,2,4,128]{4,3,2,1,0:T(4,128)S(1)}, u32[]{:S(2)}, u32[]{:S(2)}) collective-permute-start(f32[2,4,2,4,128]{4,3,2,1,0:T(4,128)S(1)} %add.25.refs_0_), channel_id=1, source_target_pairs={{0,8},{4,12},{8,0},{12,4},{16,24},{20,28},{24,16},{28,20},{1,9},{5... | collective-permute-start | bytes 98312 | tf_op jit(solution)/shard_map/ppermute | solution.py:329
  88.7 4.0 %collective-permute-start.23 = (f32[2,4,2,4,128]{4,3,2,1,0:T(4,128)S(1)}, f32[2,4,2,4,128]{4,3,2,1,0:T(4,128)S(1)}, u32[]{:S(2)}, u32[]{:S(2)}) collective-permute-start(f32[2,4,2,4,128]{4,3,2,1,0:T(4,128)S(1)} %add.26), channel_id=1, source_target_pairs={{0,16},{4,20},{8,24},{12,28},{16,0},{20,4},{24,8},{28,12},{1,17},{... | collective-permute-start | bytes 98312 | tf_op jit(solution)/shard_map/ppermute | solution.py:329

commit v7 on v6

--- a/solution.py
+++ b/solution.py
@@ -351,7 +351,7 @@
         first = iteration == 0
         parts, fresh = [], []
         if not first:
-            picks = make_picks(line, count, stations, token)
+            picks = make_picks(line, count, stations, [own[0]])
             token = [picks]
         for c, chunk in enumerate(chunks):
             fill = first and c == 0

time: 94.9 us -> 94.9 us (level)
  no operation moved by 1% of the time
where the time goes in v7:
time: 94.9 us; the launch traced here: 94.6 us
  waiting for transfers between devices  35.6 us (38%)
  starting transfers between devices  33 us (35%)
  Pallas kernels  24.3 us (26%)
    ppermute x24, waiting for transfers between devices, swap(): return lax.ppermute(values, axis, [(i, i ^ bit) for i in range(size)])  35.6 us
    ppermute x24, starting transfers between devices, swap(): return lax.ppermute(values, axis, [(i, i ^ bit) for i in range(size)])  33 us
    pallas_call x17, Pallas kernels, run(): pl.pallas_call(lambda *refs: kernel(*refs[count:]), in_specs=[OUTSIDE] *...  24.3 us
  transfers between devices with their start and end apart: 24, of which 12 were waited for; matrix products, arithmetic and copies ran while one was open for 1% of the time, Pallas kernels for 18%

profile of v7, /device:TPU:0, one launch (start us, length us, event | category | flops | bytes accessed | tf_op | source)
XLA Modules:
  0.0 94.6 jit_solution(18321273467165826152)
XLA Ops:
  0.6 6.4 %shard_map.85 = (f32[2,3,4,1,24,128]{5,4,3,2,1,0:T(8,128)S(1)}, f32[2,3,4,1,24,128]{5,4,3,2,1,0:T(8,128)S(1)}, f32[2,4,1,24,128]{4,3,2,1,0:T(8,128)S(1)}, bf16[2...) custom-call(f32[2,4,2,24,512]{4,3,2,1,0:T(8,128)} %refs_0_.1, ...), custom_call_target="tpu_custom_call" | custom-call | flops 1048576 | bytes 1024 | tf_op jit(solution)/shard_map/pallas_call | solution.py:29
  7.0 3.1 %collective-permute-start = (f32[2,3,4,1,24,128]{5,4,3,2,1,0:T(8,128)S(1)}, f32[2,3,4,1,24,128]{5,4,3,2,1,0:T(8,128)S(1)}, u32[]{:S(2)}, u32[]{:S(2)}) collective-permute-start(f32[2,3,4,1,24,128]{5,4,3,2,1,0:T(8,128)S(1)} %get-tuple-element.43), channel_id=1, source_target_pairs={{0,1},{1,0},{2,3},{3,2},{4,5},{5,4},{6,7},{7,6},{8,9},{9,8},{10,11... | collective-permute-start | bytes 884744 | tf_op jit(solution)/shard_map/ppermute | solution.py:329
  10.1 5.1 %shard_map.86 = (f32[2,3,4,1,24,128]{5,4,3,2,1,0:T(8,128)S(1)}, f32[2,3,4,1,24,128]{5,4,3,2,1,0:T(8,128)}, f32[2,4,1,24,128]{4,3,2,1,0:T(8,128)S(1)}) custom-call(f32[2,3,4,1,24,128]{5,4,3,2,1,0:T(8,128)S(1)} %get-tuple-element.37.refs_0_.refs_1_, f32[2,4,2,24,512]{4,3,2,1,0:T(8,128)S(1)} %get-tuple-element.38.refs_1_, ...), custom_call_target="tpu_custom_call" | custom-call | flops 1048576 | bytes 1024 | tf_op jit(solution)/shard_map/pallas_call | solution.py:29
  15.2 2.0 %collective-permute-done.refs_2_ = f32[2,3,4,1,24,128]{5,4,3,2,1,0:T(8,128)S(1)} collective-permute-done((f32[2,3,4,1,24,128]{5,4,3,2,1,0:T(8,128)S(1)}, f32[2,3,4,1,24,128]{5,4,3,2,1,0:T(8,128)S(1)}, u32[]{:S(2)}, u32[]{:S(2)}) %collective-permute-start) | collective-permute-done | bytes 294944 | tf_op jit(solution)/shard_map/ppermute | solution.py:329
  17.3 0.7 shard_map.87
  18.0 2.6 %collective-permute-start.2 = (f32[1,3,4,1,24,128]{5,4,3,2,1,0:T(8,128)}, f32[1,3,4,1,24,128]{5,4,3,2,1,0:T(8,128)S(1)}, u32[]{:S(2)}, u32[]{:S(2)}) collective-permute-start(f32[1,3,4,1,24,128]{5,4,3,2,1,0:T(8,128)} %get-tuple-element.47), channel_id=1, source_target_pairs={{0,2},{1,3},{2,0},{3,1},{4,6},{5,7},{6,4},{7,5},{8,10},{9,11},{10,... | collective-permute-start | bytes 442376 | tf_op jit(solution)/shard_map/ppermute | solution.py:329
  20.6 0.7 constant_dynamic-slice_fusion.refs_2_.refs_0_
  21.3 5.8 %collective-permute-done.1.refs_2_ = f32[2,3,4,1,24,128]{5,4,3,2,1,0:T(8,128)S(1)} collective-permute-done((f32[2,3,4,1,24,128]{5,4,3,2,1,0:T(8,128)}, f32[2,3,4,1,24,128]{5,4,3,2,1,0:T(8,128)S(1)}, u32[]{:S(2)}, u32[]{:S(2)}) %collective-permute-start.1) | collective-permute-done | bytes 294944 | tf_op jit(solution)/shard_map/ppermute | solution.py:329
  27.2 0.1 shard_map.89
  27.3 2.3 %collective-permute-start.3 = (f32[1,2,4,1,24,128]{5,4,2,1,3,0:T(8,128)S(1)}, f32[1,2,4,1,24,128]{5,4,2,1,3,0:T(8,128)S(1)}, u32[]{:S(2)}, u32[]{:S(2)}) collective-permute-start(f32[1,2,4,1,24,128]{5,4,2,1,3,0:T(8,128)S(1)} %bitcast.8), channel_id=1, source_target_pairs={{0,2},{1,3},{2,0},{3,1},{4,6},{5,7},{6,4},{7,5},{8,10},{9,11},{10,... | collective-permute-start | bytes 294920 | tf_op jit(solution)/shard_map/ppermute | solution.py:329
  29.6 4.0 %collective-permute-done.3 = f32[1,2,4,1,24,128]{5,4,2,1,3,0:T(8,128)S(1)} collective-permute-done((f32[1,2,4,1,24,128]{5,4,2,1,3,0:T(8,128)S(1)}, f32[1,2,4,1,24,128]{5,4,2,1,3,0:T(8,128)S(1)}, u32[]{:S(2)}, u32[]{:S(2)}) %collective-permute-start.3) | collective-permute-done | bytes 98336 | tf_op jit(solution)/shard_map/ppermute | solution.py:329
  33.6 1.9 %collective-permute-start.4 = (f32[2,2,4,1,24,128]{5,4,3,2,1,0:T(8,128)S(1)}, f32[2,2,4,1,24,128]{5,4,3,2,1,0:T(8,128)S(1)}, u32[]{:S(2)}, u32[]{:S(2)}) collective-permute-start(f32[2,2,4,1,24,128]{5,4,3,2,1,0:T(8,128)S(1)} %maximum_bitcast_fusion.refs_1_), channel_id=1, source_target_pairs={{0,1},{1,0},{2,3},{3,2},{4,5},{5,4},{6,7},{7,6},{8,9},{9,8},{10,11... | collective-permute-start | bytes 589832 | tf_op jit(solution)/shard_map/ppermute | solution.py:329
  35.5 2.2 %collective-permute-start.5 = (f32[1,3,4,1,24,128]{5,4,3,2,1,0:T(8,128)S(1)}, f32[1,3,4,1,24,128]{5,4,3,2,1,0:T(8,128)S(1)}, u32[]{:S(2)}, u32[]{:S(2)}) collective-permute-start(f32[1,3,4,1,24,128]{5,4,3,2,1,0:T(8,128)S(1)} %get-tuple-element.52), channel_id=1, source_target_pairs={{0,2},{1,3},{2,0},{3,1},{4,6},{5,7},{6,4},{7,5},{8,10},{9,11},{10,... | collective-permute-start | bytes 442376 | tf_op jit(solution)/shard_map/ppermute | solution.py:329
  37.7 5.5 %collective-permute-done.5.refs_5_ = f32[1,3,4,1,24,128]{5,4,3,2,1,0:T(8,128)S(1)} collective-permute-done((f32[1,3,4,1,24,128]{5,4,3,2,1,0:T(8,128)S(1)}, f32[1,3,4,1,24,128]{5,4,3,2,1,0:T(8,128)S(1)}, u32[]{:S(2)}, u32[]{:S(2)}) %collective-permute-start.5) | collective-permute-done | bytes 147488 | tf_op jit(solution)/shard_map/ppermute | solution.py:329
  43.2 0.1 shard_map.92
  43.4 0.4 collective-permute-start.6
  43.7 1.0 %collective-permute-start.7 = (f32[1,2,4,1,24,128]{5,4,3,2,1,0:T(8,128)S(1)}, f32[1,2,4,1,24,128]{5,4,3,2,1,0:T(8,128)S(1)}, u32[]{:S(2)}, u32[]{:S(2)}) collective-permute-start(f32[1,2,4,1,24,128]{5,4,3,2,1,0:T(8,128)S(1)} %bitcast.11), channel_id=1, source_target_pairs={{0,2},{1,3},{2,0},{3,1},{4,6},{5,7},{6,4},{7,5},{8,10},{9,11},{10,... | collective-permute-start | bytes 294920 | tf_op jit(solution)/shard_map/ppermute | solution.py:329
  44.7 3.1 %collective-permute-start.8 = (f32[1,2,4,1,24,128]{5,4,3,2,1,0:T(8,128)S(1)}, f32[1,2,4,1,24,128]{5,4,3,2,1,0:T(8,128)S(1)}, u32[]{:S(2)}, u32[]{:S(2)}) collective-permute-start(f32[1,2,4,1,24,128]{5,4,3,2,1,0:T(8,128)S(1)} %bitcast.12), channel_id=1, source_target_pairs={{0,3},{1,2},{2,1},{3,0},{4,7},{5,6},{6,5},{7,4},{8,11},{9,10},{10,... | collective-permute-start | bytes 294920 | tf_op jit(solution)/shard_map/ppermute | solution.py:329
  47.8 0.5 shard_map.90.refs_0_.refs_5_.refs_7_
  48.3 4.6 %shard_map.91 = (f32[2,3,4,1,24,128]{5,4,3,2,1,0:T(8,128)S(1)}, f32[2,3,4,1,24,128]{5,4,3,2,1,0:T(8,128)S(1)}) custom-call(bf16[2,512,2048]{2,1,0:T(8,128)(2,1)S(1)} %shard_map.90.refs_0_.refs_5_.refs_7_, f32[2,2,4,1,24,128]{5,4,3,2,1,0:T(8,128)S(1)} %maximum_bitcast_fusion.refs_1_, f32[2,2,4,1,24,128]{5,4,3,2,1,0:T(8,128)S(1)} %collective-permute-done.4.refs_2_, ...), custom_call_target="tpu_custom_call" | custom-call | flops 1048576 | bytes 1024 | tf_op jit(solution)/shard_map/pallas_call | solution.py:29
  52.9 0.1 collective-permute-start.9
  53.1 4.4 %shard_map.93 = (f32[2,3,4,1,24,128]{5,4,3,2,1,0:T(8,128)S(1)}, f32[2,3,4,1,24,128]{5,4,3,2,1,0:T(8,128)S(1)}) custom-call(f32[2,3,4,1,24,128]{5,4,3,2,1,0:T(8,128)S(1)} %get-tuple-element.50.refs_0_.refs_1_, f32[1,2,4,1,24,128]{5,4,3,2,1,0:T(8,128)S(1)} %bitcast.13, f32[1,2,4,1,24,128]{5,4,3,2,1,0:T(8,128)S(1)} %collective-permute-done.6.refs_2_, ...), custom_call_target="tpu_custom_call" | custom-call | flops 1048576 | bytes 1024 | tf_op jit(solution)/shard_map/pallas_call | solution.py:29
  57.4 2.1 %collective-permute-start.12 = (f32[2,3,4,1,24,128]{5,4,3,2,1,0:T(8,128)S(1)}, f32[2,3,4,1,24,128]{5,4,3,2,1,0:T(8,128)S(1)}, u32[]{:S(2)}, u32[]{:S(2)}) collective-permute-start(f32[2,3,4,1,24,128]{5,4,3,2,1,0:T(8,128)S(1)} %get-tuple-element.59), channel_id=1, source_target_pairs={{0,1},{1,0},{2,3},{3,2},{4,5},{5,4},{6,7},{7,6},{8,9},{9,8},{10,11... | collective-permute-start | bytes 884744 | tf_op jit(solution)/shard_map/ppermute | solution.py:329
  59.5 2.2 %collective-permute-done.9.refs_2_ = f32[2,3,4,1,24,128]{5,4,3,2,1,0:T(8,128)S(1)} collective-permute-done((f32[2,3,4,1,24,128]{5,4,3,2,1,0:T(8,128)S(1)}, f32[2,3,4,1,24,128]{5,4,3,2,1,0:T(8,128)S(1)}, u32[]{:S(2)}, u32[]{:S(2)}) %collective-permute-start.9) | collective-permute-done | bytes 294944 | tf_op jit(solution)/shard_map/ppermute | solution.py:329
  61.7 1.3 %collective-permute-start.13 = (f32[1,3,4,1,24,128]{5,4,3,2,1,0:T(8,128)S(1)}, f32[1,3,4,1,24,128]{5,4,3,2,1,0:T(8,128)S(1)}, u32[]{:S(2)}, u32[]{:S(2)}) collective-permute-start(f32[1,3,4,1,24,128]{5,4,3,2,1,0:T(8,128)S(1)} %get-tuple-element.61), channel_id=1, source_target_pairs={{0,2},{1,3},{2,0},{3,1},{4,6},{5,7},{6,4},{7,5},{8,10},{9,11},{10,... | collective-permute-start | bytes 442376 | tf_op jit(solution)/shard_map/ppermute | solution.py:329
  63.1 1.3 %collective-permute-start.11 = (f32[2,4,2,4,128]{4,3,2,1,0:T(4,128)S(1)}, f32[2,4,2,4,128]{4,3,2,1,0:T(4,128)S(1)}, u32[]{:S(2)}, u32[]{:S(2)}) collective-permute-start(f32[2,4,2,4,128]{4,3,2,1,0:T(4,128)S(1)} %add.22), channel_id=1, source_target_pairs={{0,8},{4,12},{8,0},{12,4},{16,24},{20,28},{24,16},{28,20},{1,9},{5... | collective-permute-start | bytes 98312 | tf_op jit(solution)/shard_map/ppermute | solution.py:329
  64.4 2.6 %collective-permute-done.11 = f32[2,4,2,4,128]{4,3,2,1,0:T(4,128)S(1)} collective-permute-done((f32[2,4,2,4,128]{4,3,2,1,0:T(4,128)S(1)}, f32[2,4,2,4,128]{4,3,2,1,0:T(4,128)S(1)}, u32[]{:S(2)}, u32[]{:S(2)}) %collective-permute-start.11) | collective-permute-done | bytes 32800 | tf_op jit(solution)/shard_map/ppermute | solution.py:329
  67.1 1.8 %collective-permute-start.15 = (f32[1,3,4,1,24,128]{5,4,3,2,1,0:T(8,128)S(1)}, f32[1,3,4,1,24,128]{5,4,3,2,1,0:T(8,128)S(1)}, u32[]{:S(2)}, u32[]{:S(2)}) collective-permute-start(f32[1,3,4,1,24,128]{5,4,3,2,1,0:T(8,128)S(1)} %get-tuple-element.66), channel_id=1, source_target_pairs={{0,2},{1,3},{2,0},{3,1},{4,6},{5,7},{6,4},{7,5},{8,10},{9,11},{10,... | collective-permute-start | bytes 442376 | tf_op jit(solution)/shard_map/ppermute | solution.py:329
  68.9 1.3 %collective-permute-start.14 = (f32[2,4,2,4,128]{4,3,2,1,0:T(4,128)S(1)}, f32[2,4,2,4,128]{4,3,2,1,0:T(4,128)S(1)}, u32[]{:S(2)}, u32[]{:S(2)}) collective-permute-start(f32[2,4,2,4,128]{4,3,2,1,0:T(4,128)S(1)} %add.23.refs_1_), channel_id=1, source_target_pairs={{0,16},{4,20},{8,24},{12,28},{16,0},{20,4},{24,8},{28,12},{1,17},{... | collective-permute-start | bytes 98312 | tf_op jit(solution)/shard_map/ppermute | solution.py:329
  70.2 2.6 %collective-permute-done.14 = f32[2,4,2,4,128]{4,3,2,1,0:T(4,128)S(1)} collective-permute-done((f32[2,4,2,4,128]{4,3,2,1,0:T(4,128)S(1)}, f32[2,4,2,4,128]{4,3,2,1,0:T(4,128)S(1)}, u32[]{:S(2)}, u32[]{:S(2)}) %collective-permute-start.14) | collective-permute-done | bytes 32800 | tf_op jit(solution)/shard_map/ppermute | solution.py:329
  72.8 0.1 shard_map.96
  72.9 0.1 shard_map.97
  73.1 1.3 %collective-permute-start.17 = (f32[1,2,4,1,24,128]{5,4,3,2,1,0:T(8,128)S(1)}, f32[1,2,4,1,24,128]{5,4,3,2,1,0:T(8,128)S(1)}, u32[]{:S(2)}, u32[]{:S(2)}) collective-permute-start(f32[1,2,4,1,24,128]{5,4,3,2,1,0:T(8,128)S(1)} %bitcast.14), channel_id=1, source_target_pairs={{0,2},{1,3},{2,0},{3,1},{4,6},{5,7},{6,4},{7,5},{8,10},{9,11},{10,... | collective-permute-start | bytes 294920 | tf_op jit(solution)/shard_map/ppermute | solution.py:329
  74.4 3.3 %collective-permute-done.15.refs_5_ = f32[1,3,4,1,24,128]{5,4,3,2,1,0:T(8,128)S(1)} collective-permute-done((f32[1,3,4,1,24,128]{5,4,3,2,1,0:T(8,128)S(1)}, f32[1,3,4,1,24,128]{5,4,3,2,1,0:T(8,128)S(1)}, u32[]{:S(2)}, u32[]{:S(2)}) %collective-permute-start.15) | collective-permute-done | bytes 147488 | tf_op jit(solution)/shard_map/ppermute | solution.py:329
  77.7 0.1 shard_map.98
  77.8 0.1 collective-permute-start.16
  77.9 1.2 %collective-permute-done.16 = f32[2,4,2,4,128]{4,3,2,1,0:T(4,128)S(1)} collective-permute-done((f32[2,4,2,4,128]{4,3,2,1,0:T(4,128)S(1)}, f32[2,4,2,4,128]{4,3,2,1,0:T(4,128)S(1)}, u32[]{:S(2)}, u32[]{:S(2)}) %collective-permute-start.16) | collective-permute-done | bytes 32800 | tf_op jit(solution)/shard_map/ppermute | solution.py:329
  79.1 1.1 %collective-permute-done.17.refs_2_ = f32[1,2,4,1,24,128]{5,4,3,2,1,0:T(8,128)S(1)} collective-permute-done((f32[1,2,4,1,24,128]{5,4,3,2,1,0:T(8,128)S(1)}, f32[1,2,4,1,24,128]{5,4,3,2,1,0:T(8,128)S(1)}, u32[]{:S(2)}, u32[]{:S(2)}) %collective-permute-start.17) | collective-permute-done | bytes 98336 | tf_op jit(solution)/shard_map/ppermute | solution.py:329
  80.3 0.1 collective-permute-start.18
  80.4 2.0 %collective-permute-start.19 = (f32[1,2,4,1,24,128]{5,4,3,2,1,0:T(8,128)S(1)}, f32[1,2,4,1,24,128]{5,4,3,2,1,0:T(8,128)S(1)}, u32[]{:S(2)}, u32[]{:S(2)}) collective-permute-start(f32[1,2,4,1,24,128]{5,4,3,2,1,0:T(8,128)S(1)} %bitcast.16), channel_id=1, source_target_pairs={{0,1},{1,0},{2,3},{3,2},{4,5},{5,4},{6,7},{7,6},{8,9},{9,8},{10,11... | collective-permute-start | bytes 294920 | tf_op jit(solution)/shard_map/ppermute | solution.py:329
  82.4 0.1 collective-permute-start.20
  82.5 2.3 %collective-permute-start.21 = (f32[1,2,4,1,24,128]{5,4,3,2,1,0:T(8,128)S(1)}, f32[1,2,4,1,24,128]{5,4,3,2,1,0:T(8,128)S(1)}, u32[]{:S(2)}, u32[]{:S(2)}) collective-permute-start(f32[1,2,4,1,24,128]{5,4,3,2,1,0:T(8,128)S(1)} %bitcast.18), channel_id=1, source_target_pairs={{0,3},{1,2},{2,1},{3,0},{4,7},{5,6},{6,5},{7,4},{8,11},{9,10},{10,... | collective-permute-start | bytes 294920 | tf_op jit(solution)/shard_map/ppermute | solution.py:329
  84.8 1.3 %collective-permute-start.22 = (f32[2,4,2,4,128]{4,3,2,1,0:T(4,128)S(1)}, f32[2,4,2,4,128]{4,3,2,1,0:T(4,128)S(1)}, u32[]{:S(2)}, u32[]{:S(2)}) collective-permute-start(f32[2,4,2,4,128]{4,3,2,1,0:T(4,128)S(1)} %add.25.refs_0_), channel_id=1, source_target_pairs={{0,8},{4,12},{8,0},{12,4},{16,24},{20,28},{24,16},{28,20},{1,9},{5... | collective-permute-start | bytes 98312 | tf_op jit(solution)/shard_map/ppermute | solution.py:329
  86.1 2.6 %collective-permute-done.22 = f32[2,4,2,4,128]{4,3,2,1,0:T(4,128)S(1)} collective-permute-done((f32[2,4,2,4,128]{4,3,2,1,0:T(4,128)S(1)}, f32[2,4,2,4,128]{4,3,2,1,0:T(4,128)S(1)}, u32[]{:S(2)}, u32[]{:S(2)}) %collective-permute-start.22) | collective-permute-done | bytes 32800 | tf_op jit(solution)/shard_map/ppermute | solution.py:329
  88.7 1.4 %collective-permute-start.23 = (f32[2,4,2,4,128]{4,3,2,1,0:T(4,128)S(1)}, f32[2,4,2,4,128]{4,3,2,1,0:T(4,128)S(1)}, u32[]{:S(2)}, u32[]{:S(2)}) collective-permute-start(f32[2,4,2,4,128]{4,3,2,1,0:T(4,128)S(1)} %add.26), channel_id=1, source_target_pairs={{0,16},{4,20},{8,24},{12,28},{16,0},{20,4},{24,8},{28,12},{1,17},{... | collective-permute-start | bytes 98312 | tf_op jit(solution)/shard_map/ppermute | solution.py:329
  90.1 2.6 %collective-permute-done.23 = f32[2,4,2,4,128]{4,3,2,1,0:T(4,128)S(1)} collective-permute-done((f32[2,4,2,4,128]{4,3,2,1,0:T(4,128)S(1)}, f32[2,4,2,4,128]{4,3,2,1,0:T(4,128)S(1)}, u32[]{:S(2)}, u32[]{:S(2)}) %collective-permute-start.23) | collective-permute-done | bytes 32800 | tf_op jit(solution)/shard_map/ppermute | solution.py:329
  92.7 0.9 shard_map.101
  93.6 1.0 %shard_map.100 = f32[2,4,2,24,512]{4,3,2,1,0:T(8,128)} custom-call(f32[2,2,4,1,24,128]{5,4,3,2,1,0:T(8,128)S(1)} %shard_map.99.refs_0_, f32[2,2,4,1,24,128]{5,4,3,2,1,0:T(8,128)S(1)} %collective-permute-done.18.refs_1_, f32[1,2,4,1,24,128]{5,4,3,2,1,0:T(8,128)S(1)} %bitcast.19, f32[1,2,4,1,24,128]{5,4,3,2,1,0:T(8,128)S(1)} %collective-permute-done.19.refs_3_, ...), custom_call_target="tpu_custom_call" | custom-call | flops 1048576 | bytes 1024 | tf_op jit(solution)/shard_map/pallas_call | solution.py:29
  (31 shorter events, 0.3 us)
Async XLA Ops:
  7.0 10.3 %collective-permute-start = (f32[2,3,4,1,24,128]{5,4,3,2,1,0:T(8,128)S(1)}, f32[2,3,4,1,24,128]{5,4,3,2,1,0:T(8,128)S(1)}, u32[]{:S(2)}, u32[]{:S(2)}) collective-permute-start(f32[2,3,4,1,24,128]{5,4,3,2,1,0:T(8,128)S(1)} %get-tuple-element.43), channel_id=1, source_target_pairs={{0,1},{1,0},{2,3},{3,2},{4,5},{5,4},{6,7},{7,6},{8,9},{9,8},{10,11... | collective-permute-start | bytes 884744 | tf_op jit(solution)/shard_map/ppermute | solution.py:329
  10.1 17.0 %copy-start.1 = (f32[4]{0:T(128)S(1)}, f32[4]{0:T(128)}, u32[]{:S(2)}) copy-start(f32[4]{0:T(128)} %param.9) | copy-start | bytes 52
  10.1 37.7 %copy-start = (s32[2,2048]{1,0:T(2,128)S(1)}, s32[2,2048]{1,0:T(2,128)}, u32[]{:S(2)}) copy-start(s32[2,2048]{1,0:T(2,128)} %refs_1_.3) | copy-start | bytes 49156
  15.2 11.8 %collective-permute-start.1 = (f32[2,3,4,1,24,128]{5,4,3,2,1,0:T(8,128)}, f32[2,3,4,1,24,128]{5,4,3,2,1,0:T(8,128)S(1)}, u32[]{:S(2)}, u32[]{:S(2)}) collective-permute-start(f32[2,3,4,1,24,128]{5,4,3,2,1,0:T(8,128)} %get-tuple-element.45), channel_id=1, source_target_pairs={{0,1},{1,0},{2,3},{3,2},{4,5},{5,4},{6,7},{7,6},{8,9},{9,8},{10,11... | collective-permute-start | bytes 884744 | tf_op jit(solution)/shard_map/ppermute | solution.py:329
  18.0 9.1 %collective-permute-start.2 = (f32[1,3,4,1,24,128]{5,4,3,2,1,0:T(8,128)}, f32[1,3,4,1,24,128]{5,4,3,2,1,0:T(8,128)S(1)}, u32[]{:S(2)}, u32[]{:S(2)}) collective-permute-start(f32[1,3,4,1,24,128]{5,4,3,2,1,0:T(8,128)} %get-tuple-element.47), channel_id=1, source_target_pairs={{0,2},{1,3},{2,0},{3,1},{4,6},{5,7},{6,4},{7,5},{8,10},{9,11},{10,... | collective-permute-start | bytes 442376 | tf_op jit(solution)/shard_map/ppermute | solution.py:329
  27.3 6.3 %collective-permute-start.3 = (f32[1,2,4,1,24,128]{5,4,2,1,3,0:T(8,128)S(1)}, f32[1,2,4,1,24,128]{5,4,2,1,3,0:T(8,128)S(1)}, u32[]{:S(2)}, u32[]{:S(2)}) collective-permute-start(f32[1,2,4,1,24,128]{5,4,2,1,3,0:T(8,128)S(1)} %bitcast.8), channel_id=1, source_target_pairs={{0,2},{1,3},{2,0},{3,1},{4,6},{5,7},{6,4},{7,5},{8,10},{9,11},{10,... | collective-permute-start | bytes 294920 | tf_op jit(solution)/shard_map/ppermute | solution.py:329
  33.6 14.7 %collective-permute-start.4 = (f32[2,2,4,1,24,128]{5,4,3,2,1,0:T(8,128)S(1)}, f32[2,2,4,1,24,128]{5,4,3,2,1,0:T(8,128)S(1)}, u32[]{:S(2)}, u32[]{:S(2)}) collective-permute-start(f32[2,2,4,1,24,128]{5,4,3,2,1,0:T(8,128)S(1)} %maximum_bitcast_fusion.refs_1_), channel_id=1, source_target_pairs={{0,1},{1,0},{2,3},{3,2},{4,5},{5,4},{6,7},{7,6},{8,9},{9,8},{10,11... | collective-permute-start | bytes 589832 | tf_op jit(solution)/shard_map/ppermute | solution.py:329
  35.5 7.7 %collective-permute-start.5 = (f32[1,3,4,1,24,128]{5,4,3,2,1,0:T(8,128)S(1)}, f32[1,3,4,1,24,128]{5,4,3,2,1,0:T(8,128)S(1)}, u32[]{:S(2)}, u32[]{:S(2)}) collective-permute-start(f32[1,3,4,1,24,128]{5,4,3,2,1,0:T(8,128)S(1)} %get-tuple-element.52), channel_id=1, source_target_pairs={{0,2},{1,3},{2,0},{3,1},{4,6},{5,7},{6,4},{7,5},{8,10},{9,11},{10,... | collective-permute-start | bytes 442376 | tf_op jit(solution)/shard_map/ppermute | solution.py:329
  43.4 9.7 %collective-permute-start.6 = (f32[1,2,4,1,24,128]{5,4,3,2,1,0:T(8,128)S(1)}, f32[1,2,4,1,24,128]{5,4,3,2,1,0:T(8,128)S(1)}, u32[]{:S(2)}, u32[]{:S(2)}) collective-permute-start(f32[1,2,4,1,24,128]{5,4,3,2,1,0:T(8,128)S(1)} %bitcast.10), channel_id=1, source_target_pairs={{0,1},{1,0},{2,3},{3,2},{4,5},{5,4},{6,7},{7,6},{8,9},{9,8},{10,11... | collective-permute-start | bytes 294920 | tf_op jit(solution)/shard_map/ppermute | solution.py:329
  43.7 9.3 %collective-permute-start.7 = (f32[1,2,4,1,24,128]{5,4,3,2,1,0:T(8,128)S(1)}, f32[1,2,4,1,24,128]{5,4,3,2,1,0:T(8,128)S(1)}, u32[]{:S(2)}, u32[]{:S(2)}) collective-permute-start(f32[1,2,4,1,24,128]{5,4,3,2,1,0:T(8,128)S(1)} %bitcast.11), channel_id=1, source_target_pairs={{0,2},{1,3},{2,0},{3,1},{4,6},{5,7},{6,4},{7,5},{8,10},{9,11},{10,... | collective-permute-start | bytes 294920 | tf_op jit(solution)/shard_map/ppermute | solution.py:329
  44.7 8.3 %collective-permute-start.8 = (f32[1,2,4,1,24,128]{5,4,3,2,1,0:T(8,128)S(1)}, f32[1,2,4,1,24,128]{5,4,3,2,1,0:T(8,128)S(1)}, u32[]{:S(2)}, u32[]{:S(2)}) collective-permute-start(f32[1,2,4,1,24,128]{5,4,3,2,1,0:T(8,128)S(1)} %bitcast.12), channel_id=1, source_target_pairs={{0,3},{1,2},{2,1},{3,0},{4,7},{5,6},{6,5},{7,4},{8,11},{9,10},{10,... | collective-permute-start | bytes 294920 | tf_op jit(solution)/shard_map/ppermute | solution.py:329
  52.9 8.8 %collective-permute-start.9 = (f32[2,3,4,1,24,128]{5,4,3,2,1,0:T(8,128)S(1)}, f32[2,3,4,1,24,128]{5,4,3,2,1,0:T(8,128)S(1)}, u32[]{:S(2)}, u32[]{:S(2)}) collective-permute-start(f32[2,3,4,1,24,128]{5,4,3,2,1,0:T(8,128)S(1)} %get-tuple-element.56), channel_id=1, source_target_pairs={{0,1},{1,0},{2,3},{3,2},{4,5},{5,4},{6,7},{7,6},{8,9},{9,8},{10,11... | collective-permute-start | bytes 884744 | tf_op jit(solution)/shard_map/ppermute | solution.py:329
  57.4 9.6 %collective-permute-start.12 = (f32[2,3,4,1,24,128]{5,4,3,2,1,0:T(8,128)S(1)}, f32[2,3,4,1,24,128]{5,4,3,2,1,0:T(8,128)S(1)}, u32[]{:S(2)}, u32[]{:S(2)}) collective-permute-start(f32[2,3,4,1,24,128]{5,4,3,2,1,0:T(8,128)S(1)} %get-tuple-element.59), channel_id=1, source_target_pairs={{0,1},{1,0},{2,3},{3,2},{4,5},{5,4},{6,7},{7,6},{8,9},{9,8},{10,11... | collective-permute-start | bytes 884744 | tf_op jit(solution)/shard_map/ppermute | solution.py:329
  59.5 3.5 %collective-permute-start.10 = (f32[2,4,2,4,128]{4,3,2,1,0:T(4,128)S(1)}, f32[2,4,2,4,128]{4,3,2,1,0:T(4,128)S(1)}, u32[]{:S(2)}, u32[]{:S(2)}) collective-permute-start(f32[2,4,2,4,128]{4,3,2,1,0:T(4,128)S(1)} %get-tuple-element.58), channel_id=1, source_target_pairs={{0,4},{4,0},{8,12},{12,8},{16,20},{20,16},{24,28},{28,24},{1,5},{5... | collective-permute-start | bytes 98312 | tf_op jit(solution)/shard_map/ppermute | solution.py:329
  61.7 11.2 %collective-permute-start.13 = (f32[1,3,4,1,24,128]{5,4,3,2,1,0:T(8,128)S(1)}, f32[1,3,4,1,24,128]{5,4,3,2,1,0:T(8,128)S(1)}, u32[]{:S(2)}, u32[]{:S(2)}) collective-permute-start(f32[1,3,4,1,24,128]{5,4,3,2,1,0:T(8,128)S(1)} %get-tuple-element.61), channel_id=1, source_target_pairs={{0,2},{1,3},{2,0},{3,1},{4,6},{5,7},{6,4},{7,5},{8,10},{9,11},{10,... | collective-permute-start | bytes 442376 | tf_op jit(solution)/shard_map/ppermute | solution.py:329
  63.1 4.0 %collective-permute-start.11 = (f32[2,4,2,4,128]{4,3,2,1,0:T(4,128)S(1)}, f32[2,4,2,4,128]{4,3,2,1,0:T(4,128)S(1)}, u32[]{:S(2)}, u32[]{:S(2)}) collective-permute-start(f32[2,4,2,4,128]{4,3,2,1,0:T(4,128)S(1)} %add.22), channel_id=1, source_target_pairs={{0,8},{4,12},{8,0},{12,4},{16,24},{20,28},{24,16},{28,20},{1,9},{5... | collective-permute-start | bytes 98312 | tf_op jit(solution)/shard_map/ppermute | solution.py:329
  67.1 10.6 %collective-permute-start.15 = (f32[1,3,4,1,24,128]{5,4,3,2,1,0:T(8,128)S(1)}, f32[1,3,4,1,24,128]{5,4,3,2,1,0:T(8,128)S(1)}, u32[]{:S(2)}, u32[]{:S(2)}) collective-permute-start(f32[1,3,4,1,24,128]{5,4,3,2,1,0:T(8,128)S(1)} %get-tuple-element.66), channel_id=1, source_target_pairs={{0,2},{1,3},{2,0},{3,1},{4,6},{5,7},{6,4},{7,5},{8,10},{9,11},{10,... | collective-permute-start | bytes 442376 | tf_op jit(solution)/shard_map/ppermute | solution.py:329
  68.9 3.9 %collective-permute-start.14 = (f32[2,4,2,4,128]{4,3,2,1,0:T(4,128)S(1)}, f32[2,4,2,4,128]{4,3,2,1,0:T(4,128)S(1)}, u32[]{:S(2)}, u32[]{:S(2)}) collective-permute-start(f32[2,4,2,4,128]{4,3,2,1,0:T(4,128)S(1)} %add.23.refs_1_), channel_id=1, source_target_pairs={{0,16},{4,20},{8,24},{12,28},{16,0},{20,4},{24,8},{28,12},{1,17},{... | collective-permute-start | bytes 98312 | tf_op jit(solution)/shard_map/ppermute | solution.py:329
  73.1 7.2 %collective-permute-start.17 = (f32[1,2,4,1,24,128]{5,4,3,2,1,0:T(8,128)S(1)}, f32[1,2,4,1,24,128]{5,4,3,2,1,0:T(8,128)S(1)}, u32[]{:S(2)}, u32[]{:S(2)}) collective-permute-start(f32[1,2,4,1,24,128]{5,4,3,2,1,0:T(8,128)S(1)} %bitcast.14), channel_id=1, source_target_pairs={{0,2},{1,3},{2,0},{3,1},{4,6},{5,7},{6,4},{7,5},{8,10},{9,11},{10,... | collective-permute-start | bytes 294920 | tf_op jit(solution)/shard_map/ppermute | solution.py:329
  77.8 1.3 %collective-permute-start.16 = (f32[2,4,2,4,128]{4,3,2,1,0:T(4,128)S(1)}, f32[2,4,2,4,128]{4,3,2,1,0:T(4,128)S(1)}, u32[]{:S(2)}, u32[]{:S(2)}) collective-permute-start(f32[2,4,2,4,128]{4,3,2,1,0:T(4,128)S(1)} %get-tuple-element.67), channel_id=1, source_target_pairs={{0,4},{4,0},{8,12},{12,8},{16,20},{20,16},{24,28},{28,24},{1,5},{5... | collective-permute-start | bytes 98312 | tf_op jit(solution)/shard_map/ppermute | solution.py:329
  80.3 13.3 %collective-permute-start.18 = (f32[2,2,4,1,24,128]{5,4,3,2,1,0:T(8,128)S(1)}, f32[2,2,4,1,24,128]{5,4,3,2,1,0:T(8,128)S(1)}, u32[]{:S(2)}, u32[]{:S(2)}) collective-permute-start(f32[2,2,4,1,24,128]{5,4,3,2,1,0:T(8,128)S(1)} %shard_map.99.refs_0_), channel_id=1, source_target_pairs={{0,1},{1,0},{2,3},{3,2},{4,5},{5,4},{6,7},{7,6},{8,9},{9,8},{10,11... | collective-permute-start | bytes 589832 | tf_op jit(solution)/shard_map/ppermute | solution.py:329
  80.4 13.3 %collective-permute-start.19 = (f32[1,2,4,1,24,128]{5,4,3,2,1,0:T(8,128)S(1)}, f32[1,2,4,1,24,128]{5,4,3,2,1,0:T(8,128)S(1)}, u32[]{:S(2)}, u32[]{:S(2)}) collective-permute-start(f32[1,2,4,1,24,128]{5,4,3,2,1,0:T(8,128)S(1)} %bitcast.16), channel_id=1, source_target_pairs={{0,1},{1,0},{2,3},{3,2},{4,5},{5,4},{6,7},{7,6},{8,9},{9,8},{10,11... | collective-permute-start | bytes 294920 | tf_op jit(solution)/shard_map/ppermute | solution.py:329
  82.4 11.2 %collective-permute-start.20 = (f32[1,2,4,1,24,128]{5,4,3,2,1,0:T(8,128)S(1)}, f32[1,2,4,1,24,128]{5,4,3,2,1,0:T(8,128)S(1)}, u32[]{:S(2)}, u32[]{:S(2)}) collective-permute-start(f32[1,2,4,1,24,128]{5,4,3,2,1,0:T(8,128)S(1)} %bitcast.17), channel_id=1, source_target_pairs={{0,2},{1,3},{2,0},{3,1},{4,6},{5,7},{6,4},{7,5},{8,10},{9,11},{10,... | collective-permute-start | bytes 294920 | tf_op jit(solution)/shard_map/ppermute | solution.py:329
  82.5 11.1 %collective-permute-start.21 = (f32[1,2,4,1,24,128]{5,4,3,2,1,0:T(8,128)S(1)}, f32[1,2,4,1,24,128]{5,4,3,2,1,0:T(8,128)S(1)}, u32[]{:S(2)}, u32[]{:S(2)}) collective-permute-start(f32[1,2,4,1,24,128]{5,4,3,2,1,0:T(8,128)S(1)} %bitcast.18), channel_id=1, source_target_pairs={{0,3},{1,2},{2,1},{3,0},{4,7},{5,6},{6,5},{7,4},{8,11},{9,10},{10,... | collective-permute-start | bytes 294920 | tf_op jit(solution)/shard_map/ppermute | solution.py:329
  84.8 3.9 %collective-permute-start.22 = (f32[2,4,2,4,128]{4,3,2,1,0:T(4,128)S(1)}, f32[2,4,2,4,128]{4,3,2,1,0:T(4,128)S(1)}, u32[]{:S(2)}, u32[]{:S(2)}) collective-permute-start(f32[2,4,2,4,128]{4,3,2,1,0:T(4,128)S(1)} %add.25.refs_0_), channel_id=1, source_target_pairs={{0,8},{4,12},{8,0},{12,4},{16,24},{20,28},{24,16},{28,20},{1,9},{5... | collective-permute-start | bytes 98312 | tf_op jit(solution)/shard_map/ppermute | solution.py:329
  88.7 4.0 %collective-permute-start.23 = (f32[2,4,2,4,128]{4,3,2,1,0:T(4,128)S(1)}, f32[2,4,2,4,128]{4,3,2,1,0:T(4,128)S(1)}, u32[]{:S(2)}, u32[]{:S(2)}) collective-permute-start(f32[2,4,2,4,128]{4,3,2,1,0:T(4,128)S(1)} %add.26), channel_id=1, source_target_pairs={{0,16},{4,20},{8,24},{12,28},{16,0},{20,4},{24,8},{28,12},{1,17},{... | collective-permute-start | bytes 98312 | tf_op jit(solution)/shard_map/ppermute | solution.py:329
